TPU v7x, 32 devices: a whole 2x2x4 slice. The times are simulated.
32 devices in a mesh: groups: 2 (over x), img: 16 (over z, y, core).
Axes of the slice: x: 2, y: 2, z: 4, core: 2. Of those that a mesh axis runs over, the one named last changes fastest.
Arguments:
- tokens: bfloat16 [64, 128, 768], P(('groups', 'img')), parts along dimension 0, may hold values from -6 to 6
- partners: int32 [64, 8], P(('groups', 'img')), parts along dimension 0, may hold values from 0 to 31, as said below
- counts: int32 [64], P(('groups', 'img')), parts along dimension 0, may hold values from 4 to 8, as said below
- gain_query: float32 [768], replicated, may hold values from 0.5 to 12
- gain_memory: float32 [768], replicated, may hold values from 0.25 to 1.75
- w_query: bfloat16 [768, 768], replicated, may hold values from -0.21875 to 0.21875
- w_key: bfloat16 [768, 768], replicated, may hold values from -0.21875 to 0.21875
- w_value: bfloat16 [768, 768], replicated, may hold values from -0.21875 to 0.21875
- w_out: bfloat16 [768, 768], replicated, may hold values from -0.21875 to 0.21875
Outputs:
- mixed: bfloat16 [64, 128, 768], P(('groups', 'img')), parts along dimension 0
There are 2 independent parts, one for each index of `groups`. A program takes and returns all parts, laid end to end along the dimension named above; an argument that names none is the same for every part. Nothing has to cross between parts.
Inputs may be any that keep to these rules, and one draw needn't show every extreme that they name: No image is its own partner. Over the first counts[a] partners of all images a of one device (image i belongs to device i // 2), at most 1 lie with any one device, and every device reaches 1 with some device. `counts`: every device owns an image with 8 pairs.
All inputs are finite; a program needn't handle non-finite values.
Results may differ from a plain program's by a relative error of at most 0.0067.
Values may be sent and summed in bfloat16 or wider, within the bound.
No kernel may reach another device: no remote copies, remote signals or barrier semaphores. Data moves between devices by JAX's collectives and lax.ppermute only.
A program may use at most 128 MiB of HBM per device.

v0:
```python
import jax
import jax.numpy as jnp
from jax import lax
from jax.sharding import PartitionSpec as P

HEADS = 12
HEAD_DIM = 64


def normalize(rows, gain):
    rows = rows.astype(jnp.float32)
    center = rows - jnp.mean(rows, axis=-1, keepdims=True)
    spread = jnp.mean(center * center, axis=-1, keepdims=True)
    return center * lax.rsqrt(spread + 1e-06) * gain


def slot_table(partner_rows, count_rows, own_count, peer_count):
    width = partner_rows.shape[1]
    live = (jnp.arange(width, dtype=jnp.int32)[None, :] < count_rows[:, None]).reshape(-1)
    owner = (partner_rows // own_count).reshape(-1)
    onehot = (
        (owner[:, None] == jnp.arange(peer_count, dtype=jnp.int32)[None, :]) & live[:, None]
    ).astype(jnp.int32)
    before = jnp.cumsum(onehot, axis=0) - onehot
    slot = jnp.sum(before * onehot, axis=1)
    return (owner, slot, live)


def shards(tokens, partners, counts, gain_query, gain_memory, w_query, w_key, w_value, w_out):
    own_count, tok_rows, width = tokens.shape
    listed = partners.shape[1]
    peer_count = lax.axis_size("img")
    slot_cap = (own_count * listed + peer_count - 1) // peer_count
    first_image = lax.axis_index("img") * own_count
    rows = tokens.reshape(own_count * tok_rows, width)
    normed_query = normalize(rows, gain_query).astype(jnp.bfloat16)
    normed_memory = normalize(rows, gain_memory).astype(jnp.bfloat16)
    queries = jnp.dot(normed_query, w_query, preferred_element_type=jnp.float32).astype(
        jnp.bfloat16
    )
    queries = queries.reshape(own_count, tok_rows, HEADS, HEAD_DIM)
    my_owner, my_slot, my_live = slot_table(partners, counts, own_count, peer_count)
    target = jnp.where(my_live, my_owner, peer_count)
    request = (
        jnp.full((peer_count, slot_cap), -1, jnp.int32)
        .at[target, my_slot]
        .set(partners.reshape(-1), mode="drop")
    )
    wanted = lax.all_to_all(request, "img", split_axis=0, concat_axis=0, tiled=True)
    used = wanted >= 0
    local_index = jnp.clip(wanted - first_image, 0, own_count - 1)
    pick = jnp.clip(my_owner, 0, peer_count - 1) * slot_cap + jnp.clip(my_slot, 0, slot_cap - 1)
    picked = normed_memory.reshape(own_count, tok_rows, width)[local_index]
    got_memory = lax.all_to_all(
        jnp.where(used[:, :, None, None], picked, jnp.zeros_like(picked)),
        "img",
        split_axis=0,
        concat_axis=0,
        tiled=True,
    )
    pair_memory = got_memory.reshape(peer_count * slot_cap, tok_rows, width)[pick].reshape(
        -1, width
    )
    pair_keys = jnp.dot(pair_memory, w_key, preferred_element_type=jnp.float32).astype(jnp.bfloat16)
    pair_values = jnp.dot(pair_memory, w_value, preferred_element_type=jnp.float32).astype(
        jnp.bfloat16
    )
    pair_keys = pair_keys.reshape(own_count, listed, tok_rows, HEADS, HEAD_DIM)
    pair_values = pair_values.reshape(own_count, listed, tok_rows, HEADS, HEAD_DIM)
    scale = 1.0 / HEAD_DIM**0.5

    def one_image(item):
        query_rows, key_rows, value_rows, count = item
        scores = (
            jnp.einsum("qhd,kjhd->hkqj", query_rows, key_rows, preferred_element_type=jnp.float32)
            * scale
        )
        probs = jax.nn.softmax(scores, axis=-1).astype(jnp.bfloat16)
        pair_context = jnp.einsum(
            "hkqj,kjhd->kqhd", probs, value_rows, preferred_element_type=jnp.float32
        )
        live = jnp.arange(listed, dtype=jnp.int32) < count
        total = jnp.sum(
            jnp.where(live[:, None, None, None], pair_context, jnp.float32(0.0)), axis=0
        )
        return total.reshape(tok_rows, width) / count.astype(jnp.float32)

    context = lax.map(one_image, (queries, pair_keys, pair_values, counts)).astype(jnp.bfloat16)
    mixed = rows.astype(jnp.float32) + jnp.dot(
        context.reshape(-1, width), w_out, preferred_element_type=jnp.float32
    )
    return mixed.astype(jnp.bfloat16).reshape(own_count, tok_rows, width)


def solution(mesh):
    placed = (
        P(("groups", "img"), None, None),
        P(("groups", "img"), None),
        P(("groups", "img")),
        P(),
        P(),
        P(),
        P(),
        P(),
        P(),
    )
    return jax.shard_map(
        shards,
        mesh=mesh,
        in_specs=placed,
        out_specs=P(("groups", "img"), None, None),
        check_vma=False,
    )
```

profile of v0, /device:TPU:13, one launch (start us, length us, event | category | flops | bytes accessed | tf_op | source)
XLA Modules:
  0.0 160.1 jit_solution(5718504146963567102)
XLA Ops:
  0.0 0.0 copy-start
  0.0 0.8 broadcast_clamp_fusion
  0.8 0.1 eq.15
  0.9 0.7 iota_compare_fusion.2
  1.6 0.7 broadcast_select_fusion
  2.3 0.8 reshape.260
  3.1 0.1 lt.81
  3.2 0.1 fusion.22
  3.3 0.2 select_reduce_fusion.1
  3.5 0.1 select_n.74
  3.5 0.1 min.33
  3.6 0.6 scatter_custom_fusion
  4.3 0.7 copy.39
  5.0 6.6 %all-to-all-start = ((s32[16,1,1]{2,1,0:T(1,128)}), s32[16,1,1]{2,1,0:T(1,128)S(1)}, u32[]{:S(2)}, u32[]{:S(2)}) async-start(s32[16,1,1]{2,1,0:T(1,128)} %copy.39), calls=%async_computation | async-start | bytes 16384 | tf_op jit(solution)/shard_map/all_to_all | solution.py:49
  11.5 1.1 convert_reduce_fusion
  12.6 1.2 multiply_reduce_fusion
  13.9 1.2 multiply_convert_fusion
  15.1 0.1 all-to-all-done
  15.2 0.4 fusion.20
  15.6 2.5 %gather_fusion = bf16[16,128,768]{2,1,0:T(8,128)(2,1)} fusion(bf16[2,128,768]{2,1,0:T(8,128)(2,1)S(1)} %multiply_convert_fusion, s32[1024]{0:T(1024)S(1)} %pad_clamp_fusion.1), kind=kCustom, calls=%fused_computation | custom fusion | bytes 6291520 | tf_op jit(solution)/shard_map/gather | solution.py:53
  18.1 0.4 compare_reduce_fusion
  18.5 3.9 %bitcast_select_fusion = bf16[16,1,128,768]{3,2,1,0:T(8,128)(2,1)} fusion(bf16[16,128,768]{2,1,0:T(8,128)(2,1)} %gather_fusion, pred[16]{0:T(512)(128)(4,1)S(1)} %compare_reduce_fusion), kind=kLoop, calls=%fused_computation.28 | loop fusion | flops 1572864 | bytes 6291472 | tf_op jit(solution)/shard_map/jit(_where)/select_n | solution.py:55
  22.3 0.0 copy-start.1
  22.3 0.0 copy-start.5
  22.3 0.0 copy-start.3
  22.3 7.1 %all-to-all-start.1 = ((bf16[16,1,128,768]{3,2,1,0:T(8,128)(2,1)}), bf16[16,1,128,768]{3,2,1,0:T(8,128)(2,1)}, u32[]{:S(2)}, u32[]{:S(2)}) async-start(bf16[16,1,128,768]{3,2,1,0:T(8,128)(2,1)} %bitcast_select_fusion), calls=%async_computation.1 | async-start | bytes 6291456 | tf_op jit(solution)/shard_map/all_to_all | solution.py:54
  29.4 0.0 copy-done.1
  29.4 0.0 copy-done.5
  29.4 0.2 fusion.19
  29.7 0.0 copy-done.3
  29.7 0.5 convolution_convert_fusion.2
  30.2 0.2 copy.42
  30.3 0.1 reshape.234
  30.4 0.1 copy.45
  30.5 68.9 %all-to-all-done.1 = bf16[16,1,128,768]{3,2,1,0:T(8,128)(2,1)} async-done(((bf16[16,1,128,768]{3,2,1,0:T(8,128)(2,1)}), bf16[16,1,128,768]{3,2,1,0:T(8,128)(2,1)}, u32[]{:S(2)}, u32[]{:S(2)}) %all-to-all-start.1) | async-done | bytes 3145760 | tf_op jit(solution)/shard_map/all_to_all | solution.py:54
  99.4 4.3 %gather_fusion.1 = bf16[16,128,768]{2,1,0:T(8,128)(2,1)} fusion(bf16[16,128,768]{2,1,0:T(8,128)(2,1)} %bitcast.14, s32[1024]{0:T(1024)S(1)} %pad_clamp_fusion), kind=kCustom, calls=%fused_computation.1 | custom fusion | bytes 6291520 | tf_op jit(solution)/shard_map/gather | solution.py:61
  103.8 0.0 copy-done
  103.8 6.2 %convolution_convert_fusion.1 = bf16[2048,768]{1,0:T(8,128)(2,1)} fusion(bf16[2048,768]{1,0:T(8,128)(2,1)} %bitcast.100, bf16[768,768]{1,0:T(8,128)(2,1)S(1)} %copy-done), kind=kOutput, calls=%fused_computation.27 | convolution fusion | flops 2417491968 | bytes 7471104 | tf_op jit(solution)/shard_map/dot_general | solution.py:65
  110.0 4.8 %copy.40 = bf16[2048,768]{0,1:T(8,128)(2,1)} copy(bf16[2048,768]{1,0:T(8,128)(2,1)} %convolution_convert_fusion.1) | data formatting | bytes 6291456 | tf_op jit(solution)/shard_map/convert_element_type | solution.py:65
  114.7 0.0 copy-start.2
  114.7 4.7 %copy.56 = bf16[96,8,16,128]{3,2,1,0:T(8,128)(2,1)} copy(bf16[96,8,16,128]{3,1,2,0:T(8,128)(2,1)} %bitcast.97) | data formatting | bytes 6291456
  119.4 0.0 copy-done.2
  119.5 0.0 copy-done.7
  119.5 4.0 %convolution_convert_fusion = bf16[2048,768]{1,0:T(8,128)(2,1)} fusion(bf16[2048,768]{1,0:T(8,128)(2,1)S(1)} %bitcast.101, bf16[768,768]{1,0:T(8,128)(2,1)S(1)} %copy-done.7), kind=kOutput, calls=%fused_computation.26 | convolution fusion | flops 2417491968 | bytes 7471104 | tf_op jit(solution)/shard_map/dot_general | solution.py:64
  123.4 4.8 %copy.41 = bf16[2048,768]{0,1:T(8,128)(2,1)} copy(bf16[2048,768]{1,0:T(8,128)(2,1)} %convolution_convert_fusion) | data formatting | bytes 6291456 | tf_op jit(solution)/shard_map/convert_element_type | solution.py:64
  128.2 4.7 %copy.57 = bf16[96,8,16,128]{3,2,1,0:T(8,128)(2,1)} copy(bf16[96,8,16,128]{3,1,2,0:T(8,128)(2,1)} %bitcast.98) | data formatting | bytes 6291456
  132.8 0.0 copy-done.4
  132.9 0.0 copy-done.6
  132.9 24.7 %while.10 = (s32[]{:T(128)}, bf16[2,128,768]{2,1,0:T(8,128)(2,1)S(1)}, s32[2]{0:T(128)S(1)}, bf16[2,8,128,12,64]{2,1,0,4,3:T(8,128)(2,1)}, bf16[2,8,128,12,64]{2...) while((s32[]{:T(128)}, bf16[2,128,768]{2,1,0:T(8,128)(2,1)S(1)}, s32[2]{0:T(128)S(1)}, ...), condition=%wide.region_9.10_spmd, body=%wide.region_5.9_spmd.sunk | while | flops 413761664 | bytes 36667524 | solution.py:88
  132.9 2.2 %constant_dynamic-slice_fusion.3 = (bf16[1,8,128,12,64]{2,1,0,4,3:T(8,128)(2,1)S(1)}, bf16[1,8,128,12,64]{2,1,0,4,3:T(8,128)(2,1)S(1)}) fusion(bf16[2,8,128,12,64]{2,1,0,4,3:T(8,128)(2,1)} %get-tuple-element.155, s32[]{:T(128)} %get-tuple-element.144, bf16[2,8,128,12,64]{2,1,0,4,3:T(8,128)(2,1)} %get-tuple-element.154), kind=kLoop, calls=%fused_computation.22.clone.1 | loop fusion | bytes 6291460 | tf_op jit(solution)/shard_map/while/body/jit(dynamic_index_in_dim)/dynamic_slice | solution.py:88
  135.0 1.1 fusion.46
  136.1 5.9 %fusion.47 = (f32[12,8,128]{2,1,0:T(8,128)S(1)}, f32[12,8,128,128]{2,3,1,0:T(8,128)S(1)}) fusion(f32[12,8,128,128]{3,2,1,0:T(8,128)S(1)} %fusion.46), kind=kOutput, calls=%fused_computation.70.clone.1 | output fusion | flops 6291583 | bytes 12632064 | tf_op jit(solution)/shard_map/while/body/eval_jaxpr/sub | solution.py:78
  142.0 0.6 dynamic_slice.26
  142.6 0.6 iota_compare_fusion.4
  143.3 1.0 select_reduce_fusion.3
  145.0 0.1 copy.73
  145.2 2.2 %constant_dynamic-slice_fusion.3 = (bf16[1,8,128,12,64]{2,1,0,4,3:T(8,128)(2,1)S(1)}, bf16[1,8,128,12,64]{2,1,0,4,3:T(8,128)(2,1)S(1)}) fusion(bf16[2,8,128,12,64]{2,1,0,4,3:T(8,128)(2,1)} %get-tuple-element.155, s32[]{:T(128)} %get-tuple-element.144, bf16[2,8,128,12,64]{2,1,0,4,3:T(8,128)(2,1)} %get-tuple-element.154), kind=kLoop, calls=%fused_computation.22.clone.1 | loop fusion | bytes 6291460 | tf_op jit(solution)/shard_map/while/body/jit(dynamic_index_in_dim)/dynamic_slice | solution.py:88
  147.4 1.1 fusion.46
  148.5 5.9 %fusion.47 = (f32[12,8,128]{2,1,0:T(8,128)S(1)}, f32[12,8,128,128]{2,3,1,0:T(8,128)S(1)}) fusion(f32[12,8,128,128]{3,2,1,0:T(8,128)S(1)} %fusion.46), kind=kOutput, calls=%fused_computation.70.clone.1 | output fusion | flops 6291583 | bytes 12632064 | tf_op jit(solution)/shard_map/while/body/eval_jaxpr/sub | solution.py:78
  154.4 0.6 dynamic_slice.26
  155.0 0.6 iota_compare_fusion.4
  155.7 1.0 select_reduce_fusion.3
  157.4 0.1 copy.73
  157.6 2.5 %fusion.16 = bf16[256,768]{1,0:T(8,128)(2,1)} fusion(bf16[256,768]{1,0:T(8,128)(2,1)S(1)} %bitcast.102, bf16[768,768]{1,0:T(8,128)(2,1)} %param.19, bf16[256,768]{1,0:T(8,128)(2,1)S(1)} %bitcast.99), kind=kOutput, calls=%fused_computation.30 | convolution fusion | flops 302579712 | bytes 2359296 | tf_op jit(solution)/shard_map/dot_general | solution.py:89
  (14 shorter events, 0.2 us)
Async XLA Ops:
  0.0 103.8 %copy-start = (bf16[768,768]{1,0:T(8,128)(2,1)S(1)}, bf16[768,768]{1,0:T(8,128)(2,1)}, u32[]{:S(2)}) copy-start(bf16[768,768]{1,0:T(8,128)(2,1)} %param.18) | copy-start | bytes 3538948
  5.0 10.3 %all-to-all-start = ((s32[16,1,1]{2,1,0:T(1,128)}), s32[16,1,1]{2,1,0:T(1,128)S(1)}, u32[]{:S(2)}, u32[]{:S(2)}) async-start(s32[16,1,1]{2,1,0:T(1,128)} %copy.39), calls=%async_computation | async-start | bytes 16384 | tf_op jit(solution)/shard_map/all_to_all | solution.py:49
  22.3 7.1 %copy-start.1 = (bf16[2,128,768]{2,1,0:T(8,128)(2,1)S(1)}, bf16[2,128,768]{2,1,0:T(8,128)(2,1)}, u32[]{:S(2)}) copy-start(bf16[2,128,768]{2,1,0:T(8,128)(2,1)} %param.11) | copy-start | bytes 1179652
  22.3 7.1 %copy-start.5 = (f32[768]{0:T(1024)S(1)}, f32[768]{0:T(1024)}, u32[]{:S(2)}) copy-start(f32[768]{0:T(1024)} %param.14) | copy-start | bytes 9220
  22.3 7.3 %copy-start.3 = (bf16[768,768]{1,0:T(8,128)(2,1)S(1)}, bf16[768,768]{1,0:T(8,128)(2,1)}, u32[]{:S(2)}) copy-start(bf16[768,768]{1,0:T(8,128)(2,1)} %param.16) | copy-start | bytes 3538948
  22.3 77.1 %all-to-all-start.1 = ((bf16[16,1,128,768]{3,2,1,0:T(8,128)(2,1)}), bf16[16,1,128,768]{3,2,1,0:T(8,128)(2,1)}, u32[]{:S(2)}, u32[]{:S(2)}) async-start(bf16[16,1,128,768]{3,2,1,0:T(8,128)(2,1)} %bitcast_select_fusion), calls=%async_computation.1 | async-start | bytes 6291456 | tf_op jit(solution)/shard_map/all_to_all | solution.py:54
  114.7 4.7 %copy-start.2 = (bf16[16,128,768]{2,1,0:T(8,128)(2,1)S(1)}, bf16[16,128,768]{2,1,0:T(8,128)(2,1)}, u32[]{:S(2)}) copy-start(bf16[16,128,768]{2,1,0:T(8,128)(2,1)} %gather_fusion.1) | copy-start | bytes 9437188
  114.7 4.7 %copy-start.7 = (bf16[768,768]{1,0:T(8,128)(2,1)S(1)}, bf16[768,768]{1,0:T(8,128)(2,1)}, u32[]{:S(2)}) copy-start(bf16[768,768]{1,0:T(8,128)(2,1)} %param.17) | copy-start | bytes 3538948
  128.2 4.7 %copy-start.4 = (bf16[2,128,768]{2,1,0:T(8,128)(2,1)S(1)}, bf16[2,128,768]{2,1,0:T(8,128)(2,1)}, u32[]{:S(2)}) copy-start(bf16[2,128,768]{2,1,0:T(8,128)(2,1)} %custom-call.4) | copy-start | bytes 1179652
  128.2 4.7 %copy-start.6 = (s32[2]{0:T(128)S(1)}, s32[2]{0:T(128)}, u32[]{:S(2)}) copy-start(s32[2]{0:T(128)} %param.13) | copy-start | bytes 28
where the time goes:
time: 161 us; the launch traced here: 160 us
  waiting for transfers between devices  69 us (43%)
  local copies, waits for them, and re-layouts  34.3 us (21%)
  other arithmetic  24.2 us (15%)
  matrix products  17.4 us (11%)
  starting transfers between devices  13.6 us (8%)
    all_to_all x1, waiting for transfers between devices, shards(): lax.all_to_all(jnp.where(used[:, :, None, None], picked, jnp.zeros_like(p...  68.9 us
    sub x2, other arithmetic, one_image(): probs = jax.nn.softmax(scores, axis=-1).astype(jnp.bfloat16)  11.8 us
    unnamed x18, local copies, waits for them, and re-layouts  9.42 us
    all_to_all x1, starting transfers between devices, shards(): lax.all_to_all(jnp.where(used[:, :, None, None], picked, jnp.zeros_like(p...  7.08 us
    all_to_all x1, starting transfers between devices, shards(): lax.all_to_all(request, 'img', split_axis=0, concat_axis=0, tiled=True)  6.55 us
    dot_general x1, matrix products, shards(): jnp.dot(pair_memory, w_value, preferred_element_type=jnp.float32)  6.18 us
    dynamic_slice x4, local copies, waits for them, and re-layouts, shards(): lax.map(one_image, (queries, pair_keys, pair_values, counts))  5.53 us
    convert_element_type x1, local copies, waits for them, and re-layouts, shards(): jnp.dot(pair_memory, w_value, preferred_element_type=jnp.float32)  4.76 us
  transfers between devices with their start and end apart: 2, of which 2 were waited for; matrix products, arithmetic and copies ran while one was open for 3% of the time, Pallas kernels for 0%

commit v1 on v0

v1 whole, which is shorter than its diff:
```python
import functools

import jax
import jax.numpy as jnp
from jax import lax
from jax.experimental import pallas as pl
from jax.experimental.pallas import tpu as pltpu
from jax.sharding import PartitionSpec as P

HEADS = 12
HEAD_DIM = 64
CORES = 2
PAIRED = 2 * HEAD_DIM


class Ring:
    def __init__(self, devices, columns):
        self.chips = devices // CORES
        self.columns = columns
        self.rows = self.chips // columns

    def chip(self, place):
        if self.columns == 1:
            return place
        if place < self.rows:
            return place * 2
        return (2 * self.rows - 1 - place) * 2 + 1

    def onward(self):
        pairs = []
        for place in range(self.chips):
            for core, step in ((0, 1), (1, -1)):
                target = self.chip((place + step) % self.chips)
                pairs.append((self.chip(place) * CORES + core, target * CORES + core))
        return pairs

    def sibling(self):
        return [(i, i ^ 1) for i in range(self.chips * CORES)]

    def owner(self, me, step, flip):
        chip = me // CORES
        core = lax.rem(me, CORES)
        if self.columns == 1:
            place = chip
        else:
            row = chip // 2
            place = jnp.where(lax.rem(chip, 2) == 0, row, 2 * self.rows - 1 - row)
        if flip:
            core = 1 - core
        came = lax.rem(place + self.chips + jnp.where(core == 0, -step, step), self.chips)
        if self.columns == 1:
            there = came
        else:
            there = jnp.where(came < self.rows, came * 2, (2 * self.rows - 1 - came) * 2 + 1)
        return there * CORES + core


def normalize(rows, gain):
    rows = rows.astype(jnp.float32)
    center = rows - jnp.mean(rows, axis=-1, keepdims=True)
    spread = jnp.mean(center * center, axis=-1, keepdims=True)
    return center * lax.rsqrt(spread + 1e-06) * gain


def dot(a, b, dims=((1,), (0,))):
    return lax.dot_general(a, b, (dims, ((), ())), preferred_element_type=jnp.float32)


def find_slot(owner, partners, counts, own, listed):
    image = jnp.int32(0)
    index = jnp.int32(0)
    live = jnp.int32(0)
    for a in range(own):
        for k in range(listed):
            partner = partners[a, k]
            hit = jnp.logical_and(k < counts[a], partner // own == owner)
            image = jnp.where(hit, a, image)
            index = jnp.where(hit, lax.rem(partner, own), index)
            live = jnp.where(hit, 1, live)
    return image, index, live


def stage_kernel(ring, slots, first, last, own, listed, tok, *refs):
    refs = list(refs)
    take = lambda n: [refs.pop(0) for _ in range(n)]
    sources = [take(own) for _ in slots]
    partners, counts, gain_memory, w_key = take(4)
    if first:
        tokens, gain_query, w_query, w_value = take(4)
    else:
        w_value_t, spread_q, total_in = take(3)
    if last:
        tokens, w_out = take(2)
    if last:
        (mixed,) = take(1)
        total = refs.pop()
    elif first:
        total, spread_q, w_value_t = take(3)
    else:
        (total,) = take(1)
    memory, sems = take(2)

    me = lax.axis_index("img")
    found = [find_slot(ring.owner(me, step, flip), partners, counts, own, listed) for step, flip in slots]
    for at, (image, index, live) in enumerate(found):
        for j in range(own):

            @pl.when(index == j)
            def _():
                pltpu.make_async_copy(sources[at][j], memory.at[at], sems.at[at]).start()

    if first:
        rows = tokens[...].reshape(own * tok, -1)
        normed_query = normalize(rows, gain_query[...]).astype(jnp.bfloat16)
        queries = dot(normed_query, w_query[...]).astype(jnp.bfloat16).astype(jnp.float32)
        queries_t = (queries * (1.0 / HEAD_DIM**0.5)).T.astype(jnp.bfloat16)
        zero = jnp.zeros((HEAD_DIM, tok), jnp.bfloat16)
        for a in range(own):
            for h in range(HEADS):
                part = queries_t[h * HEAD_DIM : (h + 1) * HEAD_DIM, a * tok : (a + 1) * tok]
                pieces = [part, zero] if h % 2 == 0 else [zero, part]
                spread_q[a, h * HEAD_DIM : (h + 1) * HEAD_DIM, :] = jnp.concatenate(pieces, axis=1)
        w_value_t[...] = w_value[...].astype(jnp.float32).T.astype(jnp.bfloat16)
        total[...] = jnp.zeros_like(total)
    else:
        total[...] = total_in[...]

    for at in range(len(slots)):
        pltpu.make_async_copy(sources[at][0], memory.at[at], sems.at[at]).wait()
    rows = memory[...].reshape(len(slots) * tok, -1)
    normed = normalize(rows, gain_memory[...]).astype(jnp.bfloat16)
    keys = dot(normed, w_key[...]).astype(jnp.bfloat16)
    values_t = dot(w_value_t[...], normed, ((1,), (1,))).astype(jnp.bfloat16)
    for at, (image, index, live) in enumerate(found):
        here = slice(at * tok, (at + 1) * tok)
        for g in range(HEADS // 2):
            both = slice(g * PAIRED, (g + 1) * PAIRED)
            scores = dot(keys[here, both], spread_q[image, both, :])
            weights = jnp.exp(scores - jnp.max(scores, axis=0, keepdims=True))
            share = live.astype(jnp.float32) / jnp.sum(weights, axis=0, keepdims=True)
            weights = weights.astype(jnp.bfloat16)
            for h in range(2):
                feats = slice(g * PAIRED + h * HEAD_DIM, g * PAIRED + (h + 1) * HEAD_DIM)
                asked = slice(h * tok, (h + 1) * tok)
                part = dot(values_t[feats, here], weights[:, asked])
                total[image, feats, :] += part * share[:, asked]

    if last:
        for a in range(own):
            context = (total[a] / counts[a].astype(jnp.float32)).T.astype(jnp.bfloat16)
            out = tokens[a].astype(jnp.float32) + dot(context, w_out[...])
            mixed[a] = out.astype(jnp.bfloat16)


def stage(ring, slots, sources, shared, extra, first, last, own, listed, tok, width):
    smem = pl.BlockSpec(memory_space=pltpu.SMEM)
    vmem = pl.BlockSpec(memory_space=pltpu.VMEM)
    where = [pl.BlockSpec(memory_space=pl.ANY)] * (len(slots) * own) + [smem, smem]
    where += [vmem] * (2 + len(extra))
    operands = [image for images in sources for image in images] + list(shared) + list(extra)
    total = jax.ShapeDtypeStruct((own, width, tok), jnp.float32)
    spread_q = jax.ShapeDtypeStruct((own, width, 2 * tok), jnp.bfloat16)
    w_value_t = jax.ShapeDtypeStruct((width, width), jnp.bfloat16)
    scratch = [pltpu.VMEM((len(slots), tok, width), jnp.bfloat16), pltpu.SemaphoreType.DMA((len(slots),))]
    aliases = {}
    if last:
        shapes = [jax.ShapeDtypeStruct((own, tok, width), jnp.bfloat16)]
        scratch.append(pltpu.VMEM(total.shape, total.dtype))
    elif first:
        shapes = [total, spread_q, w_value_t]
    else:
        shapes = [total]
        aliases = {len(slots) * own + 6: 0}
    rows = len(slots) * tok
    return pl.pallas_call(
        functools.partial(stage_kernel, ring, slots, first, last, own, listed, tok),
        out_shape=shapes,
        in_specs=where,
        out_specs=[vmem] * len(shapes),
        scratch_shapes=scratch,
        input_output_aliases=aliases,
        compiler_params=pltpu.CompilerParams(vmem_limit_bytes=32 << 20),
        cost_estimate=pl.CostEstimate(
            flops=4 * rows * width * (width + tok) * 2,
            bytes_accessed=2 * width * width * 2 + 3 * rows * width * 2,
            transcendentals=rows * tok * HEADS,
        ),
    )(*operands)


def shards(columns, tokens, partners, counts, gain_query, gain_memory, w_query, w_key, w_value, w_out):
    own, tok, width = tokens.shape
    listed = partners.shape[1]
    ring = Ring(lax.axis_size("img"), columns)
    onward, sibling = ring.onward(), ring.sibling()
    gain_query = gain_query.reshape(1, width)
    gain_memory = gain_memory.reshape(1, width)
    shared = (partners, counts, gain_memory, w_key)
    call = functools.partial(stage, ring, own=own, listed=listed, tok=tok, width=width)

    mine = [tokens[j] for j in range(own)]
    theirs = [lax.ppermute(image, "img", sibling) for image in mine]
    for step in range(ring.chips):
        first, last = step == 0, step == ring.chips - 1
        slots = ((step, False), (step, True))
        if first:
            extra = (tokens, gain_query, w_query, w_value)
        else:
            extra = (w_value_t, spread_q, total)
        if last:
            extra += (tokens, w_out)
        if not last:
            mine_next = [lax.ppermute(image, "img", onward) for image in mine]
            theirs_next = [lax.ppermute(image, "img", sibling) for image in mine_next]
        out = call(slots, (mine, theirs), shared, extra, first, last)
        if last:
            return out[0]
        if first:
            total, spread_q, w_value_t = out
        else:
            (total,) = out
        mine, theirs = mine_next, theirs_next


def solution(mesh):
    placed = (
        P(("groups", "img"), None, None),
        P(("groups", "img"), None),
        P(("groups", "img")),
        P(),
        P(),
        P(),
        P(),
        P(),
        P(),
    )
    columns = max(1, 4 // mesh.shape["groups"])
    return jax.shard_map(
        functools.partial(shards, columns),
        mesh=mesh,
        in_specs=placed,
        out_specs=P(("groups", "img"), None, None),
        check_vma=False,
    )
```

time: 161 us -> 79.9 us (0.50)
  the two profiles are of different devices: /device:TPU:13 before, /device:TPU:0 now
where the time goes in v1:
time: 79.9 us; the launch traced here: 79.6 us
  Pallas kernels  35.1 us (44%)
  starting transfers between devices  30 us (38%)
  local copies, waits for them, and re-layouts  8.59 us (11%)
  waiting for transfers between devices  5.54 us (7%)
    pallas_call x8, Pallas kernels, stage(): pl.pallas_call(functools.partial(stage_kernel, ring, slots, first, last,...  35.1 us
    ppermute x14, starting transfers between devices, shards(): mine_next = [lax.ppermute(image, 'img', onward) for image in mine]  26.4 us
    unnamed x20, local copies, waits for them, and re-layouts  6.16 us
    ppermute x14, waiting for transfers between devices, shards(): mine_next = [lax.ppermute(image, 'img', onward) for image in mine]  5.5 us
    ppermute x14, starting transfers between devices, shards(): theirs_next = [lax.ppermute(image, 'img', sibling) for image in mine_next]  3.07 us
  transfers between devices with their start and end apart: 30, of which 4 were waited for; matrix products, arithmetic and copies ran while one was open for 2% of the time, Pallas kernels for 37%

profile of v1, /device:TPU:0, one launch (start us, length us, event | category | flops | bytes accessed | tf_op | source)
XLA Modules:
  0.0 79.6 jit_solution(6176133700356115224)
XLA Ops:
  0.0 1.0 %slice_bitcast_fusion = (bf16[128,768]{1,0:T(8,128)(2,1)S(1)}, bf16[128,768]{1,0:T(8,128)(2,1)S(1)}) fusion(bf16[2,128,768]{2,1,0:T(8,128)(2,1)} %refs_11_.3), kind=kLoop, calls=%fused_computation | loop fusion | bytes 786432 | tf_op jit(solution)/shard_map/squeeze | solution.py:201
  1.1 3.1 %collective-permute-start = (bf16[128,768]{1,0:T(8,128)(2,1)S(1)}, bf16[128,768]{1,0:T(8,128)(2,1)S(1)}, u32[]{:S(2)}, u32[]{:S(2)}) collective-permute-start(bf16[128,768]{1,0:T(8,128)(2,1)S(1)} %get-tuple-element.12.refs_0_), channel_id=1, source_target_pairs={{0,4},{1,3},{4,8},{5,1},{8,12},{9,5},{12,14},{13,9},{14,10},{15,13... | collective-permute-start | bytes 589832 | tf_op jit(solution)/shard_map/ppermute | solution.py:213
  4.1 1.6 %collective-permute-start.7 = (bf16[128,768]{1,0:T(8,128)(2,1)S(1)}, bf16[128,768]{1,0:T(8,128)(2,1)S(1)}, u32[]{:S(2)}, u32[]{:S(2)}) collective-permute-start(bf16[128,768]{1,0:T(8,128)(2,1)S(1)} %get-tuple-element.11.refs_1_), channel_id=1, source_target_pairs={{0,4},{1,3},{4,8},{5,1},{8,12},{9,5},{12,14},{13,9},{14,10},{15,13... | collective-permute-start | bytes 589832 | tf_op jit(solution)/shard_map/ppermute | solution.py:213
  5.7 2.0 %collective-permute-done.refs_0_ = bf16[128,768]{1,0:T(8,128)(2,1)S(1)} collective-permute-done((bf16[128,768]{1,0:T(8,128)(2,1)S(1)}, bf16[128,768]{1,0:T(8,128)(2,1)S(1)}, u32[]{:S(2)}, u32[]{:S(2)}) %collective-permute-start) | collective-permute-done | bytes 196640 | tf_op jit(solution)/shard_map/ppermute | solution.py:213
  7.7 2.1 %collective-permute-start.1 = (bf16[128,768]{1,0:T(8,128)(2,1)S(1)}, bf16[128,768]{1,0:T(8,128)(2,1)S(1)}, u32[]{:S(2)}, u32[]{:S(2)}) collective-permute-start(bf16[128,768]{1,0:T(8,128)(2,1)S(1)} %collective-permute-done.refs_0_), channel_id=1, source_target_pairs={{0,4},{1,3},{4,8},{5,1},{8,12},{9,5},{12,14},{13,9},{14,10},{15,13... | collective-permute-start | bytes 589832 | tf_op jit(solution)/shard_map/ppermute | solution.py:213
  9.8 0.0 collective-permute-done.7.refs_1_
  9.8 2.1 %collective-permute-start.8 = (bf16[128,768]{1,0:T(8,128)(2,1)S(1)}, bf16[128,768]{1,0:T(8,128)(2,1)S(1)}, u32[]{:S(2)}, u32[]{:S(2)}) collective-permute-start(bf16[128,768]{1,0:T(8,128)(2,1)S(1)} %collective-permute-done.7.refs_1_), channel_id=1, source_target_pairs={{0,4},{1,3},{4,8},{5,1},{8,12},{9,5},{12,14},{13,9},{14,10},{15,13... | collective-permute-start | bytes 589832 | tf_op jit(solution)/shard_map/ppermute | solution.py:213
  11.9 1.5 %collective-permute-done.1.refs_0_ = bf16[128,768]{1,0:T(8,128)(2,1)S(1)} collective-permute-done((bf16[128,768]{1,0:T(8,128)(2,1)S(1)}, bf16[128,768]{1,0:T(8,128)(2,1)S(1)}, u32[]{:S(2)}, u32[]{:S(2)}) %collective-permute-start.1) | collective-permute-done | bytes 196640 | tf_op jit(solution)/shard_map/ppermute | solution.py:213
  13.4 2.1 %collective-permute-start.2 = (bf16[128,768]{1,0:T(8,128)(2,1)S(1)}, bf16[128,768]{1,0:T(8,128)(2,1)S(1)}, u32[]{:S(2)}, u32[]{:S(2)}) collective-permute-start(bf16[128,768]{1,0:T(8,128)(2,1)S(1)} %collective-permute-done.1.refs_0_), channel_id=1, source_target_pairs={{0,4},{1,3},{4,8},{5,1},{8,12},{9,5},{12,14},{13,9},{14,10},{15,13... | collective-permute-start | bytes 589832 | tf_op jit(solution)/shard_map/ppermute | solution.py:213
  15.5 0.0 collective-permute-done.8.refs_1_
  15.5 2.1 %collective-permute-start.9 = (bf16[128,768]{1,0:T(8,128)(2,1)S(1)}, bf16[128,768]{1,0:T(8,128)(2,1)S(1)}, u32[]{:S(2)}, u32[]{:S(2)}) collective-permute-start(bf16[128,768]{1,0:T(8,128)(2,1)S(1)} %collective-permute-done.8.refs_1_), channel_id=1, source_target_pairs={{0,4},{1,3},{4,8},{5,1},{8,12},{9,5},{12,14},{13,9},{14,10},{15,13... | collective-permute-start | bytes 589832 | tf_op jit(solution)/shard_map/ppermute | solution.py:213
  17.6 0.0 collective-permute-start.16
  17.6 0.5 collective-permute-start.17
  18.1 0.0 collective-permute-start.28
  18.1 1.0 %collective-permute-done.2.refs_0_ = bf16[128,768]{1,0:T(8,128)(2,1)S(1)} collective-permute-done((bf16[128,768]{1,0:T(8,128)(2,1)S(1)}, bf16[128,768]{1,0:T(8,128)(2,1)S(1)}, u32[]{:S(2)}, u32[]{:S(2)}) %collective-permute-start.2) | collective-permute-done | bytes 196640 | tf_op jit(solution)/shard_map/ppermute | solution.py:213
  19.1 2.1 %collective-permute-start.3 = (bf16[128,768]{1,0:T(8,128)(2,1)S(1)}, bf16[128,768]{1,0:T(8,128)(2,1)S(1)}, u32[]{:S(2)}, u32[]{:S(2)}) collective-permute-start(bf16[128,768]{1,0:T(8,128)(2,1)S(1)} %collective-permute-done.2.refs_0_), channel_id=1, source_target_pairs={{0,4},{1,3},{4,8},{5,1},{8,12},{9,5},{12,14},{13,9},{14,10},{15,13... | collective-permute-start | bytes 589832 | tf_op jit(solution)/shard_map/ppermute | solution.py:213
  21.1 0.0 collective-permute-done.9.refs_1_
  21.2 2.1 %collective-permute-start.10 = (bf16[128,768]{1,0:T(8,128)(2,1)S(1)}, bf16[128,768]{1,0:T(8,128)(2,1)S(1)}, u32[]{:S(2)}, u32[]{:S(2)}) collective-permute-start(bf16[128,768]{1,0:T(8,128)(2,1)S(1)} %collective-permute-done.9.refs_1_), channel_id=1, source_target_pairs={{0,4},{1,3},{4,8},{5,1},{8,12},{9,5},{12,14},{13,9},{14,10},{15,13... | collective-permute-start | bytes 589832 | tf_op jit(solution)/shard_map/ppermute | solution.py:213
  23.3 0.5 collective-permute-start.26
  23.8 0.1 collective-permute-start.27
  23.8 0.9 %collective-permute-done.3.refs_0_ = bf16[128,768]{1,0:T(8,128)(2,1)S(1)} collective-permute-done((bf16[128,768]{1,0:T(8,128)(2,1)S(1)}, bf16[128,768]{1,0:T(8,128)(2,1)S(1)}, u32[]{:S(2)}, u32[]{:S(2)}) %collective-permute-start.3) | collective-permute-done | bytes 196640 | tf_op jit(solution)/shard_map/ppermute | solution.py:213
  24.7 2.1 %collective-permute-start.4 = (bf16[128,768]{1,0:T(8,128)(2,1)S(1)}, bf16[128,768]{1,0:T(8,128)(2,1)S(1)}, u32[]{:S(2)}, u32[]{:S(2)}) collective-permute-start(bf16[128,768]{1,0:T(8,128)(2,1)S(1)} %collective-permute-done.3.refs_0_), channel_id=1, source_target_pairs={{0,4},{1,3},{4,8},{5,1},{8,12},{9,5},{12,14},{13,9},{14,10},{15,13... | collective-permute-start | bytes 589832 | tf_op jit(solution)/shard_map/ppermute | solution.py:213
  26.8 0.0 collective-permute-done.10.refs_1_
  26.8 2.1 %collective-permute-start.11 = (bf16[128,768]{1,0:T(8,128)(2,1)S(1)}, bf16[128,768]{1,0:T(8,128)(2,1)S(1)}, u32[]{:S(2)}, u32[]{:S(2)}) collective-permute-start(bf16[128,768]{1,0:T(8,128)(2,1)S(1)} %collective-permute-done.10.refs_1_), channel_id=1, source_target_pairs={{0,4},{1,3},{4,8},{5,1},{8,12},{9,5},{12,14},{13,9},{14,10},{15,13... | collective-permute-start | bytes 589832 | tf_op jit(solution)/shard_map/ppermute | solution.py:213
  28.9 0.7 reshape.6.refs_6_
  29.6 0.7 reshape.7.refs_9_
  30.3 0.0 collective-permute-done.29.refs_3_
  30.3 0.0 collective-permute-start.24
  30.3 0.5 collective-permute-start.25
  30.8 1.3 %copy-done = bf16[768,768]{1,0:T(8,128)(2,1)S(1)} copy-done((bf16[768,768]{1,0:T(8,128)(2,1)S(1)}, bf16[768,768]{1,0:T(8,128)(2,1)}, u32[]{:S(2)}) %copy-start) | copy-done | bytes 1179672
  32.1 1.0 %copy-done.2 = bf16[2,128,768]{2,1,0:T(8,128)(2,1)S(1)} copy-done((bf16[2,128,768]{2,1,0:T(8,128)(2,1)S(1)}, bf16[2,128,768]{2,1,0:T(8,128)(2,1)}, u32[]{:S(2)}) %copy-start.2) | copy-done | bytes 393240
  33.1 0.7 copy-done.4
  33.8 0.7 copy-done.6
  34.4 1.3 %copy-done.8 = bf16[768,768]{1,0:T(8,128)(2,1)S(1)} copy-done((bf16[768,768]{1,0:T(8,128)(2,1)S(1)}, bf16[768,768]{1,0:T(8,128)(2,1)}, u32[]{:S(2)}) %copy-start.8) | copy-done | bytes 1179672
  35.7 1.3 %copy-done.9 = bf16[768,768]{1,0:T(8,128)(2,1)S(1)} copy-done((bf16[768,768]{1,0:T(8,128)(2,1)S(1)}, bf16[768,768]{1,0:T(8,128)(2,1)}, u32[]{:S(2)}) %copy-start.9) | copy-done | bytes 1179672
  37.0 5.3 %shard_map.91 = (f32[2,768,128]{2,1,0:T(8,128)S(1)}, bf16[2,768,256]{2,1,0:T(8,128)(2,1)S(1)}, bf16[768,768]{1,0:T(8,128)(2,1)S(1)}) custom-call(bf16[128,768]{1,0:T(8,128)(2,1)S(1)} %get-tuple-element.12.refs_0_, bf16[128,768]{1,0:T(8,128)(2,1)S(1)} %get-tuple-element.11.refs_1_, bf16[128,768]{1,0:T(8,128)(2,1)S(1)} %collective-permute-done.16.refs_2_, ...), custom_call_target="tpu_custom_call" | custom-call | flops 1409286144 | bytes 3538944 | tf_op jit(solution)/shard_map/pallas_call | solution.py:175
  42.2 0.0 collective-permute-done.27.refs_3_
  42.2 0.1 collective-permute-start.22
  42.4 1.6 %collective-permute-start.5 = (bf16[128,768]{1,0:T(8,128)(2,1)S(1)}, bf16[128,768]{1,0:T(8,128)(2,1)S(1)}, u32[]{:S(2)}, u32[]{:S(2)}) collective-permute-start(bf16[128,768]{1,0:T(8,128)(2,1)S(1)} %collective-permute-done.4.refs_0_), channel_id=1, source_target_pairs={{0,4},{1,3},{4,8},{5,1},{8,12},{9,5},{12,14},{13,9},{14,10},{15,13... | collective-permute-start | bytes 589832 | tf_op jit(solution)/shard_map/ppermute | solution.py:213
  44.0 0.0 collective-permute-done.11.refs_1_
  44.0 1.6 %collective-permute-start.12 = (bf16[128,768]{1,0:T(8,128)(2,1)S(1)}, bf16[128,768]{1,0:T(8,128)(2,1)S(1)}, u32[]{:S(2)}, u32[]{:S(2)}) collective-permute-start(bf16[128,768]{1,0:T(8,128)(2,1)S(1)} %collective-permute-done.11.refs_1_), channel_id=1, source_target_pairs={{0,4},{1,3},{4,8},{5,1},{8,12},{9,5},{12,14},{13,9},{14,10},{15,13... | collective-permute-start | bytes 589832 | tf_op jit(solution)/shard_map/ppermute | solution.py:213
  45.5 4.1 %shard_map.92.refs_10_ = f32[2,768,128]{2,1,0:T(8,128)S(1)} custom-call(bf16[128,768]{1,0:T(8,128)(2,1)S(1)} %collective-permute-done.refs_0_, bf16[128,768]{1,0:T(8,128)(2,1)S(1)} %collective-permute-done.7.refs_1_, bf16[128,768]{1,0:T(8,128)(2,1)S(1)} %collective-permute-done.28.refs_2_, ...), custom_call_target="tpu_custom_call", output_to_operand_aliasing={{}: (10, {})} | custom-call | flops 1409286144 | bytes 3538944 | tf_op jit(solution)/shard_map/pallas_call | solution.py:175
  49.6 0.0 copy-start.5
  49.6 0.0 copy-start.7
  49.6 0.0 collective-permute-done.24.refs_2_
  49.6 0.1 collective-permute-start.23
  49.7 0.0 collective-permute-done.25.refs_3_
  49.7 0.5 collective-permute-start.20
  50.2 4.1 %shard_map.93.refs_10_ = f32[2,768,128]{2,1,0:T(8,128)S(1)} custom-call(bf16[128,768]{1,0:T(8,128)(2,1)S(1)} %collective-permute-done.1.refs_0_, bf16[128,768]{1,0:T(8,128)(2,1)S(1)} %collective-permute-done.8.refs_1_, bf16[128,768]{1,0:T(8,128)(2,1)S(1)} %collective-permute-done.26.refs_2_, ...), custom_call_target="tpu_custom_call", output_to_operand_aliasing={{}: (10, {})} | custom-call | flops 1409286144 | bytes 3538944 | tf_op jit(solution)/shard_map/pallas_call | solution.py:175
  54.3 0.1 collective-permute-start.21
  54.5 0.0 collective-permute-done.5.refs_0_
  54.5 1.5 %collective-permute-start.6 = (bf16[128,768]{1,0:T(8,128)(2,1)S(1)}, bf16[128,768]{1,0:T(8,128)(2,1)S(1)}, u32[]{:S(2)}, u32[]{:S(2)}) collective-permute-start(bf16[128,768]{1,0:T(8,128)(2,1)S(1)} %collective-permute-done.5.refs_0_), channel_id=1, source_target_pairs={{0,4},{1,3},{4,8},{5,1},{8,12},{9,5},{12,14},{13,9},{14,10},{15,13... | collective-permute-start | bytes 589832 | tf_op jit(solution)/shard_map/ppermute | solution.py:213
  56.0 0.0 collective-permute-done.12.refs_1_
  56.0 0.4 collective-permute-start.13
  56.4 4.2 %shard_map.94.refs_10_ = f32[2,768,128]{2,1,0:T(8,128)S(1)} custom-call(bf16[128,768]{1,0:T(8,128)(2,1)S(1)} %collective-permute-done.2.refs_0_, bf16[128,768]{1,0:T(8,128)(2,1)S(1)} %collective-permute-done.9.refs_1_, bf16[128,768]{1,0:T(8,128)(2,1)S(1)} %collective-permute-done.24.refs_2_, ...), custom_call_target="tpu_custom_call", output_to_operand_aliasing={{}: (10, {})} | custom-call | flops 1409286144 | bytes 3538944 | tf_op jit(solution)/shard_map/pallas_call | solution.py:175
  60.7 0.1 collective-permute-start.18
  60.8 0.5 collective-permute-start.19
  61.3 4.1 %shard_map.95.refs_10_ = f32[2,768,128]{2,1,0:T(8,128)S(1)} custom-call(bf16[128,768]{1,0:T(8,128)(2,1)S(1)} %collective-permute-done.3.refs_0_, bf16[128,768]{1,0:T(8,128)(2,1)S(1)} %collective-permute-done.10.refs_1_, bf16[128,768]{1,0:T(8,128)(2,1)S(1)} %collective-permute-done.22.refs_2_, ...), custom_call_target="tpu_custom_call", output_to_operand_aliasing={{}: (10, {})} | custom-call | flops 1409286144 | bytes 3538944 | tf_op jit(solution)/shard_map/pallas_call | solution.py:175
  65.4 0.1 collective-permute-start.14
  65.5 0.4 collective-permute-start.15
  65.9 4.1 %shard_map.96.refs_10_ = f32[2,768,128]{2,1,0:T(8,128)S(1)} custom-call(bf16[128,768]{1,0:T(8,128)(2,1)S(1)} %collective-permute-done.4.refs_0_, bf16[128,768]{1,0:T(8,128)(2,1)S(1)} %collective-permute-done.11.refs_1_, bf16[128,768]{1,0:T(8,128)(2,1)S(1)} %collective-permute-done.20.refs_2_, ...), custom_call_target="tpu_custom_call", output_to_operand_aliasing={{}: (10, {})} | custom-call | flops 1409286144 | bytes 3538944 | tf_op jit(solution)/shard_map/pallas_call | solution.py:175
  70.0 0.0 copy-start.3
  70.0 4.1 %shard_map.97.refs_10_ = f32[2,768,128]{2,1,0:T(8,128)S(1)} custom-call(bf16[128,768]{1,0:T(8,128)(2,1)S(1)} %collective-permute-done.5.refs_0_, bf16[128,768]{1,0:T(8,128)(2,1)S(1)} %collective-permute-done.12.refs_1_, bf16[128,768]{1,0:T(8,128)(2,1)S(1)} %collective-permute-done.18.refs_2_, ...), custom_call_target="tpu_custom_call", output_to_operand_aliasing={{}: (10, {})} | custom-call | flops 1409286144 | bytes 3538944 | tf_op jit(solution)/shard_map/pallas_call | solution.py:175
  74.1 5.3 %shard_map.98 = bf16[2,128,768]{2,1,0:T(8,128)(2,1)} custom-call(bf16[128,768]{1,0:T(8,128)(2,1)S(1)} %collective-permute-done.6.refs_0_, bf16[128,768]{1,0:T(8,128)(2,1)S(1)} %collective-permute-done.13.refs_1_, bf16[128,768]{1,0:T(8,128)(2,1)S(1)} %collective-permute-done.14.refs_2_, bf16[128,768]{1,0:T(8,128)(2,1)S(1)} %collective-permute-done.15.refs_3_, ...), custom_call_target="tpu_custom_call" | custom-call | flops 1409286144 | bytes 3538944 | tf_op jit(solution)/shard_map/pallas_call | solution.py:175
  (27 shorter events, 0.1 us)
Async XLA Ops:
  1.1 6.7 %collective-permute-start = (bf16[128,768]{1,0:T(8,128)(2,1)S(1)}, bf16[128,768]{1,0:T(8,128)(2,1)S(1)}, u32[]{:S(2)}, u32[]{:S(2)}) collective-permute-start(bf16[128,768]{1,0:T(8,128)(2,1)S(1)} %get-tuple-element.12.refs_0_), channel_id=1, source_target_pairs={{0,4},{1,3},{4,8},{5,1},{8,12},{9,5},{12,14},{13,9},{14,10},{15,13... | collective-permute-start | bytes 589832 | tf_op jit(solution)/shard_map/ppermute | solution.py:213
  4.1 5.7 %collective-permute-start.7 = (bf16[128,768]{1,0:T(8,128)(2,1)S(1)}, bf16[128,768]{1,0:T(8,128)(2,1)S(1)}, u32[]{:S(2)}, u32[]{:S(2)}) collective-permute-start(bf16[128,768]{1,0:T(8,128)(2,1)S(1)} %get-tuple-element.11.refs_1_), channel_id=1, source_target_pairs={{0,4},{1,3},{4,8},{5,1},{8,12},{9,5},{12,14},{13,9},{14,10},{15,13... | collective-permute-start | bytes 589832 | tf_op jit(solution)/shard_map/ppermute | solution.py:213
  7.7 5.7 %collective-permute-start.1 = (bf16[128,768]{1,0:T(8,128)(2,1)S(1)}, bf16[128,768]{1,0:T(8,128)(2,1)S(1)}, u32[]{:S(2)}, u32[]{:S(2)}) collective-permute-start(bf16[128,768]{1,0:T(8,128)(2,1)S(1)} %collective-permute-done.refs_0_), channel_id=1, source_target_pairs={{0,4},{1,3},{4,8},{5,1},{8,12},{9,5},{12,14},{13,9},{14,10},{15,13... | collective-permute-start | bytes 589832 | tf_op jit(solution)/shard_map/ppermute | solution.py:213
  9.8 5.7 %collective-permute-start.8 = (bf16[128,768]{1,0:T(8,128)(2,1)S(1)}, bf16[128,768]{1,0:T(8,128)(2,1)S(1)}, u32[]{:S(2)}, u32[]{:S(2)}) collective-permute-start(bf16[128,768]{1,0:T(8,128)(2,1)S(1)} %collective-permute-done.7.refs_1_), channel_id=1, source_target_pairs={{0,4},{1,3},{4,8},{5,1},{8,12},{9,5},{12,14},{13,9},{14,10},{15,13... | collective-permute-start | bytes 589832 | tf_op jit(solution)/shard_map/ppermute | solution.py:213
  13.4 5.7 %collective-permute-start.2 = (bf16[128,768]{1,0:T(8,128)(2,1)S(1)}, bf16[128,768]{1,0:T(8,128)(2,1)S(1)}, u32[]{:S(2)}, u32[]{:S(2)}) collective-permute-start(bf16[128,768]{1,0:T(8,128)(2,1)S(1)} %collective-permute-done.1.refs_0_), channel_id=1, source_target_pairs={{0,4},{1,3},{4,8},{5,1},{8,12},{9,5},{12,14},{13,9},{14,10},{15,13... | collective-permute-start | bytes 589832 | tf_op jit(solution)/shard_map/ppermute | solution.py:213
  15.5 5.7 %collective-permute-start.9 = (bf16[128,768]{1,0:T(8,128)(2,1)S(1)}, bf16[128,768]{1,0:T(8,128)(2,1)S(1)}, u32[]{:S(2)}, u32[]{:S(2)}) collective-permute-start(bf16[128,768]{1,0:T(8,128)(2,1)S(1)} %collective-permute-done.8.refs_1_), channel_id=1, source_target_pairs={{0,4},{1,3},{4,8},{5,1},{8,12},{9,5},{12,14},{13,9},{14,10},{15,13... | collective-permute-start | bytes 589832 | tf_op jit(solution)/shard_map/ppermute | solution.py:213
  17.6 5.7 %collective-permute-start.16 = (bf16[128,768]{1,0:T(8,128)(2,1)S(1)}, bf16[128,768]{1,0:T(8,128)(2,1)S(1)}, u32[]{:S(2)}, u32[]{:S(2)}) collective-permute-start(bf16[128,768]{1,0:T(8,128)(2,1)S(1)} %get-tuple-element.12.refs_0_), channel_id=1, source_target_pairs={{0,1},{1,0},{2,3},{3,2},{4,5},{5,4},{6,7},{7,6},{8,9},{9,8},{10,11... | collective-permute-start | bytes 589832 | tf_op jit(solution)/shard_map/ppermute | solution.py:202
  17.6 5.7 %collective-permute-start.17 = (bf16[128,768]{1,0:T(8,128)(2,1)S(1)}, bf16[128,768]{1,0:T(8,128)(2,1)S(1)}, u32[]{:S(2)}, u32[]{:S(2)}) collective-permute-start(bf16[128,768]{1,0:T(8,128)(2,1)S(1)} %get-tuple-element.11.refs_1_), channel_id=1, source_target_pairs={{0,1},{1,0},{2,3},{3,2},{4,5},{5,4},{6,7},{7,6},{8,9},{9,8},{10,11... | collective-permute-start | bytes 589832 | tf_op jit(solution)/shard_map/ppermute | solution.py:202
  18.1 5.7 %collective-permute-start.28 = (bf16[128,768]{1,0:T(8,128)(2,1)S(1)}, bf16[128,768]{1,0:T(8,128)(2,1)S(1)}, u32[]{:S(2)}, u32[]{:S(2)}) collective-permute-start(bf16[128,768]{1,0:T(8,128)(2,1)S(1)} %collective-permute-done.refs_0_), channel_id=1, source_target_pairs={{0,1},{1,0},{2,3},{3,2},{4,5},{5,4},{6,7},{7,6},{8,9},{9,8},{10,11... | collective-permute-start | bytes 589832 | tf_op jit(solution)/shard_map/ppermute | solution.py:214
  19.1 5.7 %collective-permute-start.3 = (bf16[128,768]{1,0:T(8,128)(2,1)S(1)}, bf16[128,768]{1,0:T(8,128)(2,1)S(1)}, u32[]{:S(2)}, u32[]{:S(2)}) collective-permute-start(bf16[128,768]{1,0:T(8,128)(2,1)S(1)} %collective-permute-done.2.refs_0_), channel_id=1, source_target_pairs={{0,4},{1,3},{4,8},{5,1},{8,12},{9,5},{12,14},{13,9},{14,10},{15,13... | collective-permute-start | bytes 589832 | tf_op jit(solution)/shard_map/ppermute | solution.py:213
  21.2 5.7 %collective-permute-start.10 = (bf16[128,768]{1,0:T(8,128)(2,1)S(1)}, bf16[128,768]{1,0:T(8,128)(2,1)S(1)}, u32[]{:S(2)}, u32[]{:S(2)}) collective-permute-start(bf16[128,768]{1,0:T(8,128)(2,1)S(1)} %collective-permute-done.9.refs_1_), channel_id=1, source_target_pairs={{0,4},{1,3},{4,8},{5,1},{8,12},{9,5},{12,14},{13,9},{14,10},{15,13... | collective-permute-start | bytes 589832 | tf_op jit(solution)/shard_map/ppermute | solution.py:213
  23.2 7.0 %collective-permute-start.29 = (bf16[128,768]{1,0:T(8,128)(2,1)S(1)}, bf16[128,768]{1,0:T(8,128)(2,1)S(1)}, u32[]{:S(2)}, u32[]{:S(2)}) collective-permute-start(bf16[128,768]{1,0:T(8,128)(2,1)S(1)} %collective-permute-done.7.refs_1_), channel_id=1, source_target_pairs={{0,1},{1,0},{2,3},{3,2},{4,5},{5,4},{6,7},{7,6},{8,9},{9,8},{10,11... | collective-permute-start | bytes 589832 | tf_op jit(solution)/shard_map/ppermute | solution.py:214
  23.3 7.0 %collective-permute-start.26 = (bf16[128,768]{1,0:T(8,128)(2,1)S(1)}, bf16[128,768]{1,0:T(8,128)(2,1)S(1)}, u32[]{:S(2)}, u32[]{:S(2)}) collective-permute-start(bf16[128,768]{1,0:T(8,128)(2,1)S(1)} %collective-permute-done.1.refs_0_), channel_id=1, source_target_pairs={{0,1},{1,0},{2,3},{3,2},{4,5},{5,4},{6,7},{7,6},{8,9},{9,8},{10,11... | collective-permute-start | bytes 589832 | tf_op jit(solution)/shard_map/ppermute | solution.py:214
  23.8 18.5 %collective-permute-start.27 = (bf16[128,768]{1,0:T(8,128)(2,1)S(1)}, bf16[128,768]{1,0:T(8,128)(2,1)S(1)}, u32[]{:S(2)}, u32[]{:S(2)}) collective-permute-start(bf16[128,768]{1,0:T(8,128)(2,1)S(1)} %collective-permute-done.8.refs_1_), channel_id=1, source_target_pairs={{0,1},{1,0},{2,3},{3,2},{4,5},{5,4},{6,7},{7,6},{8,9},{9,8},{10,11... | collective-permute-start | bytes 589832 | tf_op jit(solution)/shard_map/ppermute | solution.py:214
  24.7 17.7 %collective-permute-start.4 = (bf16[128,768]{1,0:T(8,128)(2,1)S(1)}, bf16[128,768]{1,0:T(8,128)(2,1)S(1)}, u32[]{:S(2)}, u32[]{:S(2)}) collective-permute-start(bf16[128,768]{1,0:T(8,128)(2,1)S(1)} %collective-permute-done.3.refs_0_), channel_id=1, source_target_pairs={{0,4},{1,3},{4,8},{5,1},{8,12},{9,5},{12,14},{13,9},{14,10},{15,13... | collective-permute-start | bytes 589832 | tf_op jit(solution)/shard_map/ppermute | solution.py:213
  26.8 17.1 %collective-permute-start.11 = (bf16[128,768]{1,0:T(8,128)(2,1)S(1)}, bf16[128,768]{1,0:T(8,128)(2,1)S(1)}, u32[]{:S(2)}, u32[]{:S(2)}) collective-permute-start(bf16[128,768]{1,0:T(8,128)(2,1)S(1)} %collective-permute-done.10.refs_1_), channel_id=1, source_target_pairs={{0,4},{1,3},{4,8},{5,1},{8,12},{9,5},{12,14},{13,9},{14,10},{15,13... | collective-permute-start | bytes 589832 | tf_op jit(solution)/shard_map/ppermute | solution.py:213
  30.3 19.3 %collective-permute-start.24 = (bf16[128,768]{1,0:T(8,128)(2,1)S(1)}, bf16[128,768]{1,0:T(8,128)(2,1)S(1)}, u32[]{:S(2)}, u32[]{:S(2)}) collective-permute-start(bf16[128,768]{1,0:T(8,128)(2,1)S(1)} %collective-permute-done.2.refs_0_), channel_id=1, source_target_pairs={{0,1},{1,0},{2,3},{3,2},{4,5},{5,4},{6,7},{7,6},{8,9},{9,8},{10,11... | collective-permute-start | bytes 589832 | tf_op jit(solution)/shard_map/ppermute | solution.py:214
  30.3 19.4 %collective-permute-start.25 = (bf16[128,768]{1,0:T(8,128)(2,1)S(1)}, bf16[128,768]{1,0:T(8,128)(2,1)S(1)}, u32[]{:S(2)}, u32[]{:S(2)}) collective-permute-start(bf16[128,768]{1,0:T(8,128)(2,1)S(1)} %collective-permute-done.9.refs_1_), channel_id=1, source_target_pairs={{0,1},{1,0},{2,3},{3,2},{4,5},{5,4},{6,7},{7,6},{8,9},{9,8},{10,11... | collective-permute-start | bytes 589832 | tf_op jit(solution)/shard_map/ppermute | solution.py:214
  30.8 1.3 %copy-start = (bf16[768,768]{1,0:T(8,128)(2,1)S(1)}, bf16[768,768]{1,0:T(8,128)(2,1)}, u32[]{:S(2)}) copy-start(bf16[768,768]{1,0:T(8,128)(2,1)} %refs_7_.15) | copy-start | bytes 3538948
  32.1 1.0 %copy-start.2 = (bf16[2,128,768]{2,1,0:T(8,128)(2,1)S(1)}, bf16[2,128,768]{2,1,0:T(8,128)(2,1)}, u32[]{:S(2)}) copy-start(bf16[2,128,768]{2,1,0:T(8,128)(2,1)} %refs_11_.3) | copy-start | bytes 1179652
  33.1 0.7 copy-start.4
  33.8 0.7 copy-start.6
  34.4 1.3 %copy-start.8 = (bf16[768,768]{1,0:T(8,128)(2,1)S(1)}, bf16[768,768]{1,0:T(8,128)(2,1)}, u32[]{:S(2)}) copy-start(bf16[768,768]{1,0:T(8,128)(2,1)} %refs_10_.1) | copy-start | bytes 3538948
  35.7 1.3 %copy-start.9 = (bf16[768,768]{1,0:T(8,128)(2,1)S(1)}, bf16[768,768]{1,0:T(8,128)(2,1)}, u32[]{:S(2)}) copy-start(bf16[768,768]{1,0:T(8,128)(2,1)} %refs_11_.2) | copy-start | bytes 3538948
  37.0 8.6 %copy-start.1 = (bf16[768,768]{1,0:T(8,128)(2,1)S(1)}, bf16[768,768]{1,0:T(8,128)(2,1)}, u32[]{:S(2)}) copy-start(bf16[768,768]{1,0:T(8,128)(2,1)} %refs_7_.15) | copy-start | bytes 3538948
  42.2 12.1 %collective-permute-start.22 = (bf16[128,768]{1,0:T(8,128)(2,1)S(1)}, bf16[128,768]{1,0:T(8,128)(2,1)S(1)}, u32[]{:S(2)}, u32[]{:S(2)}) collective-permute-start(bf16[128,768]{1,0:T(8,128)(2,1)S(1)} %collective-permute-done.3.refs_0_), channel_id=1, source_target_pairs={{0,1},{1,0},{2,3},{3,2},{4,5},{5,4},{6,7},{7,6},{8,9},{9,8},{10,11... | collective-permute-start | bytes 589832 | tf_op jit(solution)/shard_map/ppermute | solution.py:214
  42.4 12.1 %collective-permute-start.5 = (bf16[128,768]{1,0:T(8,128)(2,1)S(1)}, bf16[128,768]{1,0:T(8,128)(2,1)S(1)}, u32[]{:S(2)}, u32[]{:S(2)}) collective-permute-start(bf16[128,768]{1,0:T(8,128)(2,1)S(1)} %collective-permute-done.4.refs_0_), channel_id=1, source_target_pairs={{0,4},{1,3},{4,8},{5,1},{8,12},{9,5},{12,14},{13,9},{14,10},{15,13... | collective-permute-start | bytes 589832 | tf_op jit(solution)/shard_map/ppermute | solution.py:213
  44.0 12.0 %collective-permute-start.12 = (bf16[128,768]{1,0:T(8,128)(2,1)S(1)}, bf16[128,768]{1,0:T(8,128)(2,1)S(1)}, u32[]{:S(2)}, u32[]{:S(2)}) collective-permute-start(bf16[128,768]{1,0:T(8,128)(2,1)S(1)} %collective-permute-done.11.refs_1_), channel_id=1, source_target_pairs={{0,4},{1,3},{4,8},{5,1},{8,12},{9,5},{12,14},{13,9},{14,10},{15,13... | collective-permute-start | bytes 589832 | tf_op jit(solution)/shard_map/ppermute | solution.py:213
  49.6 6.8 %copy-start.5 = (s32[2,8]{1,0:T(2,128)S(1)}, s32[2,8]{1,0:T(2,128)}, u32[]{:S(2)}) copy-start(s32[2,8]{1,0:T(2,128)} %refs_4_.15) | copy-start | bytes 196
  49.6 6.8 %copy-start.7 = (s32[2]{0:T(128)S(1)}, s32[2]{0:T(128)}, u32[]{:S(2)}) copy-start(s32[2]{0:T(128)} %refs_5_.15) | copy-start | bytes 28
  49.6 11.0 %collective-permute-start.23 = (bf16[128,768]{1,0:T(8,128)(2,1)S(1)}, bf16[128,768]{1,0:T(8,128)(2,1)S(1)}, u32[]{:S(2)}, u32[]{:S(2)}) collective-permute-start(bf16[128,768]{1,0:T(8,128)(2,1)S(1)} %collective-permute-done.10.refs_1_), channel_id=1, source_target_pairs={{0,1},{1,0},{2,3},{3,2},{4,5},{5,4},{6,7},{7,6},{8,9},{9,8},{10,11... | collective-permute-start | bytes 589832 | tf_op jit(solution)/shard_map/ppermute | solution.py:214
  49.7 11.0 %collective-permute-start.20 = (bf16[128,768]{1,0:T(8,128)(2,1)S(1)}, bf16[128,768]{1,0:T(8,128)(2,1)S(1)}, u32[]{:S(2)}, u32[]{:S(2)}) collective-permute-start(bf16[128,768]{1,0:T(8,128)(2,1)S(1)} %collective-permute-done.4.refs_0_), channel_id=1, source_target_pairs={{0,1},{1,0},{2,3},{3,2},{4,5},{5,4},{6,7},{7,6},{8,9},{9,8},{10,11... | collective-permute-start | bytes 589832 | tf_op jit(solution)/shard_map/ppermute | solution.py:214
  54.3 11.6 %collective-permute-start.21 = (bf16[128,768]{1,0:T(8,128)(2,1)S(1)}, bf16[128,768]{1,0:T(8,128)(2,1)S(1)}, u32[]{:S(2)}, u32[]{:S(2)}) collective-permute-start(bf16[128,768]{1,0:T(8,128)(2,1)S(1)} %collective-permute-done.11.refs_1_), channel_id=1, source_target_pairs={{0,1},{1,0},{2,3},{3,2},{4,5},{5,4},{6,7},{7,6},{8,9},{9,8},{10,11... | collective-permute-start | bytes 589832 | tf_op jit(solution)/shard_map/ppermute | solution.py:214
  54.5 10.9 %collective-permute-start.6 = (bf16[128,768]{1,0:T(8,128)(2,1)S(1)}, bf16[128,768]{1,0:T(8,128)(2,1)S(1)}, u32[]{:S(2)}, u32[]{:S(2)}) collective-permute-start(bf16[128,768]{1,0:T(8,128)(2,1)S(1)} %collective-permute-done.5.refs_0_), channel_id=1, source_target_pairs={{0,4},{1,3},{4,8},{5,1},{8,12},{9,5},{12,14},{13,9},{14,10},{15,13... | collective-permute-start | bytes 589832 | tf_op jit(solution)/shard_map/ppermute | solution.py:213
  56.0 9.5 %collective-permute-start.13 = (bf16[128,768]{1,0:T(8,128)(2,1)S(1)}, bf16[128,768]{1,0:T(8,128)(2,1)S(1)}, u32[]{:S(2)}, u32[]{:S(2)}) collective-permute-start(bf16[128,768]{1,0:T(8,128)(2,1)S(1)} %collective-permute-done.12.refs_1_), channel_id=1, source_target_pairs={{0,4},{1,3},{4,8},{5,1},{8,12},{9,5},{12,14},{13,9},{14,10},{15,13... | collective-permute-start | bytes 589832 | tf_op jit(solution)/shard_map/ppermute | solution.py:213
  60.7 9.3 %collective-permute-start.18 = (bf16[128,768]{1,0:T(8,128)(2,1)S(1)}, bf16[128,768]{1,0:T(8,128)(2,1)S(1)}, u32[]{:S(2)}, u32[]{:S(2)}) collective-permute-start(bf16[128,768]{1,0:T(8,128)(2,1)S(1)} %collective-permute-done.5.refs_0_), channel_id=1, source_target_pairs={{0,1},{1,0},{2,3},{3,2},{4,5},{5,4},{6,7},{7,6},{8,9},{9,8},{10,11... | collective-permute-start | bytes 589832 | tf_op jit(solution)/shard_map/ppermute | solution.py:214
  60.8 9.2 %collective-permute-start.19 = (bf16[128,768]{1,0:T(8,128)(2,1)S(1)}, bf16[128,768]{1,0:T(8,128)(2,1)S(1)}, u32[]{:S(2)}, u32[]{:S(2)}) collective-permute-start(bf16[128,768]{1,0:T(8,128)(2,1)S(1)} %collective-permute-done.12.refs_1_), channel_id=1, source_target_pairs={{0,1},{1,0},{2,3},{3,2},{4,5},{5,4},{6,7},{7,6},{8,9},{9,8},{10,11... | collective-permute-start | bytes 589832 | tf_op jit(solution)/shard_map/ppermute | solution.py:214
  65.4 8.8 %collective-permute-start.14 = (bf16[128,768]{1,0:T(8,128)(2,1)S(1)}, bf16[128,768]{1,0:T(8,128)(2,1)S(1)}, u32[]{:S(2)}, u32[]{:S(2)}) collective-permute-start(bf16[128,768]{1,0:T(8,128)(2,1)S(1)} %collective-permute-done.6.refs_0_), channel_id=1, source_target_pairs={{0,1},{1,0},{2,3},{3,2},{4,5},{5,4},{6,7},{7,6},{8,9},{9,8},{10,11... | collective-permute-start | bytes 589832 | tf_op jit(solution)/shard_map/ppermute | solution.py:214
  65.5 8.6 %collective-permute-start.15 = (bf16[128,768]{1,0:T(8,128)(2,1)S(1)}, bf16[128,768]{1,0:T(8,128)(2,1)S(1)}, u32[]{:S(2)}, u32[]{:S(2)}) collective-permute-start(bf16[128,768]{1,0:T(8,128)(2,1)S(1)} %collective-permute-done.13.refs_1_), channel_id=1, source_target_pairs={{0,1},{1,0},{2,3},{3,2},{4,5},{5,4},{6,7},{7,6},{8,9},{9,8},{10,11... | collective-permute-start | bytes 589832 | tf_op jit(solution)/shard_map/ppermute | solution.py:214
  70.0 4.1 %copy-start.3 = (bf16[768,768]{1,0:T(8,128)(2,1)S(1)}, bf16[768,768]{1,0:T(8,128)(2,1)}, u32[]{:S(2)}) copy-start(bf16[768,768]{1,0:T(8,128)(2,1)} %refs_12_.1) | copy-start | bytes 3538948

commit v2 on v1

v2 whole, which is shorter than its diff:
```python
import functools

import jax
import jax.numpy as jnp
from jax import lax
from jax.experimental import pallas as pl
from jax.experimental.pallas import tpu as pltpu
from jax.sharding import PartitionSpec as P

HEADS = 12
HEAD_DIM = 64
CORES = 2
PAIRED = 2 * HEAD_DIM


class Ring:
    def __init__(self, devices, columns):
        self.chips = devices // CORES
        self.columns = columns
        self.rows = self.chips // columns

    def chip(self, place):
        if self.columns == 1:
            return place
        if place < self.rows:
            return place * 2
        return (2 * self.rows - 1 - place) * 2 + 1

    def onward(self, step):
        pairs = []
        for place in range(self.chips):
            target = self.chip((place + step) % self.chips)
            pairs += [(self.chip(place) * CORES + core, target * CORES + core) for core in range(CORES)]
        return pairs

    def sibling(self):
        return [(i, i ^ 1) for i in range(self.chips * CORES)]

    def owner(self, me, shift, flip):
        chip = me // CORES
        core = lax.rem(me, CORES)
        if flip:
            core = 1 - core
        if self.columns == 1:
            place = chip
        else:
            row = chip // 2
            place = jnp.where(lax.rem(chip, 2) == 0, row, 2 * self.rows - 1 - row)
        came = lax.rem(place + shift + self.chips, self.chips)
        if self.columns == 1:
            there = came
        else:
            there = jnp.where(came < self.rows, came * 2, (2 * self.rows - 1 - came) * 2 + 1)
        return there * CORES + core


def normalize(rows, gain):
    rows = rows.astype(jnp.float32)
    center = rows - jnp.mean(rows, axis=-1, keepdims=True)
    spread = jnp.mean(center * center, axis=-1, keepdims=True)
    return center * lax.rsqrt(spread + 1e-06) * gain


def dot(a, b, dims=((1,), (0,))):
    return lax.dot_general(a, b, (dims, ((), ())), preferred_element_type=jnp.float32)


def find_slot(owner, partners, counts, own, listed):
    image = jnp.int32(0)
    index = jnp.int32(0)
    live = jnp.int32(0)
    for a in range(own):
        for k in range(listed):
            partner = partners[a, k]
            hit = jnp.logical_and(k < counts[a], partner // own == owner)
            image = jnp.where(hit, a, image)
            index = jnp.where(hit, lax.rem(partner, own), index)
            live = jnp.where(hit, 1, live)
    return image, index, live


def attend(memory, slots, gain, w_kv, spread_q, total, tok):
    width = memory.shape[-1]
    normed = normalize(memory, gain).astype(jnp.bfloat16)
    both = dot(normed, w_kv[...]).astype(jnp.bfloat16)
    for at, (image, live) in enumerate(slots):
        here = slice(at * tok, (at + 1) * tok)
        for g in range(HEADS // 2):
            feats = slice(g * PAIRED, (g + 1) * PAIRED)
            scores = dot(both[here, feats], spread_q[image, feats, :])
            weights = jnp.exp(scores - jnp.max(scores, axis=0, keepdims=True))
            share = live.astype(jnp.float32) / jnp.sum(weights, axis=0, keepdims=True)
            weights = weights.astype(jnp.bfloat16)
            parts = []
            for h in range(2):
                values = both[here, width + g * PAIRED + h * HEAD_DIM : width + g * PAIRED + (h + 1) * HEAD_DIM]
                asked = slice(h * tok, (h + 1) * tok)
                parts.append(dot(values, weights[:, asked], ((0,), (0,))) * share[:, asked])
            total[image, feats, :] += jnp.concatenate(parts, axis=0)


def first_kernel(ring, slots, own, listed, tok, *refs):
    (tokens, partners, counts, gain_query, gain_memory, w_query, w_key, w_value, w_out) = refs[:9]
    total, spread_q, w_kv, w_out_here, tokens_here, gain_here, picks, table = refs[9:17]
    partners_here, counts_here, gain_query_here, w_query_here, sems = refs[17:]
    width = tokens.shape[-1]
    copies = [
        pltpu.make_async_copy(source, target, sems.at[i])
        for i, (source, target) in enumerate(
            (
                (partners, partners_here),
                (counts, counts_here),
                (tokens, tokens_here),
                (gain_query, gain_query_here),
                (w_query, w_query_here),
                (gain_memory, gain_here),
                (w_key, w_kv.at[:, pl.ds(0, width)]),
                (w_value, w_kv.at[:, pl.ds(width, width)]),
                (w_out, w_out_here),
            )
        )
    ]
    for copy in copies:
        copy.start()
    total[...] = jnp.zeros_like(total)
    for copy in copies[:2]:
        copy.wait()
    for owner in range(ring.chips * CORES):
        image, index, live = find_slot(owner, partners_here, counts_here, own, listed)
        table[0, owner] = image
        table[1, owner] = live
        picks[owner] = jnp.full(picks.shape[1:], index.astype(jnp.float32))
    for copy in copies[2:5]:
        copy.wait()
    rows = tokens_here[...].reshape(own * tok, -1)
    normed_query = normalize(rows, gain_query_here[...][None, :]).astype(jnp.bfloat16)
    queries = dot(normed_query, w_query_here[...]).astype(jnp.bfloat16).astype(jnp.float32)
    queries_t = (queries * (1.0 / HEAD_DIM**0.5)).T.astype(jnp.bfloat16)
    zero = jnp.zeros((HEAD_DIM, tok), jnp.bfloat16)
    for a in range(own):
        for h in range(HEADS):
            part = queries_t[h * HEAD_DIM : (h + 1) * HEAD_DIM, a * tok : (a + 1) * tok]
            pieces = [part, zero] if h % 2 == 0 else [zero, part]
            spread_q[a, h * HEAD_DIM : (h + 1) * HEAD_DIM, :] = jnp.concatenate(pieces, axis=1)
    for copy in copies[5:8]:
        copy.wait()
    me = lax.axis_index("img")
    chosen, asked = [], []
    for shift, flip, _ in slots:
        owner = ring.owner(me, shift, flip)
        chosen.append(choose([tokens_here[j] for j in range(own)], picks[owner][:1, :]))
        asked.append((table[0, owner], table[1, owner]))
    attend(jnp.concatenate(chosen, axis=0), asked, gain_here[...][None, :], w_kv, spread_q, total, tok)
    copies[8].wait()


def choose(images, pick):
    chosen = images[0].astype(jnp.float32)
    for j in range(1, len(images)):
        chosen = jnp.where(pick == j, images[j].astype(jnp.float32), chosen)
    return chosen


def later_kernel(ring, slots, last, own, tok, *refs):
    refs = list(refs)
    take = lambda n: [refs.pop(0) for _ in range(n)]
    sources = [take(n) for _, _, n in slots]
    spread_q, w_kv, gain, picks, table, _ = take(6)
    if last:
        w_out, tokens, counts, total, mixed, counts_here, table_here, sems = refs
    else:
        total, table_here, sems = refs
    copies = [pltpu.make_async_copy(table, table_here, sems.at[0])]
    if last:
        copies.append(pltpu.make_async_copy(counts, counts_here, sems.at[1]))
    for copy in copies:
        copy.start()
    me = lax.axis_index("img")
    owners = [ring.owner(me, shift, flip) for shift, flip, _ in slots]
    chosen = []
    for arrays, owner in zip(sources, owners):
        images = [arrays[0][j] for j in range(own)] if len(arrays) == 1 else [array[...] for array in arrays]
        chosen.append(choose(images, picks[owner][:1, :]))
    for copy in copies:
        copy.wait()
    asked = [(table_here[0, owner], table_here[1, owner]) for owner in owners]
    attend(jnp.concatenate(chosen, axis=0), asked, gain[...][None, :], w_kv, spread_q, total, tok)
    if last:
        for a in range(own):
            context = (total[a] / counts_here[a].astype(jnp.float32)).T.astype(jnp.bfloat16)
            out = tokens[a].astype(jnp.float32) + dot(context, w_out[...])
            mixed[a] = out.astype(jnp.bfloat16)


HBM = pl.BlockSpec(memory_space=pltpu.HBM)
ANY = pl.BlockSpec(memory_space=pl.ANY)
SMEM = pl.BlockSpec(memory_space=pltpu.SMEM)
VMEM = pl.BlockSpec(memory_space=pltpu.VMEM)


def cost(rows, tok, width):
    return pl.CostEstimate(
        flops=4 * rows * width * (width + tok) * 2,
        bytes_accessed=2 * width * width * 2 + 3 * rows * width * 2,
        transcendentals=rows * tok * HEADS,
    )


def first_stage(ring, slots, operands, own, listed, tok, width):
    devices = ring.chips * CORES
    shapes = [
        jax.ShapeDtypeStruct((own, width, tok), jnp.float32),
        jax.ShapeDtypeStruct((own, width, 2 * tok), jnp.bfloat16),
        jax.ShapeDtypeStruct((width, 2 * width), jnp.bfloat16),
        jax.ShapeDtypeStruct((width, width), jnp.bfloat16),
        jax.ShapeDtypeStruct((own, tok, width), jnp.bfloat16),
        jax.ShapeDtypeStruct((width,), jnp.float32),
        jax.ShapeDtypeStruct((devices, 8, width), jnp.float32),
        jax.ShapeDtypeStruct((2, devices), jnp.int32),
    ]
    return pl.pallas_call(
        functools.partial(first_kernel, ring, slots, own, listed, tok),
        out_shape=shapes,
        in_specs=[HBM] * len(operands),
        out_specs=[VMEM] * 7 + [SMEM],
        scratch_shapes=[
            pltpu.SMEM((own, listed), jnp.int32),
            pltpu.SMEM((own,), jnp.int32),
            pltpu.VMEM((width,), jnp.float32),
            pltpu.VMEM((width, width), jnp.bfloat16),
            pltpu.SemaphoreType.DMA((9,)),
        ],
        compiler_params=pltpu.CompilerParams(vmem_limit_bytes=32 << 20),
        cost_estimate=cost(own * tok, tok, width),
    )(*operands)


def later_stage(ring, work, state, extra, total, own, tok, width):
    slots, sources = zip(*work)
    last = len(extra) > 0
    images = [array for arrays in sources for array in arrays]
    shapes = [jax.ShapeDtypeStruct(total.shape, total.dtype)]
    scratch = [pltpu.SMEM((2, ring.chips * CORES), jnp.int32), pltpu.SemaphoreType.DMA((2,))]
    if last:
        shapes.append(jax.ShapeDtypeStruct((own, tok, width), jnp.bfloat16))
        scratch = [pltpu.SMEM((own,), jnp.int32)] + scratch
    return pl.pallas_call(
        functools.partial(later_kernel, ring, slots, last, own, tok),
        out_shape=shapes,
        in_specs=[VMEM] * (len(images) + 4) + [ANY, VMEM] + ([VMEM, VMEM, ANY] if last else []),
        out_specs=[VMEM] * len(shapes),
        scratch_shapes=scratch,
        input_output_aliases={len(images) + 5: 0},
        compiler_params=pltpu.CompilerParams(vmem_limit_bytes=32 << 20),
        cost_estimate=cost(len(slots) * tok, tok, width),
    )(*images, *state, total, *extra)


def shards(columns, tokens, partners, counts, gain_query, gain_memory, w_query, w_key, w_value, w_out):
    own, tok, width = tokens.shape
    listed = partners.shape[1]
    ring = Ring(lax.axis_size("img"), columns)
    ahead, back, sibling = ring.onward(1), ring.onward(-1), ring.sibling()
    sizes = dict(own=own, tok=tok, width=width)
    send = lambda array, to: lax.ppermute(array, "img", to)

    far = ring.chips // 2
    assert ring.chips == 2 * far and own == 2
    up, down = send(tokens, ahead), send(tokens, back)
    behind = [((0, True, 1), [send(tokens, sibling)])]
    operands = (tokens, partners, counts, gain_query, gain_memory, w_query, w_key, w_value, w_out)
    operands = [pltpu.with_memory_space_constraint(array, pltpu.HBM) for array in operands]
    total, spread_q, w_kv, w_out_here, tokens_here, gain_here, picks, table = first_stage(
        ring, ((0, False, 1),), operands, listed=listed, **sizes
    )
    state = (spread_q, w_kv, gain_here, picks, table)
    for step in range(1, far):
        waited = [array for _, arrays in behind for array in arrays]
        up, down, total, waited = lax.optimization_barrier((up, down, total, waited))
        behind = [(slot, [array]) for (slot, _), array in zip(behind, waited)]
        work = behind + [((-step, False, 1), [up]), ((step, False, 1), [down])]
        behind = [((-step, True, 1), [send(up, sibling)]), ((step, True, 1), [send(down, sibling)])]
        if step + 1 < far:
            up, down = send(up, ahead), send(down, back)
        else:
            up, down = send(up[0], ahead), send(down[1], back)
        (total,) = later_stage(ring, work, state, (), total, **sizes)
    (total,) = later_stage(ring, behind + [((far, False, own), [up, down])], state, (), total, **sizes)
    work = [((far, True, own), [send(up, sibling), send(down, sibling)])]
    _, mixed = later_stage(ring, work, state, (w_out_here, tokens_here, counts), total, **sizes)
    return mixed


def solution(mesh):
    placed = (
        P(("groups", "img"), None, None),
        P(("groups", "img"), None),
        P(("groups", "img")),
        P(),
        P(),
        P(),
        P(),
        P(),
        P(),
    )
    columns = max(1, 4 // mesh.shape["groups"])
    return jax.shard_map(
        functools.partial(shards, columns),
        mesh=mesh,
        in_specs=placed,
        out_specs=P(("groups", "img"), None, None),
        check_vma=False,
    )
```

time: 79.9 us -> 53.1 us (0.66)
  starting transfers between devices: 30 us -> 10.1 us
  waiting for transfers between devices: 5.54 us -> 22.5 us
  Pallas kernels: 35.1 us -> 20 us
  local copies, waits for them, and re-layouts: 8.59 us -> 0.03 us
    ppermute x30 -> x17, starting transfers between devices: 30 us -> 10.1 us  [shards(): send = lambda array, to: lax.ppermute(array, 'img', to)]
    ppermute x30 -> x17, waiting for transfers between devices: 5.54 us -> 22.5 us  [shards(): send = lambda array, to: lax.ppermute(array, 'img', to)]
    pallas_call x8 -> x6, Pallas kernels: 35.1 us -> 20 us  [the longest x5 15.4 us: later_stage(): pl.pallas_call(functools.partial(later_kernel, ring, slots, last, own, to...]
    unnamed x20 -> x2, local copies, waits for them, and re-layouts: 6.16 us -> 0.01 us
    reshape x2 -> x0, local copies, waits for them, and re-layouts: 1.38 us -> none  [the longest x1 0.69 us: shards(): gain_memory = gain_memory.reshape(1, width)]
    squeeze x1 -> x2, local copies, waits for them, and re-layouts: 1.05 us -> 0.03 us  [shards(): up, down = (send(up[0], ahead), send(down[1], back))]
  transfers between devices with their start and end apart: 30 -> 17, of which waited for: 4 -> 8; matrix products, arithmetic and copies ran while one was open for 2% -> 0% of each run, Pallas kernels for 37% -> 32%
where the time goes in v2:
time: 53.1 us; the launch traced here: 52.9 us
  waiting for transfers between devices  22.5 us (42%)
  Pallas kernels  20 us (38%)
  starting transfers between devices  10.1 us (19%)
    ppermute x17, waiting for transfers between devices, shards(): send = lambda array, to: lax.ppermute(array, 'img', to)  22.5 us
    pallas_call x5, Pallas kernels, later_stage(): pl.pallas_call(functools.partial(later_kernel, ring, slots, last, own, to...  15.4 us
    ppermute x17, starting transfers between devices, shards(): send = lambda array, to: lax.ppermute(array, 'img', to)  10.1 us
    pallas_call x1, Pallas kernels, first_stage(): pl.pallas_call(functools.partial(first_kernel, ring, slots, own, listed,...  4.63 us
  transfers between devices with their start and end apart: 17, of which 8 were waited for; matrix products, arithmetic and copies ran while one was open for 0% of the time, Pallas kernels for 32%

profile of v2, /device:TPU:0, one launch (start us, length us, event | category | flops | bytes accessed | tf_op | source)
XLA Modules:
  0.0 52.9 jit_solution(7098881947246348220)
XLA Ops:
  0.0 3.0 %collective-permute-start.1 = (bf16[2,128,768]{2,1,0:T(8,128)(2,1)}, bf16[2,128,768]{2,1,0:T(8,128)(2,1)S(1)}, u32[]{:S(2)}, u32[]{:S(2)}) collective-permute-start(bf16[2,128,768]{2,1,0:T(8,128)(2,1)} %refs_0_.1), channel_id=1, source_target_pairs={{0,2},{1,3},{4,0},{5,1},{8,4},{9,5},{12,8},{13,9},{14,12},{15,13},... | collective-permute-start | bytes 1179656 | tf_op jit(solution)/shard_map/ppermute | solution.py:265
  3.0 0.1 collective-permute-start
  3.0 0.0 collective-permute-start.2
  3.0 4.6 %shard_map.91 = (f32[2,768,128]{2,1,0:T(8,128)S(1)}, bf16[2,768,256]{2,1,0:T(8,128)(2,1)S(1)}, bf16[768,1536]{1,0:T(8,128)(2,1)S(1)}, bf16[768,768]{1,0:T(8,128)...) custom-call(bf16[2,128,768]{2,1,0:T(8,128)(2,1)} %refs_0_.1, ...), custom_call_target="tpu_custom_call" | custom-call | flops 1409286144 | bytes 3538944 | tf_op jit(solution)/shard_map/pallas_call | solution.py:221
  7.7 4.7 %collective-permute-done.1.refs_2_ = bf16[2,128,768]{2,1,0:T(8,128)(2,1)S(1)} collective-permute-done((bf16[2,128,768]{2,1,0:T(8,128)(2,1)}, bf16[2,128,768]{2,1,0:T(8,128)(2,1)S(1)}, u32[]{:S(2)}, u32[]{:S(2)}) %collective-permute-start.1) | collective-permute-done | bytes 393248 | tf_op jit(solution)/shard_map/ppermute | solution.py:265
  12.3 1.4 %collective-permute-done.refs_1_ = bf16[2,128,768]{2,1,0:T(8,128)(2,1)S(1)} collective-permute-done((bf16[2,128,768]{2,1,0:T(8,128)(2,1)}, bf16[2,128,768]{2,1,0:T(8,128)(2,1)S(1)}, u32[]{:S(2)}, u32[]{:S(2)}) %collective-permute-start) | collective-permute-done | bytes 393248 | tf_op jit(solution)/shard_map/ppermute | solution.py:265
  13.8 0.0 collective-permute-done.2.refs_0_
  13.8 0.0 collective-permute-start.5
  13.8 0.4 collective-permute-start.3
  14.2 0.2 collective-permute-start.6
  14.3 1.7 %collective-permute-start.4 = (bf16[2,128,768]{2,1,0:T(8,128)(2,1)S(1)}, bf16[2,128,768]{2,1,0:T(8,128)(2,1)S(1)}, u32[]{:S(2)}, u32[]{:S(2)}) collective-permute-start(bf16[2,128,768]{2,1,0:T(8,128)(2,1)S(1)} %collective-permute-done.1.refs_2_), channel_id=1, source_target_pairs={{0,2},{1,3},{4,0},{5,1},{8,4},{9,5},{12,8},{13,9},{14,12},{15,13},... | collective-permute-start | bytes 1179656 | tf_op jit(solution)/shard_map/ppermute | solution.py:265
  16.0 2.8 %shard_map.92.refs_9_ = f32[2,768,128]{2,1,0:T(8,128)S(1)} custom-call(bf16[2,128,768]{2,1,0:T(8,128)(2,1)S(1)} %collective-permute-done.2.refs_0_, bf16[2,128,768]{2,1,0:T(8,128)(2,1)S(1)} %collective-permute-done.refs_1_, bf16[2,128,768]{2,1,0:T(8,128)(2,1)S(1)} %collective-permute-done.1.refs_2_, ...), custom_call_target="tpu_custom_call", output_to_operand_aliasing={{}: (8, {})} | custom-call | flops 2113929216 | bytes 4128768 | tf_op jit(solution)/shard_map/pallas_call | solution.py:247
  18.8 0.0 collective-permute-done.5.refs_0_
  18.8 6.5 %collective-permute-done.3.refs_2_ = bf16[2,128,768]{2,1,0:T(8,128)(2,1)S(1)} collective-permute-done((bf16[2,128,768]{2,1,0:T(8,128)(2,1)S(1)}, bf16[2,128,768]{2,1,0:T(8,128)(2,1)S(1)}, u32[]{:S(2)}, u32[]{:S(2)}) %collective-permute-start.3) | collective-permute-done | bytes 393248 | tf_op jit(solution)/shard_map/ppermute | solution.py:265
  25.3 0.0 collective-permute-done.6.refs_1_
  25.3 0.4 collective-permute-done.4.refs_3_
  25.7 0.0 collective-permute-start.9
  25.7 1.7 %collective-permute-start.7 = (bf16[2,128,768]{2,1,0:T(8,128)(2,1)S(1)}, bf16[2,128,768]{2,1,0:T(8,128)(2,1)S(1)}, u32[]{:S(2)}, u32[]{:S(2)}) collective-permute-start(bf16[2,128,768]{2,1,0:T(8,128)(2,1)S(1)} %collective-permute-done.3.refs_2_), channel_id=1, source_target_pairs={{0,4},{1,5},{4,8},{5,9},{8,12},{9,13},{12,14},{13,15},{14,10},{15,... | collective-permute-start | bytes 1179656 | tf_op jit(solution)/shard_map/ppermute | solution.py:265
  27.4 0.2 collective-permute-start.10
  27.6 0.3 collective-permute-start.8
  27.9 3.4 %shard_map.93.refs_9_ = f32[2,768,128]{2,1,0:T(8,128)S(1)} custom-call(bf16[2,128,768]{2,1,0:T(8,128)(2,1)S(1)} %collective-permute-done.5.refs_0_, bf16[2,128,768]{2,1,0:T(8,128)(2,1)S(1)} %collective-permute-done.6.refs_1_, bf16[2,128,768]{2,1,0:T(8,128)(2,1)S(1)} %collective-permute-done.3.refs_2_, ...), custom_call_target="tpu_custom_call", output_to_operand_aliasing={{}: (9, {})} | custom-call | flops 2818572288 | bytes 4718592 | tf_op jit(solution)/shard_map/pallas_call | solution.py:247
  31.4 0.0 collective-permute-done.9.refs_0_
  31.4 5.8 %collective-permute-done.7.refs_2_ = bf16[2,128,768]{2,1,0:T(8,128)(2,1)S(1)} collective-permute-done((bf16[2,128,768]{2,1,0:T(8,128)(2,1)S(1)}, bf16[2,128,768]{2,1,0:T(8,128)(2,1)S(1)}, u32[]{:S(2)}, u32[]{:S(2)}) %collective-permute-start.7) | collective-permute-done | bytes 393248 | tf_op jit(solution)/shard_map/ppermute | solution.py:265
  37.2 0.0 collective-permute-done.10.refs_1_
  37.2 1.7 %collective-permute-done.8.refs_3_ = bf16[2,128,768]{2,1,0:T(8,128)(2,1)S(1)} collective-permute-done((bf16[2,128,768]{2,1,0:T(8,128)(2,1)S(1)}, bf16[2,128,768]{2,1,0:T(8,128)(2,1)S(1)}, u32[]{:S(2)}, u32[]{:S(2)}) %collective-permute-start.8) | collective-permute-done | bytes 393248 | tf_op jit(solution)/shard_map/ppermute | solution.py:265
  38.9 0.1 collective-permute-start.16
  39.0 0.4 collective-permute-start.13
  39.4 0.2 collective-permute-start.15
  39.6 1.9 %collective-permute-start.11 = (bf16[128,768]{1,0:T(8,128)(2,1)S(1)}, bf16[128,768]{1,0:T(8,128)(2,1)S(1)}, u32[]{:S(2)}, u32[]{:S(2)}) collective-permute-start(bf16[128,768]{1,0:T(8,128)(2,1)S(1)} %slice_bitcast_fusion.1), channel_id=1, source_target_pairs={{0,4},{1,5},{4,8},{5,9},{8,12},{9,13},{12,14},{13,15},{14,10},{15,... | collective-permute-start | bytes 589832 | tf_op jit(solution)/shard_map/ppermute | solution.py:265
  41.5 3.4 %shard_map.94.refs_9_ = f32[2,768,128]{2,1,0:T(8,128)S(1)} custom-call(bf16[2,128,768]{2,1,0:T(8,128)(2,1)S(1)} %collective-permute-done.9.refs_0_, bf16[2,128,768]{2,1,0:T(8,128)(2,1)S(1)} %collective-permute-done.10.refs_1_, bf16[2,128,768]{2,1,0:T(8,128)(2,1)S(1)} %collective-permute-done.7.refs_2_, ...), custom_call_target="tpu_custom_call", output_to_operand_aliasing={{}: (9, {})} | custom-call | flops 2818572288 | bytes 4718592 | tf_op jit(solution)/shard_map/pallas_call | solution.py:247
  44.9 0.0 copy-start
  44.9 1.4 %collective-permute-done.13.refs_3_ = bf16[128,768]{1,0:T(8,128)(2,1)S(1)} collective-permute-done((bf16[128,768]{1,0:T(8,128)(2,1)S(1)}, bf16[128,768]{1,0:T(8,128)(2,1)S(1)}, u32[]{:S(2)}, u32[]{:S(2)}) %collective-permute-start.13) | collective-permute-done | bytes 196640 | tf_op jit(solution)/shard_map/ppermute | solution.py:265
  46.3 0.0 collective-permute-start.14
  46.3 0.7 %collective-permute-done.11.refs_2_ = bf16[128,768]{1,0:T(8,128)(2,1)S(1)} collective-permute-done((bf16[128,768]{1,0:T(8,128)(2,1)S(1)}, bf16[128,768]{1,0:T(8,128)(2,1)S(1)}, u32[]{:S(2)}, u32[]{:S(2)}) %collective-permute-start.11) | collective-permute-done | bytes 196640 | tf_op jit(solution)/shard_map/ppermute | solution.py:265
  47.0 0.0 collective-permute-start.12
  47.0 0.0 collective-permute-done.15.refs_0_
  47.0 0.0 collective-permute-done.16.refs_1_
  47.0 2.8 %shard_map.95.refs_7_ = f32[2,768,128]{2,1,0:T(8,128)S(1)} custom-call(bf16[2,128,768]{2,1,0:T(8,128)(2,1)S(1)} %collective-permute-done.15.refs_0_, bf16[2,128,768]{2,1,0:T(8,128)(2,1)S(1)} %collective-permute-done.16.refs_1_, bf16[128,768]{1,0:T(8,128)(2,1)S(1)} %collective-permute-done.11.refs_2_, ...), custom_call_target="tpu_custom_call", output_to_operand_aliasing={{}: (9, {})} | custom-call | flops 2113929216 | bytes 4128768 | tf_op jit(solution)/shard_map/pallas_call | solution.py:247
  49.8 0.0 collective-permute-done.14.refs_1_
  49.8 0.0 collective-permute-done.12.refs_0_
  49.8 0.0 copy-done
  49.8 2.9 %shard_map.96 = (f32[2,768,128]{2,1,0:T(8,128)S(1)}, bf16[2,128,768]{2,1,0:T(8,128)(2,1)}) custom-call(bf16[128,768]{1,0:T(8,128)(2,1)S(1)} %collective-permute-done.12.refs_0_, bf16[128,768]{1,0:T(8,128)(2,1)S(1)} %collective-permute-done.14.refs_1_, ...), custom_call_target="tpu_custom_call", output_to_operand_aliasing={{0}: (7, {})} | custom-call | flops 704643072 | bytes 2949120 | tf_op jit(solution)/shard_map/pallas_call | solution.py:247
  (2 shorter events, 0.0 us)
Async XLA Ops:
  0.0 12.3 %collective-permute-start.1 = (bf16[2,128,768]{2,1,0:T(8,128)(2,1)}, bf16[2,128,768]{2,1,0:T(8,128)(2,1)S(1)}, u32[]{:S(2)}, u32[]{:S(2)}) collective-permute-start(bf16[2,128,768]{2,1,0:T(8,128)(2,1)} %refs_0_.1), channel_id=1, source_target_pairs={{0,2},{1,3},{4,0},{5,1},{8,4},{9,5},{12,8},{13,9},{14,12},{15,13},... | collective-permute-start | bytes 1179656 | tf_op jit(solution)/shard_map/ppermute | solution.py:265
  3.0 10.8 %collective-permute-start = (bf16[2,128,768]{2,1,0:T(8,128)(2,1)}, bf16[2,128,768]{2,1,0:T(8,128)(2,1)S(1)}, u32[]{:S(2)}, u32[]{:S(2)}) collective-permute-start(bf16[2,128,768]{2,1,0:T(8,128)(2,1)} %refs_0_.1), channel_id=1, source_target_pairs={{0,4},{1,5},{4,8},{5,9},{8,12},{9,13},{12,14},{13,15},{14,10},{15,... | collective-permute-start | bytes 1179656 | tf_op jit(solution)/shard_map/ppermute | solution.py:265
  3.0 10.7 %collective-permute-start.2 = (bf16[2,128,768]{2,1,0:T(8,128)(2,1)}, bf16[2,128,768]{2,1,0:T(8,128)(2,1)S(1)}, u32[]{:S(2)}, u32[]{:S(2)}) collective-permute-start(bf16[2,128,768]{2,1,0:T(8,128)(2,1)} %refs_0_.1), channel_id=1, source_target_pairs={{0,1},{1,0},{2,3},{3,2},{4,5},{5,4},{6,7},{7,6},{8,9},{9,8},{10,11... | collective-permute-start | bytes 1179656 | tf_op jit(solution)/shard_map/ppermute | solution.py:265
  13.8 5.1 %collective-permute-start.5 = (bf16[2,128,768]{2,1,0:T(8,128)(2,1)S(1)}, bf16[2,128,768]{2,1,0:T(8,128)(2,1)S(1)}, u32[]{:S(2)}, u32[]{:S(2)}) collective-permute-start(bf16[2,128,768]{2,1,0:T(8,128)(2,1)S(1)} %collective-permute-done.refs_1_), channel_id=1, source_target_pairs={{0,1},{1,0},{2,3},{3,2},{4,5},{5,4},{6,7},{7,6},{8,9},{9,8},{10,11... | collective-permute-start | bytes 1179656 | tf_op jit(solution)/shard_map/ppermute | solution.py:265
  13.8 11.5 %collective-permute-start.3 = (bf16[2,128,768]{2,1,0:T(8,128)(2,1)S(1)}, bf16[2,128,768]{2,1,0:T(8,128)(2,1)S(1)}, u32[]{:S(2)}, u32[]{:S(2)}) collective-permute-start(bf16[2,128,768]{2,1,0:T(8,128)(2,1)S(1)} %collective-permute-done.refs_1_), channel_id=1, source_target_pairs={{0,4},{1,5},{4,8},{5,9},{8,12},{9,13},{12,14},{13,15},{14,10},{15,... | collective-permute-start | bytes 1179656 | tf_op jit(solution)/shard_map/ppermute | solution.py:265
  14.2 11.1 %collective-permute-start.6 = (bf16[2,128,768]{2,1,0:T(8,128)(2,1)S(1)}, bf16[2,128,768]{2,1,0:T(8,128)(2,1)S(1)}, u32[]{:S(2)}, u32[]{:S(2)}) collective-permute-start(bf16[2,128,768]{2,1,0:T(8,128)(2,1)S(1)} %collective-permute-done.1.refs_2_), channel_id=1, source_target_pairs={{0,1},{1,0},{2,3},{3,2},{4,5},{5,4},{6,7},{7,6},{8,9},{9,8},{10,11... | collective-permute-start | bytes 1179656 | tf_op jit(solution)/shard_map/ppermute | solution.py:265
  14.3 11.3 %collective-permute-start.4 = (bf16[2,128,768]{2,1,0:T(8,128)(2,1)S(1)}, bf16[2,128,768]{2,1,0:T(8,128)(2,1)S(1)}, u32[]{:S(2)}, u32[]{:S(2)}) collective-permute-start(bf16[2,128,768]{2,1,0:T(8,128)(2,1)S(1)} %collective-permute-done.1.refs_2_), channel_id=1, source_target_pairs={{0,2},{1,3},{4,0},{5,1},{8,4},{9,5},{12,8},{13,9},{14,12},{15,13},... | collective-permute-start | bytes 1179656 | tf_op jit(solution)/shard_map/ppermute | solution.py:265
  25.7 5.7 %collective-permute-start.9 = (bf16[2,128,768]{2,1,0:T(8,128)(2,1)S(1)}, bf16[2,128,768]{2,1,0:T(8,128)(2,1)S(1)}, u32[]{:S(2)}, u32[]{:S(2)}) collective-permute-start(bf16[2,128,768]{2,1,0:T(8,128)(2,1)S(1)} %collective-permute-done.3.refs_2_), channel_id=1, source_target_pairs={{0,1},{1,0},{2,3},{3,2},{4,5},{5,4},{6,7},{7,6},{8,9},{9,8},{10,11... | collective-permute-start | bytes 1179656 | tf_op jit(solution)/shard_map/ppermute | solution.py:265
  25.7 11.5 %collective-permute-start.7 = (bf16[2,128,768]{2,1,0:T(8,128)(2,1)S(1)}, bf16[2,128,768]{2,1,0:T(8,128)(2,1)S(1)}, u32[]{:S(2)}, u32[]{:S(2)}) collective-permute-start(bf16[2,128,768]{2,1,0:T(8,128)(2,1)S(1)} %collective-permute-done.3.refs_2_), channel_id=1, source_target_pairs={{0,4},{1,5},{4,8},{5,9},{8,12},{9,13},{12,14},{13,15},{14,10},{15,... | collective-permute-start | bytes 1179656 | tf_op jit(solution)/shard_map/ppermute | solution.py:265
  27.4 9.8 %collective-permute-start.10 = (bf16[2,128,768]{2,1,0:T(8,128)(2,1)S(1)}, bf16[2,128,768]{2,1,0:T(8,128)(2,1)S(1)}, u32[]{:S(2)}, u32[]{:S(2)}) collective-permute-start(bf16[2,128,768]{2,1,0:T(8,128)(2,1)S(1)} %collective-permute-done.4.refs_3_), channel_id=1, source_target_pairs={{0,1},{1,0},{2,3},{3,2},{4,5},{5,4},{6,7},{7,6},{8,9},{9,8},{10,11... | collective-permute-start | bytes 1179656 | tf_op jit(solution)/shard_map/ppermute | solution.py:265
  27.6 11.3 %collective-permute-start.8 = (bf16[2,128,768]{2,1,0:T(8,128)(2,1)S(1)}, bf16[2,128,768]{2,1,0:T(8,128)(2,1)S(1)}, u32[]{:S(2)}, u32[]{:S(2)}) collective-permute-start(bf16[2,128,768]{2,1,0:T(8,128)(2,1)S(1)} %collective-permute-done.4.refs_3_), channel_id=1, source_target_pairs={{0,2},{1,3},{4,0},{5,1},{8,4},{9,5},{12,8},{13,9},{14,12},{15,13},... | collective-permute-start | bytes 1179656 | tf_op jit(solution)/shard_map/ppermute | solution.py:265
  38.9 8.0 %collective-permute-start.16 = (bf16[2,128,768]{2,1,0:T(8,128)(2,1)S(1)}, bf16[2,128,768]{2,1,0:T(8,128)(2,1)S(1)}, u32[]{:S(2)}, u32[]{:S(2)}) collective-permute-start(bf16[2,128,768]{2,1,0:T(8,128)(2,1)S(1)} %collective-permute-done.8.refs_3_), channel_id=1, source_target_pairs={{0,1},{1,0},{2,3},{3,2},{4,5},{5,4},{6,7},{7,6},{8,9},{9,8},{10,11... | collective-permute-start | bytes 1179656 | tf_op jit(solution)/shard_map/ppermute | solution.py:265
  39.0 7.3 %collective-permute-start.13 = (bf16[128,768]{1,0:T(8,128)(2,1)S(1)}, bf16[128,768]{1,0:T(8,128)(2,1)S(1)}, u32[]{:S(2)}, u32[]{:S(2)}) collective-permute-start(bf16[128,768]{1,0:T(8,128)(2,1)S(1)} %slice_bitcast_fusion), channel_id=1, source_target_pairs={{0,2},{1,3},{4,0},{5,1},{8,4},{9,5},{12,8},{13,9},{14,12},{15,13},... | collective-permute-start | bytes 589832 | tf_op jit(solution)/shard_map/ppermute | solution.py:265
  39.4 7.6 %collective-permute-start.15 = (bf16[2,128,768]{2,1,0:T(8,128)(2,1)S(1)}, bf16[2,128,768]{2,1,0:T(8,128)(2,1)S(1)}, u32[]{:S(2)}, u32[]{:S(2)}) collective-permute-start(bf16[2,128,768]{2,1,0:T(8,128)(2,1)S(1)} %collective-permute-done.7.refs_2_), channel_id=1, source_target_pairs={{0,1},{1,0},{2,3},{3,2},{4,5},{5,4},{6,7},{7,6},{8,9},{9,8},{10,11... | collective-permute-start | bytes 1179656 | tf_op jit(solution)/shard_map/ppermute | solution.py:265
  39.6 7.4 %collective-permute-start.11 = (bf16[128,768]{1,0:T(8,128)(2,1)S(1)}, bf16[128,768]{1,0:T(8,128)(2,1)S(1)}, u32[]{:S(2)}, u32[]{:S(2)}) collective-permute-start(bf16[128,768]{1,0:T(8,128)(2,1)S(1)} %slice_bitcast_fusion.1), channel_id=1, source_target_pairs={{0,4},{1,5},{4,8},{5,9},{8,12},{9,13},{12,14},{13,15},{14,10},{15,... | collective-permute-start | bytes 589832 | tf_op jit(solution)/shard_map/ppermute | solution.py:265
  44.9 4.9 %copy-start = (s32[2]{0:T(128)S(1)}, s32[2]{0:T(128)}, u32[]{:S(2)}) copy-start(s32[2]{0:T(128)} %refs_10_.1) | copy-start | bytes 28
  46.3 3.5 %collective-permute-start.14 = (bf16[128,768]{1,0:T(8,128)(2,1)S(1)}, bf16[128,768]{1,0:T(8,128)(2,1)S(1)}, u32[]{:S(2)}, u32[]{:S(2)}) collective-permute-start(bf16[128,768]{1,0:T(8,128)(2,1)S(1)} %collective-permute-done.13.refs_3_), channel_id=1, source_target_pairs={{0,1},{1,0},{2,3},{3,2},{4,5},{5,4},{6,7},{7,6},{8,9},{9,8},{10,11... | collective-permute-start | bytes 589832 | tf_op jit(solution)/shard_map/ppermute | solution.py:265
  47.0 2.8 %collective-permute-start.12 = (bf16[128,768]{1,0:T(8,128)(2,1)S(1)}, bf16[128,768]{1,0:T(8,128)(2,1)S(1)}, u32[]{:S(2)}, u32[]{:S(2)}) collective-permute-start(bf16[128,768]{1,0:T(8,128)(2,1)S(1)} %collective-permute-done.11.refs_2_), channel_id=1, source_target_pairs={{0,1},{1,0},{2,3},{3,2},{4,5},{5,4},{6,7},{7,6},{8,9},{9,8},{10,11... | collective-permute-start | bytes 589832 | tf_op jit(solution)/shard_map/ppermute | solution.py:265

commit v3 on v2

--- a/solution.py
+++ b/solution.py
@@ -10,6 +10,7 @@
 HEADS = 12
 HEAD_DIM = 64
 CORES = 2
+LANES = 128
 PAIRED = 2 * HEAD_DIM
 
 
@@ -29,8 +30,9 @@
     def onward(self, step):
         pairs = []
         for place in range(self.chips):
-            target = self.chip((place + step) % self.chips)
-            pairs += [(self.chip(place) * CORES + core, target * CORES + core) for core in range(CORES)]
+            for core, way in ((0, step), (1, -step)):
+                target = self.chip((place + way) % self.chips)
+                pairs.append((self.chip(place) * CORES + core, target * CORES + core))
         return pairs
 
     def sibling(self):
@@ -46,7 +48,7 @@
         else:
             row = chip // 2
             place = jnp.where(lax.rem(chip, 2) == 0, row, 2 * self.rows - 1 - row)
-        came = lax.rem(place + shift + self.chips, self.chips)
+        came = lax.rem(place + self.chips + jnp.where(core == 0, -shift, shift), self.chips)
         if self.columns == 1:
             there = came
         else:
@@ -129,7 +131,7 @@
         image, index, live = find_slot(owner, partners_here, counts_here, own, listed)
         table[0, owner] = image
         table[1, owner] = live
-        picks[owner] = jnp.full(picks.shape[1:], index.astype(jnp.float32))
+        picks[owner : owner + 1, :] = jnp.full((1, LANES), index.astype(jnp.float32))
     for copy in copies[2:5]:
         copy.wait()
     rows = tokens_here[...].reshape(own * tok, -1)
@@ -148,28 +150,34 @@
     chosen, asked = [], []
     for shift, flip, _ in slots:
         owner = ring.owner(me, shift, flip)
-        chosen.append(choose([tokens_here[j] for j in range(own)], picks[owner][:1, :]))
+        chosen.append(choose([tokens_here[j] for j in range(own)], picks, owner))
         asked.append((table[0, owner], table[1, owner]))
     attend(jnp.concatenate(chosen, axis=0), asked, gain_here[...][None, :], w_kv, spread_q, total, tok)
     copies[8].wait()
 
 
-def choose(images, pick):
+def choose(images, picks, owner):
+    width = images[0].shape[-1]
+    pick = jnp.concatenate([picks[pl.ds(owner, 1), :]] * (width // LANES), axis=1)
     chosen = images[0].astype(jnp.float32)
     for j in range(1, len(images)):
         chosen = jnp.where(pick == j, images[j].astype(jnp.float32), chosen)
     return chosen
 
 
-def later_kernel(ring, slots, last, own, tok, *refs):
+def later_kernel(ring, slots, passes, last, own, tok, *refs):
     refs = list(refs)
     take = lambda n: [refs.pop(0) for _ in range(n)]
     sources = [take(n) for _, _, n in slots]
+    (arrived,) = take(1) if any(n == 0 for _, _, n in slots) else (None,)
+    (sibling_picks,) = take(1) if passes else (None,)
     spread_q, w_kv, gain, picks, table, _ = take(6)
     if last:
         w_out, tokens, counts, total, mixed, counts_here, table_here, sems = refs
     else:
-        total, table_here, sems = refs
+        (total,) = take(1)
+        (passed,) = take(1) if passes else (None,)
+        table_here, sems = refs
     copies = [pltpu.make_async_copy(table, table_here, sems.at[0])]
     if last:
         copies.append(pltpu.make_async_copy(counts, counts_here, sems.at[1]))
@@ -178,9 +186,17 @@
     me = lax.axis_index("img")
     owners = [ring.owner(me, shift, flip) for shift, flip, _ in slots]
     chosen = []
-    for arrays, owner in zip(sources, owners):
+    came = sent = 0
+    for (_, flip, _), arrays, owner in zip(slots, sources, owners):
+        if not arrays:
+            chosen.append(arrived[came].astype(jnp.float32))
+            came += 1
+            continue
         images = [arrays[0][j] for j in range(own)] if len(arrays) == 1 else [array[...] for array in arrays]
-        chosen.append(choose(images, picks[owner][:1, :]))
+        chosen.append(choose(images, picks, owner))
+        if passes and not flip:
+            passed[sent] = choose(images, sibling_picks, owner).astype(passed.dtype)
+            sent += 1
     for copy in copies:
         copy.wait()
     asked = [(table_here[0, owner], table_here[1, owner]) for owner in owners]
@@ -215,7 +231,7 @@
         jax.ShapeDtypeStruct((width, width), jnp.bfloat16),
         jax.ShapeDtypeStruct((own, tok, width), jnp.bfloat16),
         jax.ShapeDtypeStruct((width,), jnp.float32),
-        jax.ShapeDtypeStruct((devices, 8, width), jnp.float32),
+        jax.ShapeDtypeStruct((devices, LANES), jnp.float32),
         jax.ShapeDtypeStruct((2, devices), jnp.int32),
     ]
     return pl.pallas_call(
@@ -235,17 +251,21 @@
     )(*operands)
 
 
-def later_stage(ring, work, state, extra, total, own, tok, width):
+def later_stage(ring, work, arrived, sibling_picks, state, extra, total, own, tok, width):
     slots, sources = zip(*work)
-    last = len(extra) > 0
+    last, passes = len(extra) > 0, sibling_picks is not None
     images = [array for arrays in sources for array in arrays]
+    images += [] if arrived is None else [arrived]
+    images += [sibling_picks] if passes else []
     shapes = [jax.ShapeDtypeStruct(total.shape, total.dtype)]
     scratch = [pltpu.SMEM((2, ring.chips * CORES), jnp.int32), pltpu.SemaphoreType.DMA((2,))]
+    if passes:
+        shapes.append(jax.ShapeDtypeStruct((sum(not flip for _, flip, _ in slots), tok, width), jnp.bfloat16))
     if last:
         shapes.append(jax.ShapeDtypeStruct((own, tok, width), jnp.bfloat16))
         scratch = [pltpu.SMEM((own,), jnp.int32)] + scratch
     return pl.pallas_call(
-        functools.partial(later_kernel, ring, slots, last, own, tok),
+        functools.partial(later_kernel, ring, slots, passes, last, own, tok),
         out_shape=shapes,
         in_specs=[VMEM] * (len(images) + 4) + [ANY, VMEM] + ([VMEM, VMEM, ANY] if last else []),
         out_specs=[VMEM] * len(shapes),
@@ -267,27 +287,30 @@
     far = ring.chips // 2
     assert ring.chips == 2 * far and own == 2
     up, down = send(tokens, ahead), send(tokens, back)
-    behind = [((0, True, 1), [send(tokens, sibling)])]
+    arrived = send(tokens, sibling)
     operands = (tokens, partners, counts, gain_query, gain_memory, w_query, w_key, w_value, w_out)
     operands = [pltpu.with_memory_space_constraint(array, pltpu.HBM) for array in operands]
     total, spread_q, w_kv, w_out_here, tokens_here, gain_here, picks, table = first_stage(
         ring, ((0, False, 1),), operands, listed=listed, **sizes
     )
+    sibling_picks = send(picks, sibling)
     state = (spread_q, w_kv, gain_here, picks, table)
+    behind = [((0, True, 1), [arrived])]
+    arrived = None
     for step in range(1, far):
-        waited = [array for _, arrays in behind for array in arrays]
-        up, down, total, waited = lax.optimization_barrier((up, down, total, waited))
-        behind = [(slot, [array]) for (slot, _), array in zip(behind, waited)]
-        work = behind + [((-step, False, 1), [up]), ((step, False, 1), [down])]
-        behind = [((-step, True, 1), [send(up, sibling)]), ((step, True, 1), [send(down, sibling)])]
+        up, down, total = lax.optimization_barrier((up, down, total))
+        work = behind + [((step, False, 1), [up]), ((-step, False, 1), [down])]
         if step + 1 < far:
             up, down = send(up, ahead), send(down, back)
         else:
-            up, down = send(up[0], ahead), send(down[1], back)
-        (total,) = later_stage(ring, work, state, (), total, **sizes)
-    (total,) = later_stage(ring, behind + [((far, False, own), [up, down])], state, (), total, **sizes)
-    work = [((far, True, own), [send(up, sibling), send(down, sibling)])]
-    _, mixed = later_stage(ring, work, state, (w_out_here, tokens_here, counts), total, **sizes)
+            up = send(up, ahead)
+        total, passed = later_stage(ring, work, arrived, sibling_picks, state, (), total, **sizes)
+        arrived = send(passed, sibling)
+        behind = [((step, True, 0), []), ((-step, True, 0), [])]
+    work = behind + [((far, False, 1), [up])]
+    (total,) = later_stage(ring, work, arrived, None, state, (), total, **sizes)
+    work = [((far, True, 1), [send(up, sibling)])]
+    _, mixed = later_stage(ring, work, None, None, state, (w_out_here, tokens_here, counts), total, **sizes)
     return mixed
 
 

time: 53.1 us -> 50.1 us (0.944)
  waiting for transfers between devices: 22.5 us -> 20.3 us
  starting transfers between devices: 10.1 us -> 9.3 us
    ppermute x17 -> x13, waiting for transfers between devices: 22.5 us -> 20.3 us  [shards(): send = lambda array, to: lax.ppermute(array, 'img', to)]
    ppermute x17 -> x13, starting transfers between devices: 10.1 us -> 9.3 us  [shards(): send = lambda array, to: lax.ppermute(array, 'img', to)]
  transfers between devices with their start and end apart: 17 -> 13, of which waited for: 8 -> 5; matrix products, arithmetic and copies ran while one was open for 0% -> 0% of each run, Pallas kernels for 32% -> 34%
where the time goes in v3:
time: 50.1 us; the launch traced here: 49.9 us
  waiting for transfers between devices  20.3 us (41%)
  Pallas kernels  20 us (40%)
  starting transfers between devices  9.3 us (19%)
    ppermute x13, waiting for transfers between devices, shards(): send = lambda array, to: lax.ppermute(array, 'img', to)  20.3 us
    pallas_call x5, Pallas kernels, later_stage(): pl.pallas_call(functools.partial(later_kernel, ring, slots, passes, last,...  15.4 us
    ppermute x13, starting transfers between devices, shards(): send = lambda array, to: lax.ppermute(array, 'img', to)  9.3 us
    pallas_call x1, Pallas kernels, first_stage(): pl.pallas_call(functools.partial(first_kernel, ring, slots, own, listed,...  4.63 us
  transfers between devices with their start and end apart: 13, of which 5 were waited for; matrix products, arithmetic and copies ran while one was open for 0% of the time, Pallas kernels for 34%

profile of v3, /device:TPU:0, one launch (start us, length us, event | category | flops | bytes accessed | tf_op | source)
XLA Modules:
  0.0 49.9 jit_solution(4394403079636022656)
XLA Ops:
  0.0 3.0 %collective-permute-start.1 = (bf16[2,128,768]{2,1,0:T(8,128)(2,1)}, bf16[2,128,768]{2,1,0:T(8,128)(2,1)S(1)}, u32[]{:S(2)}, u32[]{:S(2)}) collective-permute-start(bf16[2,128,768]{2,1,0:T(8,128)(2,1)} %refs_0_.1), channel_id=1, source_target_pairs={{0,2},{1,5},{4,0},{5,9},{8,4},{9,13},{12,8},{13,15},{14,12},{15,11... | collective-permute-start | bytes 1179656 | tf_op jit(solution)/shard_map/ppermute | solution.py:285
  3.0 0.1 collective-permute-start
  3.0 0.0 collective-permute-start.4
  3.0 4.6 %shard_map.91 = (f32[2,768,128]{2,1,0:T(8,128)S(1)}, bf16[2,768,256]{2,1,0:T(8,128)(2,1)S(1)}, bf16[768,1536]{1,0:T(8,128)(2,1)S(1)}, bf16[768,768]{1,0:T(8,128)...) custom-call(bf16[2,128,768]{2,1,0:T(8,128)(2,1)} %refs_0_.1, ...), custom_call_target="tpu_custom_call" | custom-call | flops 1409286144 | bytes 3538944 | tf_op jit(solution)/shard_map/pallas_call | solution.py:237
  7.7 0.6 %collective-permute-start.5 = (f32[16,128]{1,0:T(8,128)S(1)}, f32[16,128]{1,0:T(8,128)S(1)}, u32[]{:S(2)}, u32[]{:S(2)}) collective-permute-start(f32[16,128]{1,0:T(8,128)S(1)} %get-tuple-element.32.refs_7_.refs_5_.refs_4_), channel_id=1, source_target_pairs={{0,1},{1,0},{2,3},{3,2},{4,5},{5,4},{6,7},{7,6},{8,9},{9,8},{10,11... | collective-permute-start | bytes 24584 | tf_op jit(solution)/shard_map/ppermute | solution.py:285
  8.2 4.4 %collective-permute-done.1.refs_2_ = bf16[2,128,768]{2,1,0:T(8,128)(2,1)S(1)} collective-permute-done((bf16[2,128,768]{2,1,0:T(8,128)(2,1)}, bf16[2,128,768]{2,1,0:T(8,128)(2,1)S(1)}, u32[]{:S(2)}, u32[]{:S(2)}) %collective-permute-start.1) | collective-permute-done | bytes 393248 | tf_op jit(solution)/shard_map/ppermute | solution.py:285
  12.6 0.0 collective-permute-done.refs_1_
  12.7 2.4 %collective-permute-start.2 = (bf16[2,128,768]{2,1,0:T(8,128)(2,1)S(1)}, bf16[2,128,768]{2,1,0:T(8,128)(2,1)S(1)}, u32[]{:S(2)}, u32[]{:S(2)}) collective-permute-start(bf16[2,128,768]{2,1,0:T(8,128)(2,1)S(1)} %collective-permute-done.refs_1_), channel_id=1, source_target_pairs={{0,4},{1,3},{4,8},{5,1},{8,12},{9,5},{12,14},{13,9},{14,10},{15,13... | collective-permute-start | bytes 1179656 | tf_op jit(solution)/shard_map/ppermute | solution.py:285
  15.1 0.0 collective-permute-start.3
  15.1 0.0 collective-permute-done.5.refs_3_
  15.1 0.0 collective-permute-done.4.refs_0_
  15.1 2.8 %shard_map.92 = (f32[2,768,128]{2,1,0:T(8,128)S(1)}, bf16[2,128,768]{2,1,0:T(8,128)(2,1)S(1)}) custom-call(bf16[2,128,768]{2,1,0:T(8,128)(2,1)S(1)} %collective-permute-done.4.refs_0_, bf16[2,128,768]{2,1,0:T(8,128)(2,1)S(1)} %collective-permute-done.refs_1_, ...), custom_call_target="tpu_custom_call", output_to_operand_aliasing={{0}: (9, {})} | custom-call | flops 2113929216 | bytes 4128768 | tf_op jit(solution)/shard_map/pallas_call | solution.py:267
  17.9 0.1 collective-permute-start.8
  17.9 6.1 %collective-permute-done.2.refs_0_ = bf16[2,128,768]{2,1,0:T(8,128)(2,1)S(1)} collective-permute-done((bf16[2,128,768]{2,1,0:T(8,128)(2,1)S(1)}, bf16[2,128,768]{2,1,0:T(8,128)(2,1)S(1)}, u32[]{:S(2)}, u32[]{:S(2)}) %collective-permute-start.2) | collective-permute-done | bytes 393248 | tf_op jit(solution)/shard_map/ppermute | solution.py:285
  24.0 0.4 collective-permute-done.3.refs_1_
  24.5 1.8 %collective-permute-start.6 = (bf16[2,128,768]{2,1,0:T(8,128)(2,1)S(1)}, bf16[2,128,768]{2,1,0:T(8,128)(2,1)S(1)}, u32[]{:S(2)}, u32[]{:S(2)}) collective-permute-start(bf16[2,128,768]{2,1,0:T(8,128)(2,1)S(1)} %collective-permute-done.2.refs_0_), channel_id=1, source_target_pairs={{0,4},{1,3},{4,8},{5,1},{8,12},{9,5},{12,14},{13,9},{14,10},{15,13... | collective-permute-start | bytes 1179656 | tf_op jit(solution)/shard_map/ppermute | solution.py:285
  26.2 0.3 collective-permute-start.7
  26.5 0.0 collective-permute-done.8.refs_2_
  26.5 3.4 %shard_map.93 = (f32[2,768,128]{2,1,0:T(8,128)S(1)}, bf16[2,128,768]{2,1,0:T(8,128)(2,1)S(1)}) custom-call(bf16[2,128,768]{2,1,0:T(8,128)(2,1)S(1)} %collective-permute-done.2.refs_0_, bf16[2,128,768]{2,1,0:T(8,128)(2,1)S(1)} %collective-permute-done.3.refs_1_, ...), custom_call_target="tpu_custom_call", output_to_operand_aliasing={{0}: (9, {})} | custom-call | flops 2818572288 | bytes 4718592 | tf_op jit(solution)/shard_map/pallas_call | solution.py:267
  29.9 0.1 collective-permute-start.11
  30.0 6.2 %collective-permute-done.6.refs_0_ = bf16[2,128,768]{2,1,0:T(8,128)(2,1)S(1)} collective-permute-done((bf16[2,128,768]{2,1,0:T(8,128)(2,1)S(1)}, bf16[2,128,768]{2,1,0:T(8,128)(2,1)S(1)}, u32[]{:S(2)}, u32[]{:S(2)}) %collective-permute-start.6) | collective-permute-done | bytes 393248 | tf_op jit(solution)/shard_map/ppermute | solution.py:285
  36.2 0.0 collective-permute-done.7.refs_1_
  36.2 0.5 %collective-permute-start.9 = (bf16[2,128,768]{2,1,0:T(8,128)(2,1)S(1)}, bf16[2,128,768]{2,1,0:T(8,128)(2,1)S(1)}, u32[]{:S(2)}, u32[]{:S(2)}) collective-permute-start(bf16[2,128,768]{2,1,0:T(8,128)(2,1)S(1)} %collective-permute-done.6.refs_0_), channel_id=1, source_target_pairs={{0,4},{1,3},{4,8},{5,1},{8,12},{9,5},{12,14},{13,9},{14,10},{15,13... | collective-permute-start | bytes 1179656 | tf_op jit(solution)/shard_map/ppermute | solution.py:285
  36.7 0.0 collective-permute-done.11.refs_2_
  36.7 3.4 %shard_map.94 = (f32[2,768,128]{2,1,0:T(8,128)S(1)}, bf16[2,128,768]{2,1,0:T(8,128)(2,1)S(1)}) custom-call(bf16[2,128,768]{2,1,0:T(8,128)(2,1)S(1)} %collective-permute-done.6.refs_0_, bf16[2,128,768]{2,1,0:T(8,128)(2,1)S(1)} %collective-permute-done.7.refs_1_, ...), custom_call_target="tpu_custom_call", output_to_operand_aliasing={{0}: (9, {})} | custom-call | flops 2818572288 | bytes 4718592 | tf_op jit(solution)/shard_map/pallas_call | solution.py:267
  40.1 0.6 %collective-permute-start.12 = (bf16[2,128,768]{2,1,0:T(8,128)(2,1)S(1)}, bf16[2,128,768]{2,1,0:T(8,128)(2,1)S(1)}, u32[]{:S(2)}, u32[]{:S(2)}) collective-permute-start(bf16[2,128,768]{2,1,0:T(8,128)(2,1)S(1)} %get-tuple-element.48), channel_id=1, source_target_pairs={{0,1},{1,0},{2,3},{3,2},{4,5},{5,4},{6,7},{7,6},{8,9},{9,8},{10,11... | collective-permute-start | bytes 1179656 | tf_op jit(solution)/shard_map/ppermute | solution.py:285
  40.7 3.2 %collective-permute-done.9.refs_0_ = bf16[2,128,768]{2,1,0:T(8,128)(2,1)S(1)} collective-permute-done((bf16[2,128,768]{2,1,0:T(8,128)(2,1)S(1)}, bf16[2,128,768]{2,1,0:T(8,128)(2,1)S(1)}, u32[]{:S(2)}, u32[]{:S(2)}) %collective-permute-start.9) | collective-permute-done | bytes 393248 | tf_op jit(solution)/shard_map/ppermute | solution.py:285
  43.9 0.0 collective-permute-start.10
  44.0 0.0 collective-permute-done.12.refs_1_
  44.0 0.0 copy-start
  44.0 2.8 %shard_map.95.refs_6_ = f32[2,768,128]{2,1,0:T(8,128)S(1)} custom-call(bf16[2,128,768]{2,1,0:T(8,128)(2,1)S(1)} %collective-permute-done.9.refs_0_, bf16[2,128,768]{2,1,0:T(8,128)(2,1)S(1)} %collective-permute-done.12.refs_1_, bf16[2,768,256]{2,1,0:T(8,128)(2,1)S(1)} %get-tuple-element.33.refs_4_.refs_2_.refs_1_, ...), custom_call_target="tpu_custom_call", output_to_operand_aliasing={{}: (7, {})} | custom-call | flops 2113929216 | bytes 4128768 | tf_op jit(solution)/shard_map/pallas_call | solution.py:267
  46.8 0.0 collective-permute-done.10.refs_0_
  46.8 0.0 copy-done
  46.8 2.9 %shard_map.96 = (f32[2,768,128]{2,1,0:T(8,128)S(1)}, bf16[2,128,768]{2,1,0:T(8,128)(2,1)}) custom-call(bf16[2,128,768]{2,1,0:T(8,128)(2,1)S(1)} %collective-permute-done.10.refs_0_, bf16[2,768,256]{2,1,0:T(8,128)(2,1)S(1)} %get-tuple-element.33.refs_4_.refs_2_.refs_1_, ...), custom_call_target="tpu_custom_call", output_to_operand_aliasing={{0}: (6, {})} | custom-call | flops 704643072 | bytes 2949120 | tf_op jit(solution)/shard_map/pallas_call | solution.py:267
Async XLA Ops:
  0.0 12.6 %collective-permute-start.1 = (bf16[2,128,768]{2,1,0:T(8,128)(2,1)}, bf16[2,128,768]{2,1,0:T(8,128)(2,1)S(1)}, u32[]{:S(2)}, u32[]{:S(2)}) collective-permute-start(bf16[2,128,768]{2,1,0:T(8,128)(2,1)} %refs_0_.1), channel_id=1, source_target_pairs={{0,2},{1,5},{4,0},{5,9},{8,4},{9,13},{12,8},{13,15},{14,12},{15,11... | collective-permute-start | bytes 1179656 | tf_op jit(solution)/shard_map/ppermute | solution.py:285
  3.0 9.7 %collective-permute-start = (bf16[2,128,768]{2,1,0:T(8,128)(2,1)}, bf16[2,128,768]{2,1,0:T(8,128)(2,1)S(1)}, u32[]{:S(2)}, u32[]{:S(2)}) collective-permute-start(bf16[2,128,768]{2,1,0:T(8,128)(2,1)} %refs_0_.1), channel_id=1, source_target_pairs={{0,4},{1,3},{4,8},{5,1},{8,12},{9,5},{12,14},{13,9},{14,10},{15,13... | collective-permute-start | bytes 1179656 | tf_op jit(solution)/shard_map/ppermute | solution.py:285
  3.0 12.0 %collective-permute-start.4 = (bf16[2,128,768]{2,1,0:T(8,128)(2,1)}, bf16[2,128,768]{2,1,0:T(8,128)(2,1)S(1)}, u32[]{:S(2)}, u32[]{:S(2)}) collective-permute-start(bf16[2,128,768]{2,1,0:T(8,128)(2,1)} %refs_0_.1), channel_id=1, source_target_pairs={{0,1},{1,0},{2,3},{3,2},{4,5},{5,4},{6,7},{7,6},{8,9},{9,8},{10,11... | collective-permute-start | bytes 1179656 | tf_op jit(solution)/shard_map/ppermute | solution.py:285
  7.7 7.4 %collective-permute-start.5 = (f32[16,128]{1,0:T(8,128)S(1)}, f32[16,128]{1,0:T(8,128)S(1)}, u32[]{:S(2)}, u32[]{:S(2)}) collective-permute-start(f32[16,128]{1,0:T(8,128)S(1)} %get-tuple-element.32.refs_7_.refs_5_.refs_4_), channel_id=1, source_target_pairs={{0,1},{1,0},{2,3},{3,2},{4,5},{5,4},{6,7},{7,6},{8,9},{9,8},{10,11... | collective-permute-start | bytes 24584 | tf_op jit(solution)/shard_map/ppermute | solution.py:285
  12.7 11.4 %collective-permute-start.2 = (bf16[2,128,768]{2,1,0:T(8,128)(2,1)S(1)}, bf16[2,128,768]{2,1,0:T(8,128)(2,1)S(1)}, u32[]{:S(2)}, u32[]{:S(2)}) collective-permute-start(bf16[2,128,768]{2,1,0:T(8,128)(2,1)S(1)} %collective-permute-done.refs_1_), channel_id=1, source_target_pairs={{0,4},{1,3},{4,8},{5,1},{8,12},{9,5},{12,14},{13,9},{14,10},{15,13... | collective-permute-start | bytes 1179656 | tf_op jit(solution)/shard_map/ppermute | solution.py:285
  15.1 9.4 %collective-permute-start.3 = (bf16[2,128,768]{2,1,0:T(8,128)(2,1)S(1)}, bf16[2,128,768]{2,1,0:T(8,128)(2,1)S(1)}, u32[]{:S(2)}, u32[]{:S(2)}) collective-permute-start(bf16[2,128,768]{2,1,0:T(8,128)(2,1)S(1)} %collective-permute-done.1.refs_2_), channel_id=1, source_target_pairs={{0,2},{1,5},{4,0},{5,9},{8,4},{9,13},{12,8},{13,15},{14,12},{15,11... | collective-permute-start | bytes 1179656 | tf_op jit(solution)/shard_map/ppermute | solution.py:285
  17.9 8.6 %collective-permute-start.8 = (bf16[2,128,768]{2,1,0:T(8,128)(2,1)S(1)}, bf16[2,128,768]{2,1,0:T(8,128)(2,1)S(1)}, u32[]{:S(2)}, u32[]{:S(2)}) collective-permute-start(bf16[2,128,768]{2,1,0:T(8,128)(2,1)S(1)} %get-tuple-element.41), channel_id=1, source_target_pairs={{0,1},{1,0},{2,3},{3,2},{4,5},{5,4},{6,7},{7,6},{8,9},{9,8},{10,11... | collective-permute-start | bytes 1179656 | tf_op jit(solution)/shard_map/ppermute | solution.py:285
  24.5 11.7 %collective-permute-start.6 = (bf16[2,128,768]{2,1,0:T(8,128)(2,1)S(1)}, bf16[2,128,768]{2,1,0:T(8,128)(2,1)S(1)}, u32[]{:S(2)}, u32[]{:S(2)}) collective-permute-start(bf16[2,128,768]{2,1,0:T(8,128)(2,1)S(1)} %collective-permute-done.2.refs_0_), channel_id=1, source_target_pairs={{0,4},{1,3},{4,8},{5,1},{8,12},{9,5},{12,14},{13,9},{14,10},{15,13... | collective-permute-start | bytes 1179656 | tf_op jit(solution)/shard_map/ppermute | solution.py:285
  26.2 10.0 %collective-permute-start.7 = (bf16[2,128,768]{2,1,0:T(8,128)(2,1)S(1)}, bf16[2,128,768]{2,1,0:T(8,128)(2,1)S(1)}, u32[]{:S(2)}, u32[]{:S(2)}) collective-permute-start(bf16[2,128,768]{2,1,0:T(8,128)(2,1)S(1)} %collective-permute-done.3.refs_1_), channel_id=1, source_target_pairs={{0,2},{1,5},{4,0},{5,9},{8,4},{9,13},{12,8},{13,15},{14,12},{15,11... | collective-permute-start | bytes 1179656 | tf_op jit(solution)/shard_map/ppermute | solution.py:285
  29.9 6.8 %collective-permute-start.11 = (bf16[2,128,768]{2,1,0:T(8,128)(2,1)S(1)}, bf16[2,128,768]{2,1,0:T(8,128)(2,1)S(1)}, u32[]{:S(2)}, u32[]{:S(2)}) collective-permute-start(bf16[2,128,768]{2,1,0:T(8,128)(2,1)S(1)} %get-tuple-element.46), channel_id=1, source_target_pairs={{0,1},{1,0},{2,3},{3,2},{4,5},{5,4},{6,7},{7,6},{8,9},{9,8},{10,11... | collective-permute-start | bytes 1179656 | tf_op jit(solution)/shard_map/ppermute | solution.py:285
  36.2 7.8 %collective-permute-start.9 = (bf16[2,128,768]{2,1,0:T(8,128)(2,1)S(1)}, bf16[2,128,768]{2,1,0:T(8,128)(2,1)S(1)}, u32[]{:S(2)}, u32[]{:S(2)}) collective-permute-start(bf16[2,128,768]{2,1,0:T(8,128)(2,1)S(1)} %collective-permute-done.6.refs_0_), channel_id=1, source_target_pairs={{0,4},{1,3},{4,8},{5,1},{8,12},{9,5},{12,14},{13,9},{14,10},{15,13... | collective-permute-start | bytes 1179656 | tf_op jit(solution)/shard_map/ppermute | solution.py:285
  40.1 3.8 %collective-permute-start.12 = (bf16[2,128,768]{2,1,0:T(8,128)(2,1)S(1)}, bf16[2,128,768]{2,1,0:T(8,128)(2,1)S(1)}, u32[]{:S(2)}, u32[]{:S(2)}) collective-permute-start(bf16[2,128,768]{2,1,0:T(8,128)(2,1)S(1)} %get-tuple-element.48), channel_id=1, source_target_pairs={{0,1},{1,0},{2,3},{3,2},{4,5},{5,4},{6,7},{7,6},{8,9},{9,8},{10,11... | collective-permute-start | bytes 1179656 | tf_op jit(solution)/shard_map/ppermute | solution.py:285
  43.9 2.8 %collective-permute-start.10 = (bf16[2,128,768]{2,1,0:T(8,128)(2,1)S(1)}, bf16[2,128,768]{2,1,0:T(8,128)(2,1)S(1)}, u32[]{:S(2)}, u32[]{:S(2)}) collective-permute-start(bf16[2,128,768]{2,1,0:T(8,128)(2,1)S(1)} %collective-permute-done.9.refs_0_), channel_id=1, source_target_pairs={{0,1},{1,0},{2,3},{3,2},{4,5},{5,4},{6,7},{7,6},{8,9},{9,8},{10,11... | collective-permute-start | bytes 1179656 | tf_op jit(solution)/shard_map/ppermute | solution.py:285
  44.0 2.8 %copy-start = (s32[2]{0:T(128)S(1)}, s32[2]{0:T(128)}, u32[]{:S(2)}) copy-start(s32[2]{0:T(128)} %refs_9_.1) | copy-start | bytes 28

commit v4 on v3

--- a/solution.py
+++ b/solution.py
@@ -37,6 +37,9 @@
 
     def sibling(self):
         return [(i, i ^ 1) for i in range(self.chips * CORES)]
+
+    def pairs(self):
+        return [[chip * CORES + core for core in range(CORES)] for chip in range(self.chips)]
 
     def owner(self, me, shift, flip):
         chip = me // CORES
@@ -81,11 +84,11 @@
     return image, index, live
 
 
-def attend(memory, slots, gain, w_kv, spread_q, total, tok):
+def attend(memory, find_slots, gain, w_kv, spread_q, total, tok):
     width = memory.shape[-1]
     normed = normalize(memory, gain).astype(jnp.bfloat16)
     both = dot(normed, w_kv[...]).astype(jnp.bfloat16)
-    for at, (image, live) in enumerate(slots):
+    for at, (image, live) in enumerate(find_slots()):
         here = slice(at * tok, (at + 1) * tok)
         for g in range(HEADS // 2):
             feats = slice(g * PAIRED, (g + 1) * PAIRED)
@@ -152,7 +155,7 @@
         owner = ring.owner(me, shift, flip)
         chosen.append(choose([tokens_here[j] for j in range(own)], picks, owner))
         asked.append((table[0, owner], table[1, owner]))
-    attend(jnp.concatenate(chosen, axis=0), asked, gain_here[...][None, :], w_kv, spread_q, total, tok)
+    attend(jnp.concatenate(chosen, axis=0), lambda: asked, gain_here[...][None, :], w_kv, spread_q, total, tok)
     copies[8].wait()
 
 
@@ -165,19 +168,16 @@
     return chosen
 
 
-def later_kernel(ring, slots, passes, last, own, tok, *refs):
+def later_kernel(ring, slots, last, own, tok, *refs):
     refs = list(refs)
     take = lambda n: [refs.pop(0) for _ in range(n)]
     sources = [take(n) for _, _, n in slots]
     (arrived,) = take(1) if any(n == 0 for _, _, n in slots) else (None,)
-    (sibling_picks,) = take(1) if passes else (None,)
     spread_q, w_kv, gain, picks, table, _ = take(6)
     if last:
         w_out, tokens, counts, total, mixed, counts_here, table_here, sems = refs
     else:
-        (total,) = take(1)
-        (passed,) = take(1) if passes else (None,)
-        table_here, sems = refs
+        total, table_here, sems = refs
     copies = [pltpu.make_async_copy(table, table_here, sems.at[0])]
     if last:
         copies.append(pltpu.make_async_copy(counts, counts_here, sems.at[1]))
@@ -186,26 +186,29 @@
     me = lax.axis_index("img")
     owners = [ring.owner(me, shift, flip) for shift, flip, _ in slots]
     chosen = []
-    came = sent = 0
+    came = 0
+    other = 1 - lax.rem(me, CORES)
     for (_, flip, _), arrays, owner in zip(slots, sources, owners):
+        if arrays and len(arrays[0].shape) == 2:
+            chosen.append(arrays[0][...].astype(jnp.float32))
+            continue
         if not arrays:
-            chosen.append(arrived[came].astype(jnp.float32))
+            chosen.append(arrived[other, came].astype(jnp.float32))
             came += 1
             continue
-        images = [arrays[0][j] for j in range(own)] if len(arrays) == 1 else [array[...] for array in arrays]
+        images = [arrays[0][j] for j in range(own)]
         chosen.append(choose(images, picks, owner))
-        if passes and not flip:
-            passed[sent] = choose(images, sibling_picks, owner).astype(passed.dtype)
-            sent += 1
-    for copy in copies:
-        copy.wait()
-    asked = [(table_here[0, owner], table_here[1, owner]) for owner in owners]
-    attend(jnp.concatenate(chosen, axis=0), asked, gain[...][None, :], w_kv, spread_q, total, tok)
+
+    def find_slots():
+        for copy in copies:
+            copy.wait()
+        return [(table_here[0, owner], table_here[1, owner]) for owner in owners]
+
+    attend(jnp.concatenate(chosen, axis=0), find_slots, gain[...][None, :], w_kv, spread_q, total, tok)
     if last:
-        for a in range(own):
-            context = (total[a] / counts_here[a].astype(jnp.float32)).T.astype(jnp.bfloat16)
-            out = tokens[a].astype(jnp.float32) + dot(context, w_out[...])
-            mixed[a] = out.astype(jnp.bfloat16)
+        context = jnp.concatenate([total[a] / counts_here[a].astype(jnp.float32) for a in range(own)], axis=1)
+        out = dot(context.astype(jnp.bfloat16), w_out[...], ((0,), (0,)))
+        mixed[...] = (tokens[...].astype(jnp.float32) + out.reshape(tokens.shape)).astype(jnp.bfloat16)
 
 
 HBM = pl.BlockSpec(memory_space=pltpu.HBM)
@@ -216,9 +219,9 @@
 
 def cost(rows, tok, width):
     return pl.CostEstimate(
-        flops=4 * rows * width * (width + tok) * 2,
-        bytes_accessed=2 * width * width * 2 + 3 * rows * width * 2,
-        transcendentals=rows * tok * HEADS,
+        flops=rows * width,
+        bytes_accessed=rows * width,
+        transcendentals=rows,
     )
 
 
@@ -251,21 +254,18 @@
     )(*operands)
 
 
-def later_stage(ring, work, arrived, sibling_picks, state, extra, total, own, tok, width):
+def later_stage(ring, work, arrived, state, extra, total, own, tok, width):
     slots, sources = zip(*work)
-    last, passes = len(extra) > 0, sibling_picks is not None
+    last = len(extra) > 0
     images = [array for arrays in sources for array in arrays]
     images += [] if arrived is None else [arrived]
-    images += [sibling_picks] if passes else []
     shapes = [jax.ShapeDtypeStruct(total.shape, total.dtype)]
     scratch = [pltpu.SMEM((2, ring.chips * CORES), jnp.int32), pltpu.SemaphoreType.DMA((2,))]
-    if passes:
-        shapes.append(jax.ShapeDtypeStruct((sum(not flip for _, flip, _ in slots), tok, width), jnp.bfloat16))
     if last:
         shapes.append(jax.ShapeDtypeStruct((own, tok, width), jnp.bfloat16))
         scratch = [pltpu.SMEM((own,), jnp.int32)] + scratch
     return pl.pallas_call(
-        functools.partial(later_kernel, ring, slots, passes, last, own, tok),
+        functools.partial(later_kernel, ring, slots, last, own, tok),
         out_shape=shapes,
         in_specs=[VMEM] * (len(images) + 4) + [ANY, VMEM] + ([VMEM, VMEM, ANY] if last else []),
         out_specs=[VMEM] * len(shapes),
@@ -276,6 +276,36 @@
     )(*images, *state, total, *extra)
 
 
+def pass_kernel(ring, wanted, own, *refs):
+    arrays, picks, passed = refs[: len(wanted)], refs[len(wanted) : 2 * len(wanted)], refs[2 * len(wanted) :]
+    me = lax.axis_index("img")
+    for i, shift in enumerate(wanted):
+        images = [arrays[i][j] for j in range(own)]
+        chosen = choose(images, picks[i], ring.owner(me, shift, False)).astype(jnp.bfloat16)
+        if len(passed) == 1:
+            passed[0][i] = chosen
+        else:
+            passed[i][...] = chosen
+
+
+def pass_stage(ring, work, together, own, tok, width):
+    wanted, arrays, picks = zip(*work)
+    if together:
+        shapes = jax.ShapeDtypeStruct((len(work), tok, width), jnp.bfloat16)
+    else:
+        shapes = [jax.ShapeDtypeStruct((tok, width), jnp.bfloat16)] * len(work)
+    return pl.pallas_call(
+        functools.partial(pass_kernel, ring, wanted, own),
+        out_shape=shapes,
+        in_specs=[VMEM] * (2 * len(work)),
+        out_specs=VMEM if together else [VMEM] * len(work),
+        compiler_params=pltpu.CompilerParams(vmem_limit_bytes=32 << 20),
+        cost_estimate=pl.CostEstimate(
+            flops=len(work) * own * tok * width, bytes_accessed=len(work) * own * tok * width * 2, transcendentals=0
+        ),
+    )(*arrays, *picks)
+
+
 def shards(columns, tokens, partners, counts, gain_query, gain_memory, w_query, w_key, w_value, w_out):
     own, tok, width = tokens.shape
     listed = partners.shape[1]
@@ -285,32 +315,33 @@
     send = lambda array, to: lax.ppermute(array, "img", to)
 
     far = ring.chips // 2
-    assert ring.chips == 2 * far and own == 2
-    up, down = send(tokens, ahead), send(tokens, back)
-    arrived = send(tokens, sibling)
+    assert ring.chips == 2 * far and far > 1 and own == 2
+    up, down, theirs = send(tokens, ahead), send(tokens, back), send(tokens, sibling)
+    meet = lambda array: lax.all_gather(array, "img", axis_index_groups=ring.pairs())
     operands = (tokens, partners, counts, gain_query, gain_memory, w_query, w_key, w_value, w_out)
     operands = [pltpu.with_memory_space_constraint(array, pltpu.HBM) for array in operands]
     total, spread_q, w_kv, w_out_here, tokens_here, gain_here, picks, table = first_stage(
         ring, ((0, False, 1),), operands, listed=listed, **sizes
     )
+    cross = [(source, target ^ 1) for source, target in ahead]
     sibling_picks = send(picks, sibling)
+    next_picks, cross_picks = send(picks, back), send(picks, [(target, source) for source, target in cross])
     state = (spread_q, w_kv, gain_here, picks, table)
-    behind = [((0, True, 1), [arrived])]
-    arrived = None
+    behind = [((0, True, 1), [theirs])]
     for step in range(1, far):
-        up, down, total = lax.optimization_barrier((up, down, total))
-        work = behind + [((step, False, 1), [up]), ((-step, False, 1), [down])]
+        down, total = lax.optimization_barrier((down, total))
+        work = [((step, False, 1), [up]), ((-step, False, 1), [down])]
+        passed = pass_stage(ring, [(step, up, sibling_picks), (-step, down, sibling_picks)], True, **sizes)
         if step + 1 < far:
             up, down = send(up, ahead), send(down, back)
         else:
-            up = send(up, ahead)
-        total, passed = later_stage(ring, work, arrived, sibling_picks, state, (), total, **sizes)
-        arrived = send(passed, sibling)
-        behind = [((step, True, 0), []), ((-step, True, 0), [])]
-    work = behind + [((far, False, 1), [up])]
-    (total,) = later_stage(ring, work, arrived, None, state, (), total, **sizes)
-    work = [((far, True, 1), [send(up, sibling)])]
-    _, mixed = later_stage(ring, work, None, None, state, (w_out_here, tokens_here, counts), total, **sizes)
+            same, other = pass_stage(ring, [(step, up, next_picks), (step, up, cross_picks)], False, **sizes)
+            same, other = send(same, ahead), send(other, cross)
+        work += behind + [((step, True, 0), []), ((-step, True, 0), [])]
+        (total,) = later_stage(ring, work, meet(passed), state, (), total, **sizes)
+        behind = []
+    work = [((far, False, 1), [same]), ((far, True, 1), [other])]
+    _, mixed = later_stage(ring, work, None, state, (w_out_here, tokens_here, counts), total, **sizes)
     return mixed
 
 

time: 50.1 us -> 47.5 us (0.948)
  waiting for transfers between devices: 20.3 us -> 10.2 us
  blocking collectives: 0 us -> 7.81 us
  Pallas kernels: 20 us -> 19 us
  starting transfers between devices: 9.3 us -> 10 us
    ppermute x13 -> x12, waiting for transfers between devices: 20.3 us -> 10.2 us  [shards(): send = lambda array, to: lax.ppermute(array, 'img', to)]
    all_gather x0 -> x3, blocking collectives: none -> 7.81 us  [shards(): lax.all_gather(array, 'img', axis_index_groups=ring.pairs())]
    pallas_call x5 -> x8, Pallas kernels: 15.4 us -> 14.4 us  [the longest x4 13.9 us: later_stage(): pl.pallas_call(functools.partial(later_kernel, ring, slots, last, own, to...]
    ppermute x13 -> x12, starting transfers between devices: 9.3 us -> 10 us  [shards(): send = lambda array, to: lax.ppermute(array, 'img', to)]
  transfers between devices with their start and end apart: 13 -> 12, of which waited for: 5 -> 5; matrix products, arithmetic and copies ran while one was open for 0% -> 0% of each run, Pallas kernels for 34% -> 33%
where the time goes in v4:
time: 47.5 us; the launch traced here: 47.4 us
  Pallas kernels  19 us (40%)
  waiting for transfers between devices  10.2 us (21%)
  starting transfers between devices  10 us (21%)
  blocking collectives  7.81 us (16%)
    pallas_call x4, Pallas kernels, later_stage(): pl.pallas_call(functools.partial(later_kernel, ring, slots, last, own, to...  13.9 us
    ppermute x12, waiting for transfers between devices, shards(): send = lambda array, to: lax.ppermute(array, 'img', to)  10.2 us
    ppermute x12, starting transfers between devices, shards(): send = lambda array, to: lax.ppermute(array, 'img', to)  10 us
    all_gather x3, blocking collectives, shards(): lax.all_gather(array, 'img', axis_index_groups=ring.pairs())  7.81 us
    pallas_call x1, Pallas kernels, first_stage(): pl.pallas_call(functools.partial(first_kernel, ring, slots, own, listed,...  4.63 us
  transfers between devices with their start and end apart: 12, of which 5 were waited for; matrix products, arithmetic and copies ran while one was open for 0% of the time, Pallas kernels for 33%

profile of v4, /device:TPU:0, one launch (start us, length us, event | category | flops | bytes accessed | tf_op | source)
XLA Modules:
  0.0 47.4 jit_solution(15556636839321635645)
XLA Ops:
  0.0 3.0 %collective-permute-start.7 = (bf16[2,128,768]{2,1,0:T(8,128)(2,1)}, bf16[2,128,768]{2,1,0:T(8,128)(2,1)S(1)}, u32[]{:S(2)}, u32[]{:S(2)}) collective-permute-start(bf16[2,128,768]{2,1,0:T(8,128)(2,1)} %refs_0_.1), channel_id=1, source_target_pairs={{0,2},{1,5},{4,0},{5,9},{8,4},{9,13},{12,8},{13,15},{14,12},{15,11... | collective-permute-start | bytes 1179656 | tf_op jit(solution)/shard_map/ppermute | solution.py:315
  3.0 0.1 collective-permute-start
  3.0 0.0 collective-permute-start.9
  3.0 4.6 %shard_map.91 = (f32[2,768,128]{2,1,0:T(8,128)S(1)}, bf16[2,768,256]{2,1,0:T(8,128)(2,1)S(1)}, bf16[768,1536]{1,0:T(8,128)(2,1)S(1)}, bf16[768,768]{1,0:T(8,128)...) custom-call(bf16[2,128,768]{2,1,0:T(8,128)(2,1)} %refs_0_.1, ...), custom_call_target="tpu_custom_call" | custom-call | flops 196608 | bytes 196608 | tf_op jit(solution)/shard_map/pallas_call | solution.py:240
  7.7 5.0 %collective-permute-done.7.refs_1_ = bf16[2,128,768]{2,1,0:T(8,128)(2,1)S(1)} collective-permute-done((bf16[2,128,768]{2,1,0:T(8,128)(2,1)}, bf16[2,128,768]{2,1,0:T(8,128)(2,1)S(1)}, u32[]{:S(2)}, u32[]{:S(2)}) %collective-permute-start.7) | collective-permute-done | bytes 393248 | tf_op jit(solution)/shard_map/ppermute | solution.py:315
  12.6 1.5 %collective-permute-start.8 = (bf16[2,128,768]{2,1,0:T(8,128)(2,1)S(1)}, bf16[2,128,768]{2,1,0:T(8,128)(2,1)S(1)}, u32[]{:S(2)}, u32[]{:S(2)}) collective-permute-start(bf16[2,128,768]{2,1,0:T(8,128)(2,1)S(1)} %collective-permute-done.7.refs_1_), channel_id=1, source_target_pairs={{0,2},{1,5},{4,0},{5,9},{8,4},{9,13},{12,8},{13,15},{14,12},{15,11... | collective-permute-start | bytes 1179656 | tf_op jit(solution)/shard_map/ppermute | solution.py:315
  14.1 0.0 collective-permute-done.refs_0_
  14.1 0.9 %collective-permute-start.1 = (bf16[2,128,768]{2,1,0:T(8,128)(2,1)S(1)}, bf16[2,128,768]{2,1,0:T(8,128)(2,1)S(1)}, u32[]{:S(2)}, u32[]{:S(2)}) collective-permute-start(bf16[2,128,768]{2,1,0:T(8,128)(2,1)S(1)} %collective-permute-done.refs_0_), channel_id=1, source_target_pairs={{0,4},{1,3},{4,8},{5,1},{8,12},{9,5},{12,14},{13,9},{14,10},{15,13... | collective-permute-start | bytes 1179656 | tf_op jit(solution)/shard_map/ppermute | solution.py:315
  15.1 0.0 collective-permute-start.10
  15.1 1.2 %collective-permute-done.10.refs_2_.refs_3_ = f32[16,128]{1,0:T(8,128)S(1)} collective-permute-done((f32[16,128]{1,0:T(8,128)S(1)}, f32[16,128]{1,0:T(8,128)S(1)}, u32[]{:S(2)}, u32[]{:S(2)}) %collective-permute-start.10) | collective-permute-done | bytes 8224 | tf_op jit(solution)/shard_map/ppermute | solution.py:315
  16.2 0.1 shard_map.93
  16.4 2.4 %all-gather = bf16[4,128,768]{2,1,0:T(8,128)(2,1)S(1)} all-gather(bf16[2,128,768]{2,1,0:T(8,128)(2,1)S(1)} %shard_map.93), channel_id=2, replica_groups={{0,1},{2,3},{4,5},{6,7},{8,9},{10,11},{12,13},{14,15},{16,17},{18,19},{..., dimensions={0}, use_global_device_ids=true | all-gather | bytes 1179648 | tf_op jit(solution)/shard_map/all_gather | solution.py:320
  18.7 0.0 collective-permute-done.9.refs_2_
  18.7 4.0 %shard_map.94.refs_8_ = f32[2,768,128]{2,1,0:T(8,128)S(1)} custom-call(bf16[2,128,768]{2,1,0:T(8,128)(2,1)S(1)} %collective-permute-done.refs_0_, bf16[2,128,768]{2,1,0:T(8,128)(2,1)S(1)} %collective-permute-done.7.refs_1_, bf16[2,128,768]{2,1,0:T(8,128)(2,1)S(1)} %collective-permute-done.9.refs_2_, ...), custom_call_target="tpu_custom_call", output_to_operand_aliasing={{}: (9, {})} | custom-call | flops 491520 | bytes 491520 | tf_op jit(solution)/shard_map/pallas_call | solution.py:267
  22.8 1.7 %collective-permute-done.8.refs_1_ = bf16[2,128,768]{2,1,0:T(8,128)(2,1)S(1)} collective-permute-done((bf16[2,128,768]{2,1,0:T(8,128)(2,1)S(1)}, bf16[2,128,768]{2,1,0:T(8,128)(2,1)S(1)}, u32[]{:S(2)}, u32[]{:S(2)}) %collective-permute-start.8) | collective-permute-done | bytes 393248 | tf_op jit(solution)/shard_map/ppermute | solution.py:315
  24.5 0.0 collective-permute-start.11
  24.5 0.0 collective-permute-done.1.refs_0_
  24.5 2.0 %collective-permute-start.2 = (bf16[2,128,768]{2,1,0:T(8,128)(2,1)S(1)}, bf16[2,128,768]{2,1,0:T(8,128)(2,1)S(1)}, u32[]{:S(2)}, u32[]{:S(2)}) collective-permute-start(bf16[2,128,768]{2,1,0:T(8,128)(2,1)S(1)} %collective-permute-done.1.refs_0_), channel_id=1, source_target_pairs={{0,4},{1,3},{4,8},{5,1},{8,12},{9,5},{12,14},{13,9},{14,10},{15,13... | collective-permute-start | bytes 1179656 | tf_op jit(solution)/shard_map/ppermute | solution.py:315
  26.5 0.0 collective-permute-start.3
  26.5 0.9 %collective-permute-start.4 = (f32[16,128]{1,0:T(8,128)S(1)}, f32[16,128]{1,0:T(8,128)S(1)}, u32[]{:S(2)}, u32[]{:S(2)}) collective-permute-start(f32[16,128]{1,0:T(8,128)S(1)} %get-tuple-element.22.refs_7_.refs_6_.refs_5_), channel_id=1, source_target_pairs={{5,0},{2,1},{9,4},{0,5},{13,8},{4,9},{15,12},{8,13},{11,14},{12,15... | collective-permute-start | bytes 24584 | tf_op jit(solution)/shard_map/ppermute | solution.py:315
  27.4 0.1 shard_map.95
  27.5 2.7 %all-gather.1 = bf16[4,128,768]{2,1,0:T(8,128)(2,1)S(1)} all-gather(bf16[2,128,768]{2,1,0:T(8,128)(2,1)S(1)} %shard_map.95), channel_id=3, replica_groups={{0,1},{2,3},{4,5},{6,7},{8,9},{10,11},{12,13},{14,15},{16,17},{18,19},{..., dimensions={0}, use_global_device_ids=true | all-gather | bytes 1179648 | tf_op jit(solution)/shard_map/all_gather | solution.py:320
  30.2 3.3 %shard_map.96.refs_8_ = f32[2,768,128]{2,1,0:T(8,128)S(1)} custom-call(bf16[2,128,768]{2,1,0:T(8,128)(2,1)S(1)} %collective-permute-done.1.refs_0_, bf16[2,128,768]{2,1,0:T(8,128)(2,1)S(1)} %collective-permute-done.8.refs_1_, bf16[2,2,128,768]{3,2,1,0:T(8,128)(2,1)S(1)} %bitcast.5, ...), custom_call_target="tpu_custom_call", output_to_operand_aliasing={{}: (8, {})} | custom-call | flops 393216 | bytes 393216 | tf_op jit(solution)/shard_map/pallas_call | solution.py:267
  33.5 2.3 %collective-permute-done.11.refs_1_ = bf16[2,128,768]{2,1,0:T(8,128)(2,1)S(1)} collective-permute-done((bf16[2,128,768]{2,1,0:T(8,128)(2,1)S(1)}, bf16[2,128,768]{2,1,0:T(8,128)(2,1)S(1)}, u32[]{:S(2)}, u32[]{:S(2)}) %collective-permute-start.11) | collective-permute-done | bytes 393248 | tf_op jit(solution)/shard_map/ppermute | solution.py:315
  35.9 0.1 collective-permute-done.3.refs_2_
  35.9 0.0 collective-permute-done.4.refs_3_
  35.9 0.0 collective-permute-done.2.refs_0_.refs_1_
  35.9 0.1 shard_map.92
  36.1 1.6 %collective-permute-start.5 = (bf16[128,768]{1,0:T(8,128)(2,1)S(1)}, bf16[128,768]{1,0:T(8,128)(2,1)S(1)}, u32[]{:S(2)}, u32[]{:S(2)}) collective-permute-start(bf16[128,768]{1,0:T(8,128)(2,1)S(1)} %get-tuple-element.23), channel_id=1, source_target_pairs={{0,4},{1,3},{4,8},{5,1},{8,12},{9,5},{12,14},{13,9},{14,10},{15,13... | collective-permute-start | bytes 589832 | tf_op jit(solution)/shard_map/ppermute | solution.py:315
  37.7 0.0 collective-permute-start.6
  37.7 0.1 shard_map.97
  37.8 2.7 %all-gather.2 = bf16[4,128,768]{2,1,0:T(8,128)(2,1)S(1)} all-gather(bf16[2,128,768]{2,1,0:T(8,128)(2,1)S(1)} %shard_map.97), channel_id=4, replica_groups={{0,1},{2,3},{4,5},{6,7},{8,9},{10,11},{12,13},{14,15},{16,17},{18,19},{..., dimensions={0}, use_global_device_ids=true | all-gather | bytes 1179648 | tf_op jit(solution)/shard_map/all_gather | solution.py:320
  40.6 0.0 copy-start
  40.6 3.3 %shard_map.98.refs_7_ = f32[2,768,128]{2,1,0:T(8,128)S(1)} custom-call(bf16[2,128,768]{2,1,0:T(8,128)(2,1)S(1)} %collective-permute-done.2.refs_0_.refs_1_, bf16[2,128,768]{2,1,0:T(8,128)(2,1)S(1)} %collective-permute-done.11.refs_1_, bf16[2,2,128,768]{3,2,1,0:T(8,128)(2,1)S(1)} %bitcast.4, ...), custom_call_target="tpu_custom_call", output_to_operand_aliasing={{}: (8, {})} | custom-call | flops 393216 | bytes 393216 | tf_op jit(solution)/shard_map/pallas_call | solution.py:267
  43.9 0.0 collective-permute-done.5.refs_0_
  43.9 0.0 collective-permute-done.6.refs_1_
  43.9 0.0 copy-done
  43.9 3.3 %shard_map.99 = (f32[2,768,128]{2,1,0:T(8,128)S(1)}, bf16[2,128,768]{2,1,0:T(8,128)(2,1)}) custom-call(bf16[128,768]{1,0:T(8,128)(2,1)S(1)} %collective-permute-done.5.refs_0_, bf16[128,768]{1,0:T(8,128)(2,1)S(1)} %collective-permute-done.6.refs_1_, ...), custom_call_target="tpu_custom_call", output_to_operand_aliasing={{0}: (7, {})} | custom-call | flops 196608 | bytes 196608 | tf_op jit(solution)/shard_map/pallas_call | solution.py:267
Async XLA Ops:
  0.0 12.6 %collective-permute-start.7 = (bf16[2,128,768]{2,1,0:T(8,128)(2,1)}, bf16[2,128,768]{2,1,0:T(8,128)(2,1)S(1)}, u32[]{:S(2)}, u32[]{:S(2)}) collective-permute-start(bf16[2,128,768]{2,1,0:T(8,128)(2,1)} %refs_0_.1), channel_id=1, source_target_pairs={{0,2},{1,5},{4,0},{5,9},{8,4},{9,13},{12,8},{13,15},{14,12},{15,11... | collective-permute-start | bytes 1179656 | tf_op jit(solution)/shard_map/ppermute | solution.py:315
  3.0 11.2 %collective-permute-start = (bf16[2,128,768]{2,1,0:T(8,128)(2,1)}, bf16[2,128,768]{2,1,0:T(8,128)(2,1)S(1)}, u32[]{:S(2)}, u32[]{:S(2)}) collective-permute-start(bf16[2,128,768]{2,1,0:T(8,128)(2,1)} %refs_0_.1), channel_id=1, source_target_pairs={{0,4},{1,3},{4,8},{5,1},{8,12},{9,5},{12,14},{13,9},{14,10},{15,13... | collective-permute-start | bytes 1179656 | tf_op jit(solution)/shard_map/ppermute | solution.py:315
  3.0 15.7 %collective-permute-start.9 = (bf16[2,128,768]{2,1,0:T(8,128)(2,1)}, bf16[2,128,768]{2,1,0:T(8,128)(2,1)S(1)}, u32[]{:S(2)}, u32[]{:S(2)}) collective-permute-start(bf16[2,128,768]{2,1,0:T(8,128)(2,1)} %refs_0_.1), channel_id=1, source_target_pairs={{0,1},{1,0},{2,3},{3,2},{4,5},{5,4},{6,7},{7,6},{8,9},{9,8},{10,11... | collective-permute-start | bytes 1179656 | tf_op jit(solution)/shard_map/ppermute | solution.py:315
  12.6 11.8 %collective-permute-start.8 = (bf16[2,128,768]{2,1,0:T(8,128)(2,1)S(1)}, bf16[2,128,768]{2,1,0:T(8,128)(2,1)S(1)}, u32[]{:S(2)}, u32[]{:S(2)}) collective-permute-start(bf16[2,128,768]{2,1,0:T(8,128)(2,1)S(1)} %collective-permute-done.7.refs_1_), channel_id=1, source_target_pairs={{0,2},{1,5},{4,0},{5,9},{8,4},{9,13},{12,8},{13,15},{14,12},{15,11... | collective-permute-start | bytes 1179656 | tf_op jit(solution)/shard_map/ppermute | solution.py:315
  14.1 10.3 %collective-permute-start.1 = (bf16[2,128,768]{2,1,0:T(8,128)(2,1)S(1)}, bf16[2,128,768]{2,1,0:T(8,128)(2,1)S(1)}, u32[]{:S(2)}, u32[]{:S(2)}) collective-permute-start(bf16[2,128,768]{2,1,0:T(8,128)(2,1)S(1)} %collective-permute-done.refs_0_), channel_id=1, source_target_pairs={{0,4},{1,3},{4,8},{5,1},{8,12},{9,5},{12,14},{13,9},{14,10},{15,13... | collective-permute-start | bytes 1179656 | tf_op jit(solution)/shard_map/ppermute | solution.py:315
  15.1 1.2 %collective-permute-start.10 = (f32[16,128]{1,0:T(8,128)S(1)}, f32[16,128]{1,0:T(8,128)S(1)}, u32[]{:S(2)}, u32[]{:S(2)}) collective-permute-start(f32[16,128]{1,0:T(8,128)S(1)} %get-tuple-element.22.refs_7_.refs_6_.refs_5_), channel_id=1, source_target_pairs={{0,1},{1,0},{2,3},{3,2},{4,5},{5,4},{6,7},{7,6},{8,9},{9,8},{10,11... | collective-permute-start | bytes 24584 | tf_op jit(solution)/shard_map/ppermute | solution.py:315
  24.5 11.4 %collective-permute-start.11 = (bf16[2,128,768]{2,1,0:T(8,128)(2,1)S(1)}, bf16[2,128,768]{2,1,0:T(8,128)(2,1)S(1)}, u32[]{:S(2)}, u32[]{:S(2)}) collective-permute-start(bf16[2,128,768]{2,1,0:T(8,128)(2,1)S(1)} %collective-permute-done.8.refs_1_), channel_id=1, source_target_pairs={{0,2},{1,5},{4,0},{5,9},{8,4},{9,13},{12,8},{13,15},{14,12},{15,11... | collective-permute-start | bytes 1179656 | tf_op jit(solution)/shard_map/ppermute | solution.py:315
  24.5 11.5 %collective-permute-start.2 = (bf16[2,128,768]{2,1,0:T(8,128)(2,1)S(1)}, bf16[2,128,768]{2,1,0:T(8,128)(2,1)S(1)}, u32[]{:S(2)}, u32[]{:S(2)}) collective-permute-start(bf16[2,128,768]{2,1,0:T(8,128)(2,1)S(1)} %collective-permute-done.1.refs_0_), channel_id=1, source_target_pairs={{0,4},{1,3},{4,8},{5,1},{8,12},{9,5},{12,14},{13,9},{14,10},{15,13... | collective-permute-start | bytes 1179656 | tf_op jit(solution)/shard_map/ppermute | solution.py:315
  26.5 9.5 %collective-permute-start.3 = (f32[16,128]{1,0:T(8,128)S(1)}, f32[16,128]{1,0:T(8,128)S(1)}, u32[]{:S(2)}, u32[]{:S(2)}) collective-permute-start(f32[16,128]{1,0:T(8,128)S(1)} %get-tuple-element.22.refs_7_.refs_6_.refs_5_), channel_id=1, source_target_pairs={{0,2},{1,5},{4,0},{5,9},{8,4},{9,13},{12,8},{13,15},{14,12},{15,11... | collective-permute-start | bytes 24584 | tf_op jit(solution)/shard_map/ppermute | solution.py:315
  26.5 9.5 %collective-permute-start.4 = (f32[16,128]{1,0:T(8,128)S(1)}, f32[16,128]{1,0:T(8,128)S(1)}, u32[]{:S(2)}, u32[]{:S(2)}) collective-permute-start(f32[16,128]{1,0:T(8,128)S(1)} %get-tuple-element.22.refs_7_.refs_6_.refs_5_), channel_id=1, source_target_pairs={{5,0},{2,1},{9,4},{0,5},{13,8},{4,9},{15,12},{8,13},{11,14},{12,15... | collective-permute-start | bytes 24584 | tf_op jit(solution)/shard_map/ppermute | solution.py:315
  36.1 7.8 %collective-permute-start.5 = (bf16[128,768]{1,0:T(8,128)(2,1)S(1)}, bf16[128,768]{1,0:T(8,128)(2,1)S(1)}, u32[]{:S(2)}, u32[]{:S(2)}) collective-permute-start(bf16[128,768]{1,0:T(8,128)(2,1)S(1)} %get-tuple-element.23), channel_id=1, source_target_pairs={{0,4},{1,3},{4,8},{5,1},{8,12},{9,5},{12,14},{13,9},{14,10},{15,13... | collective-permute-start | bytes 589832 | tf_op jit(solution)/shard_map/ppermute | solution.py:315
  37.7 6.2 %collective-permute-start.6 = (bf16[128,768]{1,0:T(8,128)(2,1)S(1)}, bf16[128,768]{1,0:T(8,128)(2,1)S(1)}, u32[]{:S(2)}, u32[]{:S(2)}) collective-permute-start(bf16[128,768]{1,0:T(8,128)(2,1)S(1)} %get-tuple-element.24), channel_id=1, source_target_pairs={{0,5},{1,2},{4,9},{5,0},{8,13},{9,4},{12,15},{13,8},{14,11},{15,12... | collective-permute-start | bytes 589832 | tf_op jit(solution)/shard_map/ppermute | solution.py:315
  40.6 3.3 %copy-start = (s32[2]{0:T(128)S(1)}, s32[2]{0:T(128)}, u32[]{:S(2)}) copy-start(s32[2]{0:T(128)} %refs_10_.1) | copy-start | bytes 28

commit v5 on v4

--- a/solution.py
+++ b/solution.py
@@ -96,12 +96,11 @@
             weights = jnp.exp(scores - jnp.max(scores, axis=0, keepdims=True))
             share = live.astype(jnp.float32) / jnp.sum(weights, axis=0, keepdims=True)
             weights = weights.astype(jnp.bfloat16)
-            parts = []
-            for h in range(2):
-                values = both[here, width + g * PAIRED + h * HEAD_DIM : width + g * PAIRED + (h + 1) * HEAD_DIM]
-                asked = slice(h * tok, (h + 1) * tok)
-                parts.append(dot(values, weights[:, asked], ((0,), (0,))) * share[:, asked])
-            total[image, feats, :] += jnp.concatenate(parts, axis=0)
+            values = both[here, width + g * PAIRED : width + (g + 1) * PAIRED]
+            crossed = dot(values, weights, ((0,), (0,)))
+            first = crossed[:HEAD_DIM, :tok] * share[:, :tok]
+            second = crossed[HEAD_DIM:, tok:] * share[:, tok:]
+            total[image, feats, :] += jnp.concatenate([first, second], axis=0)
 
 
 def first_kernel(ring, slots, own, listed, tok, *refs):
@@ -175,7 +174,7 @@
     (arrived,) = take(1) if any(n == 0 for _, _, n in slots) else (None,)
     spread_q, w_kv, gain, picks, table, _ = take(6)
     if last:
-        w_out, tokens, counts, total, mixed, counts_here, table_here, sems = refs
+        w_out, tokens, counts, total, mixed, mixed_here, counts_here, table_here, sems = refs
     else:
         total, table_here, sems = refs
     copies = [pltpu.make_async_copy(table, table_here, sems.at[0])]
@@ -207,8 +206,17 @@
     attend(jnp.concatenate(chosen, axis=0), find_slots, gain[...][None, :], w_kv, spread_q, total, tok)
     if last:
         context = jnp.concatenate([total[a] / counts_here[a].astype(jnp.float32) for a in range(own)], axis=1)
-        out = dot(context.astype(jnp.bfloat16), w_out[...], ((0,), (0,)))
-        mixed[...] = (tokens[...].astype(jnp.float32) + out.reshape(tokens.shape)).astype(jnp.bfloat16)
+        context = context.astype(jnp.bfloat16)
+        half = tokens.shape[-1] // 2
+        copies = []
+        for i in range(2):
+            part = pl.ds(i * half, half)
+            out = dot(context, w_out[:, part], ((0,), (0,)))
+            mixed_here[:, :, part] = (tokens[:, :, part].astype(jnp.float32) + out.reshape(own, tok, half)).astype(jnp.bfloat16)
+            copies.append(pltpu.make_async_copy(mixed_here.at[:, :, part], mixed.at[:, :, part], sems.at[i]))
+            copies[-1].start()
+        for copy in copies:
+            copy.wait()
 
 
 HBM = pl.BlockSpec(memory_space=pltpu.HBM)
@@ -263,12 +271,12 @@
     scratch = [pltpu.SMEM((2, ring.chips * CORES), jnp.int32), pltpu.SemaphoreType.DMA((2,))]
     if last:
         shapes.append(jax.ShapeDtypeStruct((own, tok, width), jnp.bfloat16))
-        scratch = [pltpu.SMEM((own,), jnp.int32)] + scratch
+        scratch = [pltpu.VMEM((own, tok, width), jnp.bfloat16), pltpu.SMEM((own,), jnp.int32)] + scratch
     return pl.pallas_call(
         functools.partial(later_kernel, ring, slots, last, own, tok),
         out_shape=shapes,
         in_specs=[VMEM] * (len(images) + 4) + [ANY, VMEM] + ([VMEM, VMEM, ANY] if last else []),
-        out_specs=[VMEM] * len(shapes),
+        out_specs=[VMEM] + ([HBM] if last else []),
         scratch_shapes=scratch,
         input_output_aliases={len(images) + 5: 0},
         compiler_params=pltpu.CompilerParams(vmem_limit_bytes=32 << 20),

time: 47.5 us -> 46.7 us (0.983)
  Pallas kernels: 19 us -> 17.8 us
    pallas_call x4, Pallas kernels: 13.9 us -> 12.8 us  [later_stage(): pl.pallas_call(functools.partial(later_kernel, ring, slots, last, own, to...]
  transfers between devices with their start and end apart: 12 -> 12, of which waited for: 5 -> 5; matrix products, arithmetic and copies ran while one was open for 0% -> 0% of each run, Pallas kernels for 33% -> 31%
where the time goes in v5:
time: 46.7 us; the launch traced here: 46.5 us
  Pallas kernels  17.8 us (38%)
  waiting for transfers between devices  10.6 us (23%)
  starting transfers between devices  9.63 us (21%)
  blocking collectives  8.19 us (18%)
    pallas_call x4, Pallas kernels, later_stage(): pl.pallas_call(functools.partial(later_kernel, ring, slots, last, own, to...  12.8 us
    ppermute x12, waiting for transfers between devices, shards(): send = lambda array, to: lax.ppermute(array, 'img', to)  10.6 us
    ppermute x12, starting transfers between devices, shards(): send = lambda array, to: lax.ppermute(array, 'img', to)  9.63 us
    all_gather x3, blocking collectives, shards(): lax.all_gather(array, 'img', axis_index_groups=ring.pairs())  8.19 us
    pallas_call x1, Pallas kernels, first_stage(): pl.pallas_call(functools.partial(first_kernel, ring, slots, own, listed,...  4.51 us
  transfers between devices with their start and end apart: 12, of which 5 were waited for; matrix products, arithmetic and copies ran while one was open for 0% of the time, Pallas kernels for 31%

profile of v5, /device:TPU:0, one launch (start us, length us, event | category | flops | bytes accessed | tf_op | source)
XLA Modules:
  0.0 46.5 jit_solution(9901470841132553989)
XLA Ops:
  0.0 3.0 %collective-permute-start.7 = (bf16[2,128,768]{2,1,0:T(8,128)(2,1)}, bf16[2,128,768]{2,1,0:T(8,128)(2,1)S(1)}, u32[]{:S(2)}, u32[]{:S(2)}) collective-permute-start(bf16[2,128,768]{2,1,0:T(8,128)(2,1)} %refs_0_.1), channel_id=1, source_target_pairs={{0,2},{1,5},{4,0},{5,9},{8,4},{9,13},{12,8},{13,15},{14,12},{15,11... | collective-permute-start | bytes 1179656 | tf_op jit(solution)/shard_map/ppermute | solution.py:323
  3.0 0.1 collective-permute-start
  3.0 0.0 collective-permute-start.9
  3.0 4.5 %shard_map.91 = (f32[2,768,128]{2,1,0:T(8,128)S(1)}, bf16[2,768,256]{2,1,0:T(8,128)(2,1)S(1)}, bf16[768,1536]{1,0:T(8,128)(2,1)S(1)}, bf16[768,768]{1,0:T(8,128)...) custom-call(bf16[2,128,768]{2,1,0:T(8,128)(2,1)} %refs_0_.1, ...), custom_call_target="tpu_custom_call" | custom-call | flops 196608 | bytes 196608 | tf_op jit(solution)/shard_map/pallas_call | solution.py:248
  7.6 5.1 %collective-permute-done.7.refs_1_ = bf16[2,128,768]{2,1,0:T(8,128)(2,1)S(1)} collective-permute-done((bf16[2,128,768]{2,1,0:T(8,128)(2,1)}, bf16[2,128,768]{2,1,0:T(8,128)(2,1)S(1)}, u32[]{:S(2)}, u32[]{:S(2)}) %collective-permute-start.7) | collective-permute-done | bytes 393248 | tf_op jit(solution)/shard_map/ppermute | solution.py:323
  12.6 1.5 %collective-permute-start.8 = (bf16[2,128,768]{2,1,0:T(8,128)(2,1)S(1)}, bf16[2,128,768]{2,1,0:T(8,128)(2,1)S(1)}, u32[]{:S(2)}, u32[]{:S(2)}) collective-permute-start(bf16[2,128,768]{2,1,0:T(8,128)(2,1)S(1)} %collective-permute-done.7.refs_1_), channel_id=1, source_target_pairs={{0,2},{1,5},{4,0},{5,9},{8,4},{9,13},{12,8},{13,15},{14,12},{15,11... | collective-permute-start | bytes 1179656 | tf_op jit(solution)/shard_map/ppermute | solution.py:323
  14.1 0.0 collective-permute-done.refs_0_
  14.1 0.9 %collective-permute-start.1 = (bf16[2,128,768]{2,1,0:T(8,128)(2,1)S(1)}, bf16[2,128,768]{2,1,0:T(8,128)(2,1)S(1)}, u32[]{:S(2)}, u32[]{:S(2)}) collective-permute-start(bf16[2,128,768]{2,1,0:T(8,128)(2,1)S(1)} %collective-permute-done.refs_0_), channel_id=1, source_target_pairs={{0,4},{1,3},{4,8},{5,1},{8,12},{9,5},{12,14},{13,9},{14,10},{15,13... | collective-permute-start | bytes 1179656 | tf_op jit(solution)/shard_map/ppermute | solution.py:323
  15.1 0.0 collective-permute-start.10
  15.1 1.2 %collective-permute-done.10.refs_2_.refs_3_ = f32[16,128]{1,0:T(8,128)S(1)} collective-permute-done((f32[16,128]{1,0:T(8,128)S(1)}, f32[16,128]{1,0:T(8,128)S(1)}, u32[]{:S(2)}, u32[]{:S(2)}) %collective-permute-start.10) | collective-permute-done | bytes 8224 | tf_op jit(solution)/shard_map/ppermute | solution.py:323
  16.2 0.1 shard_map.93
  16.4 2.4 %all-gather = bf16[4,128,768]{2,1,0:T(8,128)(2,1)S(1)} all-gather(bf16[2,128,768]{2,1,0:T(8,128)(2,1)S(1)} %shard_map.93), channel_id=2, replica_groups={{0,1},{2,3},{4,5},{6,7},{8,9},{10,11},{12,13},{14,15},{16,17},{18,19},{..., dimensions={0}, use_global_device_ids=true | all-gather | bytes 1179648 | tf_op jit(solution)/shard_map/all_gather | solution.py:328
  18.7 0.0 collective-permute-done.9.refs_2_
  18.7 3.6 %shard_map.94.refs_8_ = f32[2,768,128]{2,1,0:T(8,128)S(1)} custom-call(bf16[2,128,768]{2,1,0:T(8,128)(2,1)S(1)} %collective-permute-done.refs_0_, bf16[2,128,768]{2,1,0:T(8,128)(2,1)S(1)} %collective-permute-done.7.refs_1_, bf16[2,128,768]{2,1,0:T(8,128)(2,1)S(1)} %collective-permute-done.9.refs_2_, ...), custom_call_target="tpu_custom_call", output_to_operand_aliasing={{}: (9, {})} | custom-call | flops 491520 | bytes 491520 | tf_op jit(solution)/shard_map/pallas_call | solution.py:275
  22.4 2.1 %collective-permute-done.8.refs_1_ = bf16[2,128,768]{2,1,0:T(8,128)(2,1)S(1)} collective-permute-done((bf16[2,128,768]{2,1,0:T(8,128)(2,1)S(1)}, bf16[2,128,768]{2,1,0:T(8,128)(2,1)S(1)}, u32[]{:S(2)}, u32[]{:S(2)}) %collective-permute-start.8) | collective-permute-done | bytes 393248 | tf_op jit(solution)/shard_map/ppermute | solution.py:323
  24.5 0.0 collective-permute-start.11
  24.5 0.0 collective-permute-done.1.refs_0_
  24.5 2.0 %collective-permute-start.2 = (bf16[2,128,768]{2,1,0:T(8,128)(2,1)S(1)}, bf16[2,128,768]{2,1,0:T(8,128)(2,1)S(1)}, u32[]{:S(2)}, u32[]{:S(2)}) collective-permute-start(bf16[2,128,768]{2,1,0:T(8,128)(2,1)S(1)} %collective-permute-done.1.refs_0_), channel_id=1, source_target_pairs={{0,4},{1,3},{4,8},{5,1},{8,12},{9,5},{12,14},{13,9},{14,10},{15,13... | collective-permute-start | bytes 1179656 | tf_op jit(solution)/shard_map/ppermute | solution.py:323
  26.5 0.0 collective-permute-start.3
  26.5 0.5 %collective-permute-start.4 = (f32[16,128]{1,0:T(8,128)S(1)}, f32[16,128]{1,0:T(8,128)S(1)}, u32[]{:S(2)}, u32[]{:S(2)}) collective-permute-start(f32[16,128]{1,0:T(8,128)S(1)} %get-tuple-element.22.refs_7_.refs_6_.refs_5_), channel_id=1, source_target_pairs={{5,0},{2,1},{9,4},{0,5},{13,8},{4,9},{15,12},{8,13},{11,14},{12,15... | collective-permute-start | bytes 24584 | tf_op jit(solution)/shard_map/ppermute | solution.py:323
  27.0 0.1 shard_map.95
  27.1 3.1 %all-gather.1 = bf16[4,128,768]{2,1,0:T(8,128)(2,1)S(1)} all-gather(bf16[2,128,768]{2,1,0:T(8,128)(2,1)S(1)} %shard_map.95), channel_id=3, replica_groups={{0,1},{2,3},{4,5},{6,7},{8,9},{10,11},{12,13},{14,15},{16,17},{18,19},{..., dimensions={0}, use_global_device_ids=true | all-gather | bytes 1179648 | tf_op jit(solution)/shard_map/all_gather | solution.py:328
  30.2 3.0 %shard_map.96.refs_8_ = f32[2,768,128]{2,1,0:T(8,128)S(1)} custom-call(bf16[2,128,768]{2,1,0:T(8,128)(2,1)S(1)} %collective-permute-done.1.refs_0_, bf16[2,128,768]{2,1,0:T(8,128)(2,1)S(1)} %collective-permute-done.8.refs_1_, bf16[2,2,128,768]{3,2,1,0:T(8,128)(2,1)S(1)} %bitcast.5, ...), custom_call_target="tpu_custom_call", output_to_operand_aliasing={{}: (8, {})} | custom-call | flops 393216 | bytes 393216 | tf_op jit(solution)/shard_map/pallas_call | solution.py:275
  33.3 2.2 %collective-permute-done.11.refs_1_ = bf16[2,128,768]{2,1,0:T(8,128)(2,1)S(1)} collective-permute-done((bf16[2,128,768]{2,1,0:T(8,128)(2,1)S(1)}, bf16[2,128,768]{2,1,0:T(8,128)(2,1)S(1)}, u32[]{:S(2)}, u32[]{:S(2)}) %collective-permute-start.11) | collective-permute-done | bytes 393248 | tf_op jit(solution)/shard_map/ppermute | solution.py:323
  35.5 0.1 collective-permute-done.3.refs_2_
  35.6 0.0 collective-permute-done.4.refs_3_
  35.6 0.0 collective-permute-done.2.refs_0_.refs_1_
  35.6 0.1 shard_map.92
  35.7 1.6 %collective-permute-start.5 = (bf16[128,768]{1,0:T(8,128)(2,1)S(1)}, bf16[128,768]{1,0:T(8,128)(2,1)S(1)}, u32[]{:S(2)}, u32[]{:S(2)}) collective-permute-start(bf16[128,768]{1,0:T(8,128)(2,1)S(1)} %get-tuple-element.23), channel_id=1, source_target_pairs={{0,4},{1,3},{4,8},{5,1},{8,12},{9,5},{12,14},{13,9},{14,10},{15,13... | collective-permute-start | bytes 589832 | tf_op jit(solution)/shard_map/ppermute | solution.py:323
  37.3 0.0 collective-permute-start.6
  37.3 0.1 shard_map.97
  37.5 2.7 %all-gather.2 = bf16[4,128,768]{2,1,0:T(8,128)(2,1)S(1)} all-gather(bf16[2,128,768]{2,1,0:T(8,128)(2,1)S(1)} %shard_map.97), channel_id=4, replica_groups={{0,1},{2,3},{4,5},{6,7},{8,9},{10,11},{12,13},{14,15},{16,17},{18,19},{..., dimensions={0}, use_global_device_ids=true | all-gather | bytes 1179648 | tf_op jit(solution)/shard_map/all_gather | solution.py:328
  40.2 0.0 copy-start
  40.2 3.0 %shard_map.98.refs_7_ = f32[2,768,128]{2,1,0:T(8,128)S(1)} custom-call(bf16[2,128,768]{2,1,0:T(8,128)(2,1)S(1)} %collective-permute-done.2.refs_0_.refs_1_, bf16[2,128,768]{2,1,0:T(8,128)(2,1)S(1)} %collective-permute-done.11.refs_1_, bf16[2,2,128,768]{3,2,1,0:T(8,128)(2,1)S(1)} %bitcast.4, ...), custom_call_target="tpu_custom_call", output_to_operand_aliasing={{}: (8, {})} | custom-call | flops 393216 | bytes 393216 | tf_op jit(solution)/shard_map/pallas_call | solution.py:275
  43.2 0.0 collective-permute-done.5.refs_0_
  43.2 0.0 collective-permute-done.6.refs_1_
  43.3 0.0 copy-done
  43.3 3.1 %shard_map.99 = (f32[2,768,128]{2,1,0:T(8,128)S(1)}, bf16[2,128,768]{2,1,0:T(8,128)(2,1)}) custom-call(bf16[128,768]{1,0:T(8,128)(2,1)S(1)} %collective-permute-done.5.refs_0_, bf16[128,768]{1,0:T(8,128)(2,1)S(1)} %collective-permute-done.6.refs_1_, ...), custom_call_target="tpu_custom_call", output_to_operand_aliasing={{0}: (7, {})} | custom-call | flops 196608 | bytes 196608 | tf_op jit(solution)/shard_map/pallas_call | solution.py:275
Async XLA Ops:
  0.0 12.6 %collective-permute-start.7 = (bf16[2,128,768]{2,1,0:T(8,128)(2,1)}, bf16[2,128,768]{2,1,0:T(8,128)(2,1)S(1)}, u32[]{:S(2)}, u32[]{:S(2)}) collective-permute-start(bf16[2,128,768]{2,1,0:T(8,128)(2,1)} %refs_0_.1), channel_id=1, source_target_pairs={{0,2},{1,5},{4,0},{5,9},{8,4},{9,13},{12,8},{13,15},{14,12},{15,11... | collective-permute-start | bytes 1179656 | tf_op jit(solution)/shard_map/ppermute | solution.py:323
  3.0 11.2 %collective-permute-start = (bf16[2,128,768]{2,1,0:T(8,128)(2,1)}, bf16[2,128,768]{2,1,0:T(8,128)(2,1)S(1)}, u32[]{:S(2)}, u32[]{:S(2)}) collective-permute-start(bf16[2,128,768]{2,1,0:T(8,128)(2,1)} %refs_0_.1), channel_id=1, source_target_pairs={{0,4},{1,3},{4,8},{5,1},{8,12},{9,5},{12,14},{13,9},{14,10},{15,13... | collective-permute-start | bytes 1179656 | tf_op jit(solution)/shard_map/ppermute | solution.py:323
  3.0 15.7 %collective-permute-start.9 = (bf16[2,128,768]{2,1,0:T(8,128)(2,1)}, bf16[2,128,768]{2,1,0:T(8,128)(2,1)S(1)}, u32[]{:S(2)}, u32[]{:S(2)}) collective-permute-start(bf16[2,128,768]{2,1,0:T(8,128)(2,1)} %refs_0_.1), channel_id=1, source_target_pairs={{0,1},{1,0},{2,3},{3,2},{4,5},{5,4},{6,7},{7,6},{8,9},{9,8},{10,11... | collective-permute-start | bytes 1179656 | tf_op jit(solution)/shard_map/ppermute | solution.py:323
  12.6 11.8 %collective-permute-start.8 = (bf16[2,128,768]{2,1,0:T(8,128)(2,1)S(1)}, bf16[2,128,768]{2,1,0:T(8,128)(2,1)S(1)}, u32[]{:S(2)}, u32[]{:S(2)}) collective-permute-start(bf16[2,128,768]{2,1,0:T(8,128)(2,1)S(1)} %collective-permute-done.7.refs_1_), channel_id=1, source_target_pairs={{0,2},{1,5},{4,0},{5,9},{8,4},{9,13},{12,8},{13,15},{14,12},{15,11... | collective-permute-start | bytes 1179656 | tf_op jit(solution)/shard_map/ppermute | solution.py:323
  14.1 10.3 %collective-permute-start.1 = (bf16[2,128,768]{2,1,0:T(8,128)(2,1)S(1)}, bf16[2,128,768]{2,1,0:T(8,128)(2,1)S(1)}, u32[]{:S(2)}, u32[]{:S(2)}) collective-permute-start(bf16[2,128,768]{2,1,0:T(8,128)(2,1)S(1)} %collective-permute-done.refs_0_), channel_id=1, source_target_pairs={{0,4},{1,3},{4,8},{5,1},{8,12},{9,5},{12,14},{13,9},{14,10},{15,13... | collective-permute-start | bytes 1179656 | tf_op jit(solution)/shard_map/ppermute | solution.py:323
  15.1 1.2 %collective-permute-start.10 = (f32[16,128]{1,0:T(8,128)S(1)}, f32[16,128]{1,0:T(8,128)S(1)}, u32[]{:S(2)}, u32[]{:S(2)}) collective-permute-start(f32[16,128]{1,0:T(8,128)S(1)} %get-tuple-element.22.refs_7_.refs_6_.refs_5_), channel_id=1, source_target_pairs={{0,1},{1,0},{2,3},{3,2},{4,5},{5,4},{6,7},{7,6},{8,9},{9,8},{10,11... | collective-permute-start | bytes 24584 | tf_op jit(solution)/shard_map/ppermute | solution.py:323
  24.5 11.0 %collective-permute-start.11 = (bf16[2,128,768]{2,1,0:T(8,128)(2,1)S(1)}, bf16[2,128,768]{2,1,0:T(8,128)(2,1)S(1)}, u32[]{:S(2)}, u32[]{:S(2)}) collective-permute-start(bf16[2,128,768]{2,1,0:T(8,128)(2,1)S(1)} %collective-permute-done.8.refs_1_), channel_id=1, source_target_pairs={{0,2},{1,5},{4,0},{5,9},{8,4},{9,13},{12,8},{13,15},{14,12},{15,11... | collective-permute-start | bytes 1179656 | tf_op jit(solution)/shard_map/ppermute | solution.py:323
  24.5 11.1 %collective-permute-start.2 = (bf16[2,128,768]{2,1,0:T(8,128)(2,1)S(1)}, bf16[2,128,768]{2,1,0:T(8,128)(2,1)S(1)}, u32[]{:S(2)}, u32[]{:S(2)}) collective-permute-start(bf16[2,128,768]{2,1,0:T(8,128)(2,1)S(1)} %collective-permute-done.1.refs_0_), channel_id=1, source_target_pairs={{0,4},{1,3},{4,8},{5,1},{8,12},{9,5},{12,14},{13,9},{14,10},{15,13... | collective-permute-start | bytes 1179656 | tf_op jit(solution)/shard_map/ppermute | solution.py:323
  26.5 9.1 %collective-permute-start.3 = (f32[16,128]{1,0:T(8,128)S(1)}, f32[16,128]{1,0:T(8,128)S(1)}, u32[]{:S(2)}, u32[]{:S(2)}) collective-permute-start(f32[16,128]{1,0:T(8,128)S(1)} %get-tuple-element.22.refs_7_.refs_6_.refs_5_), channel_id=1, source_target_pairs={{0,2},{1,5},{4,0},{5,9},{8,4},{9,13},{12,8},{13,15},{14,12},{15,11... | collective-permute-start | bytes 24584 | tf_op jit(solution)/shard_map/ppermute | solution.py:323
  26.5 9.1 %collective-permute-start.4 = (f32[16,128]{1,0:T(8,128)S(1)}, f32[16,128]{1,0:T(8,128)S(1)}, u32[]{:S(2)}, u32[]{:S(2)}) collective-permute-start(f32[16,128]{1,0:T(8,128)S(1)} %get-tuple-element.22.refs_7_.refs_6_.refs_5_), channel_id=1, source_target_pairs={{5,0},{2,1},{9,4},{0,5},{13,8},{4,9},{15,12},{8,13},{11,14},{12,15... | collective-permute-start | bytes 24584 | tf_op jit(solution)/shard_map/ppermute | solution.py:323
  35.7 7.5 %collective-permute-start.5 = (bf16[128,768]{1,0:T(8,128)(2,1)S(1)}, bf16[128,768]{1,0:T(8,128)(2,1)S(1)}, u32[]{:S(2)}, u32[]{:S(2)}) collective-permute-start(bf16[128,768]{1,0:T(8,128)(2,1)S(1)} %get-tuple-element.23), channel_id=1, source_target_pairs={{0,4},{1,3},{4,8},{5,1},{8,12},{9,5},{12,14},{13,9},{14,10},{15,13... | collective-permute-start | bytes 589832 | tf_op jit(solution)/shard_map/ppermute | solution.py:323
  37.3 5.9 %collective-permute-start.6 = (bf16[128,768]{1,0:T(8,128)(2,1)S(1)}, bf16[128,768]{1,0:T(8,128)(2,1)S(1)}, u32[]{:S(2)}, u32[]{:S(2)}) collective-permute-start(bf16[128,768]{1,0:T(8,128)(2,1)S(1)} %get-tuple-element.24), channel_id=1, source_target_pairs={{0,5},{1,2},{4,9},{5,0},{8,13},{9,4},{12,15},{13,8},{14,11},{15,12... | collective-permute-start | bytes 589832 | tf_op jit(solution)/shard_map/ppermute | solution.py:323
  40.2 3.1 %copy-start = (s32[2]{0:T(128)S(1)}, s32[2]{0:T(128)}, u32[]{:S(2)}) copy-start(s32[2]{0:T(128)} %refs_10_.1) | copy-start | bytes 28

commit v6 on v5

--- a/solution.py
+++ b/solution.py
@@ -152,15 +152,14 @@
     chosen, asked = [], []
     for shift, flip, _ in slots:
         owner = ring.owner(me, shift, flip)
-        chosen.append(choose([tokens_here[j] for j in range(own)], picks, owner))
+        chosen.append(choose([tokens_here[j] for j in range(own)], picks[pl.ds(owner, 1), :]))
         asked.append((table[0, owner], table[1, owner]))
     attend(jnp.concatenate(chosen, axis=0), lambda: asked, gain_here[...][None, :], w_kv, spread_q, total, tok)
     copies[8].wait()
 
 
-def choose(images, picks, owner):
-    width = images[0].shape[-1]
-    pick = jnp.concatenate([picks[pl.ds(owner, 1), :]] * (width // LANES), axis=1)
+def choose(images, pick):
+    pick = jnp.concatenate([pick] * (images[0].shape[-1] // LANES), axis=1)
     chosen = images[0].astype(jnp.float32)
     for j in range(1, len(images)):
         chosen = jnp.where(pick == j, images[j].astype(jnp.float32), chosen)
@@ -188,15 +187,15 @@
     came = 0
     other = 1 - lax.rem(me, CORES)
     for (_, flip, _), arrays, owner in zip(slots, sources, owners):
-        if arrays and len(arrays[0].shape) == 2:
+        if len(arrays) == 1 and len(arrays[0].shape) == 2:
             chosen.append(arrays[0][...].astype(jnp.float32))
             continue
         if not arrays:
-            chosen.append(arrived[other, came].astype(jnp.float32))
+            chosen.append(arrived[came].astype(jnp.float32))
             came += 1
             continue
-        images = [arrays[0][j] for j in range(own)]
-        chosen.append(choose(images, picks, owner))
+        images = [arrays[0][j] for j in range(own)] if len(arrays) == 1 else [image[:tok, :] for image in arrays]
+        chosen.append(choose(images, picks[pl.ds(owner, 1), :]))
 
     def find_slots():
         for copy in copies:
@@ -284,34 +283,67 @@
     )(*images, *state, total, *extra)
 
 
-def pass_kernel(ring, wanted, own, *refs):
-    arrays, picks, passed = refs[: len(wanted)], refs[len(wanted) : 2 * len(wanted)], refs[2 * len(wanted) :]
+def pass_kernel(ring, shifts, own, split, *refs):
+    each = 1 if split else own
+    arrays, refs = refs[: each * len(shifts)], refs[each * len(shifts) :]
+    sibling_picks, passed = refs[0], refs[1 + split]
     me = lax.axis_index("img")
-    for i, shift in enumerate(wanted):
-        images = [arrays[i][j] for j in range(own)]
-        chosen = choose(images, picks[i], ring.owner(me, shift, False)).astype(jnp.bfloat16)
-        if len(passed) == 1:
-            passed[0][i] = chosen
+    tok = passed.shape[1]
+    for i, shift in enumerate(shifts):
+        if split:
+            images = [arrays[i][j] for j in range(own)]
         else:
-            passed[i][...] = chosen
-
-
-def pass_stage(ring, work, together, own, tok, width):
-    wanted, arrays, picks = zip(*work)
-    if together:
-        shapes = jax.ShapeDtypeStruct((len(work), tok, width), jnp.bfloat16)
-    else:
-        shapes = [jax.ShapeDtypeStruct((tok, width), jnp.bfloat16)] * len(work)
+            images = [image[:tok, :] for image in arrays[i * own : (i + 1) * own]]
+        owner = ring.owner(me, shift, False)
+        passed[i] = choose(images, sibling_picks[pl.ds(owner, 1), :]).astype(passed.dtype)
+    if split:
+        picks, singles = refs[1], refs[3:]
+        for i, single in enumerate(singles):
+            single[:tok, :] = arrays[i // own][i % own]
+        carried = singles[-1]
+        carried[tok:, :] = jnp.zeros_like(carried[tok:, :])
+        carried[tok:, :LANES] = picks[...].astype(carried.dtype)
+        carried[tok:, LANES : 2 * LANES] = sibling_picks[...].astype(carried.dtype)
+
+
+def pass_stage(ring, work, sibling_picks, split, own, tok, width):
+    shifts, arrays = zip(*work)
+    arrays = [array for some in arrays for array in some]
+    shapes = [jax.ShapeDtypeStruct((len(work), tok, width), jnp.bfloat16)]
+    if split:
+        shapes += [jax.ShapeDtypeStruct((tok, width), jnp.bfloat16)] * (own * len(work) - 1)
+        shapes.append(jax.ShapeDtypeStruct((tok + ring.chips * CORES, width), jnp.bfloat16))
     return pl.pallas_call(
-        functools.partial(pass_kernel, ring, wanted, own),
+        functools.partial(pass_kernel, ring, shifts, own, len(split)),
         out_shape=shapes,
-        in_specs=[VMEM] * (2 * len(work)),
-        out_specs=VMEM if together else [VMEM] * len(work),
+        in_specs=[VMEM] * (len(arrays) + 1 + len(split)),
+        out_specs=[VMEM] * len(shapes),
         compiler_params=pltpu.CompilerParams(vmem_limit_bytes=32 << 20),
-        cost_estimate=pl.CostEstimate(
-            flops=len(work) * own * tok * width, bytes_accessed=len(work) * own * tok * width * 2, transcendentals=0
-        ),
-    )(*arrays, *picks)
+        cost_estimate=pl.CostEstimate(flops=len(arrays) * tok * width, bytes_accessed=tok * width, transcendentals=0),
+    )(*arrays, sibling_picks, *split)
+
+
+def far_kernel(ring, shift, own, *refs):
+    arrays, carried, outs = refs[:own], refs[own], refs[own + 1 :]
+    tok = outs[0].shape[0]
+    owner = ring.owner(lax.axis_index("img"), shift, False)
+    rows = carried[tok:, : 2 * LANES].astype(jnp.float32)
+    rows = jnp.where(lax.broadcasted_iota(jnp.int32, rows.shape, 0) == owner, rows, 0.0)
+    pick = jnp.sum(rows, axis=0, keepdims=True)
+    for i, out in enumerate(outs):
+        images = [image[:tok, :] for image in arrays]
+        out[...] = choose(images, pick[:, i * LANES : (i + 1) * LANES]).astype(out.dtype)
+
+
+def far_stage(ring, shift, images, carried, own, tok, width):
+    return pl.pallas_call(
+        functools.partial(far_kernel, ring, shift, own),
+        out_shape=[jax.ShapeDtypeStruct((tok, width), jnp.bfloat16)] * CORES,
+        in_specs=[VMEM] * (own + 1),
+        out_specs=[VMEM] * CORES,
+        compiler_params=pltpu.CompilerParams(vmem_limit_bytes=32 << 20),
+        cost_estimate=pl.CostEstimate(flops=own * tok * width, bytes_accessed=tok * width, transcendentals=0),
+    )(*images, carried)
 
 
 def shards(columns, tokens, partners, counts, gain_query, gain_memory, w_query, w_key, w_value, w_out):
@@ -323,9 +355,8 @@
     send = lambda array, to: lax.ppermute(array, "img", to)
 
     far = ring.chips // 2
-    assert ring.chips == 2 * far and far > 1 and own == 2
-    up, down, theirs = send(tokens, ahead), send(tokens, back), send(tokens, sibling)
-    meet = lambda array: lax.all_gather(array, "img", axis_index_groups=ring.pairs())
+    assert ring.chips == 2 * far and far > 2 and own == 2
+    up, down, theirs = [send(tokens, ahead)], [send(tokens, back)], send(tokens, sibling)
     operands = (tokens, partners, counts, gain_query, gain_memory, w_query, w_key, w_value, w_out)
     operands = [pltpu.with_memory_space_constraint(array, pltpu.HBM) for array in operands]
     total, spread_q, w_kv, w_out_here, tokens_here, gain_here, picks, table = first_stage(
@@ -333,21 +364,29 @@
     )
     cross = [(source, target ^ 1) for source, target in ahead]
     sibling_picks = send(picks, sibling)
-    next_picks, cross_picks = send(picks, back), send(picks, [(target, source) for source, target in cross])
     state = (spread_q, w_kv, gain_here, picks, table)
-    behind = [((0, True, 1), [theirs])]
+    arrived, behind = None, [((0, True, 1), [theirs])]
     for step in range(1, far):
-        down, total = lax.optimization_barrier((down, total))
-        work = [((step, False, 1), [up]), ((-step, False, 1), [down])]
-        passed = pass_stage(ring, [(step, up, sibling_picks), (-step, down, sibling_picks)], True, **sizes)
+        down[0], total = lax.optimization_barrier((down[0], total))
+        work = [((step, False, len(up)), up), ((-step, False, len(down)), down)] + behind
+        passing = [(step, up), (-step, down)]
+        if step == 1:
+            passed, *singles = pass_stage(ring, passing, sibling_picks, [picks], **sizes)
+            up, down = singles[:own], singles[own:]
+        else:
+            (passed,) = pass_stage(ring, passing, sibling_picks, [], **sizes)
+        if step == 2:
+            carried = down[1]
+        came = send(passed, sibling)
         if step + 1 < far:
-            up, down = send(up, ahead), send(down, back)
+            up, down = [send(image, ahead) for image in up], [send(image, back) for image in down]
         else:
-            same, other = pass_stage(ring, [(step, up, next_picks), (step, up, cross_picks)], False, **sizes)
+            same, other = far_stage(ring, step, up, carried, **sizes)
             same, other = send(same, ahead), send(other, cross)
-        work += behind + [((step, True, 0), []), ((-step, True, 0), [])]
-        (total,) = later_stage(ring, work, meet(passed), state, (), total, **sizes)
-        behind = []
+        (total,) = later_stage(ring, work, arrived, state, (), total, **sizes)
+        arrived = came
+        behind = [((step, True, 0), []), ((-step, True, 0), [])]
+    (total,) = later_stage(ring, behind, arrived, state, (), total, **sizes)
     work = [((far, False, 1), [same]), ((far, True, 1), [other])]
     _, mixed = later_stage(ring, work, None, state, (w_out_here, tokens_here, counts), total, **sizes)
     return mixed

time: 46.7 us -> 45.3 us (0.970)
  starting transfers between devices: 9.63 us -> 18.2 us
  blocking collectives: 8.19 us -> 0 us
  waiting for transfers between devices: 10.6 us -> 8.11 us
  Pallas kernels: 17.8 us -> 18.5 us
    ppermute x12 -> x17, starting transfers between devices: 9.63 us -> 18.2 us  [shards(): send = lambda array, to: lax.ppermute(array, 'img', to)]
    all_gather x3 -> x0, blocking collectives: 8.19 us -> none  [shards(): lax.all_gather(array, 'img', axis_index_groups=ring.pairs())]
    ppermute x12 -> x17, waiting for transfers between devices: 10.6 us -> 8.11 us  [shards(): send = lambda array, to: lax.ppermute(array, 'img', to)]
    pallas_call x4 -> x5, Pallas kernels: 12.8 us -> 13.5 us  [later_stage(): pl.pallas_call(functools.partial(later_kernel, ring, slots, last, own, to...]
  transfers between devices with their start and end apart: 12 -> 17, of which waited for: 5 -> 5; matrix products, arithmetic and copies ran while one was open for 0% -> 0% of each run, Pallas kernels for 31% -> 34%
where the time goes in v6:
time: 45.3 us; the launch traced here: 45.1 us
  Pallas kernels  18.5 us (41%)
  starting transfers between devices  18.2 us (40%)
  waiting for transfers between devices  8.11 us (18%)
    ppermute x17, starting transfers between devices, shards(): send = lambda array, to: lax.ppermute(array, 'img', to)  18.2 us
    pallas_call x5, Pallas kernels, later_stage(): pl.pallas_call(functools.partial(later_kernel, ring, slots, last, own, to...  13.5 us
    ppermute x17, waiting for transfers between devices, shards(): send = lambda array, to: lax.ppermute(array, 'img', to)  8.11 us
    pallas_call x1, Pallas kernels, first_stage(): pl.pallas_call(functools.partial(first_kernel, ring, slots, own, listed,...  4.51 us
  transfers between devices with their start and end apart: 17, of which 5 were waited for; matrix products, arithmetic and copies ran while one was open for 0% of the time, Pallas kernels for 34%

profile of v6, /device:TPU:0, one launch (start us, length us, event | category | flops | bytes accessed | tf_op | source)
XLA Modules:
  0.0 45.1 jit_solution(4537712569094115960)
XLA Ops:
  0.0 3.0 %collective-permute-start.1 = (bf16[2,128,768]{2,1,0:T(8,128)(2,1)}, bf16[2,128,768]{2,1,0:T(8,128)(2,1)S(1)}, u32[]{:S(2)}, u32[]{:S(2)}) collective-permute-start(bf16[2,128,768]{2,1,0:T(8,128)(2,1)} %refs_0_.1), channel_id=1, source_target_pairs={{0,2},{1,5},{4,0},{5,9},{8,4},{9,13},{12,8},{13,15},{14,12},{15,11... | collective-permute-start | bytes 1179656 | tf_op jit(solution)/shard_map/ppermute | solution.py:355
  3.0 0.1 collective-permute-start
  3.0 0.0 collective-permute-start.11
  3.0 4.5 %shard_map.91 = (f32[2,768,128]{2,1,0:T(8,128)S(1)}, bf16[2,768,256]{2,1,0:T(8,128)(2,1)S(1)}, bf16[768,1536]{1,0:T(8,128)(2,1)S(1)}, bf16[768,768]{1,0:T(8,128)...) custom-call(bf16[2,128,768]{2,1,0:T(8,128)(2,1)} %refs_0_.1, ...), custom_call_target="tpu_custom_call" | custom-call | flops 196608 | bytes 196608 | tf_op jit(solution)/shard_map/pallas_call | solution.py:247
  7.6 0.6 %collective-permute-start.2 = (f32[16,128]{1,0:T(8,128)S(1)}, f32[16,128]{1,0:T(8,128)S(1)}, u32[]{:S(2)}, u32[]{:S(2)}) collective-permute-start(f32[16,128]{1,0:T(8,128)S(1)} %get-tuple-element.29.refs_3_.refs_6_.refs_8_.refs_4_.refs_5_), channel_id=1, source_target_pairs={{0,1},{1,0},{2,3},{3,2},{4,5},{5,4},{6,7},{7,6},{8,9},{9,8},{10,11... | collective-permute-start | bytes 24584 | tf_op jit(solution)/shard_map/ppermute | solution.py:355
  8.1 4.5 %collective-permute-done.1.refs_1_ = bf16[2,128,768]{2,1,0:T(8,128)(2,1)S(1)} collective-permute-done((bf16[2,128,768]{2,1,0:T(8,128)(2,1)}, bf16[2,128,768]{2,1,0:T(8,128)(2,1)S(1)}, u32[]{:S(2)}, u32[]{:S(2)}) %collective-permute-start.1) | collective-permute-done | bytes 393248 | tf_op jit(solution)/shard_map/ppermute | solution.py:355
  12.6 0.0 collective-permute-done.2.refs_2_.refs_4_
  12.7 0.0 collective-permute-done.refs_0_
  12.7 0.1 shard_map.92
  12.8 1.5 %collective-permute-start.7 = (bf16[144,768]{1,0:T(8,128)(2,1)S(1)}, bf16[144,768]{1,0:T(8,128)(2,1)S(1)}, u32[]{:S(2)}, u32[]{:S(2)}) collective-permute-start(bf16[144,768]{1,0:T(8,128)(2,1)S(1)} %get-tuple-element.32), channel_id=1, source_target_pairs={{0,2},{1,5},{4,0},{5,9},{8,4},{9,13},{12,8},{13,15},{14,12},{15,11... | collective-permute-start | bytes 663560 | tf_op jit(solution)/shard_map/ppermute | solution.py:355
  14.3 1.7 %collective-permute-start.10 = (bf16[128,768]{1,0:T(8,128)(2,1)S(1)}, bf16[128,768]{1,0:T(8,128)(2,1)S(1)}, u32[]{:S(2)}, u32[]{:S(2)}) collective-permute-start(bf16[128,768]{1,0:T(8,128)(2,1)S(1)} %get-tuple-element.39), channel_id=1, source_target_pairs={{0,2},{1,5},{4,0},{5,9},{8,4},{9,13},{12,8},{13,15},{14,12},{15,11... | collective-permute-start | bytes 589832 | tf_op jit(solution)/shard_map/ppermute | solution.py:355
  16.0 0.4 collective-permute-start.13
  16.4 1.6 %collective-permute-start.3 = (bf16[128,768]{1,0:T(8,128)(2,1)S(1)}, bf16[128,768]{1,0:T(8,128)(2,1)S(1)}, u32[]{:S(2)}, u32[]{:S(2)}) collective-permute-start(bf16[128,768]{1,0:T(8,128)(2,1)S(1)} %get-tuple-element.30), channel_id=1, source_target_pairs={{0,4},{1,3},{4,8},{5,1},{8,12},{9,5},{12,14},{13,9},{14,10},{15,13... | collective-permute-start | bytes 589832 | tf_op jit(solution)/shard_map/ppermute | solution.py:355
  18.0 0.0 collective-permute-done.11.refs_2_
  18.0 0.3 collective-permute-start.5
  18.4 0.8 %collective-permute-done.7.refs_2_.refs_3_ = bf16[144,768]{1,0:T(8,128)(2,1)S(1)} collective-permute-done((bf16[144,768]{1,0:T(8,128)(2,1)S(1)}, bf16[144,768]{1,0:T(8,128)(2,1)S(1)}, u32[]{:S(2)}, u32[]{:S(2)}) %collective-permute-start.7) | collective-permute-done | bytes 221216 | tf_op jit(solution)/shard_map/ppermute | solution.py:355
  19.2 1.1 %collective-permute-start.14 = (bf16[144,768]{1,0:T(8,128)(2,1)S(1)}, bf16[144,768]{1,0:T(8,128)(2,1)S(1)}, u32[]{:S(2)}, u32[]{:S(2)}) collective-permute-start(bf16[144,768]{1,0:T(8,128)(2,1)S(1)} %collective-permute-done.7.refs_2_.refs_3_), channel_id=1, source_target_pairs={{0,2},{1,5},{4,0},{5,9},{8,4},{9,13},{12,8},{13,15},{14,12},{15,11... | collective-permute-start | bytes 663560 | tf_op jit(solution)/shard_map/ppermute | solution.py:355
  20.3 2.5 %shard_map.94.refs_10_ = f32[2,768,128]{2,1,0:T(8,128)S(1)} custom-call(bf16[2,128,768]{2,1,0:T(8,128)(2,1)S(1)} %collective-permute-done.refs_0_, bf16[2,128,768]{2,1,0:T(8,128)(2,1)S(1)} %collective-permute-done.1.refs_1_, bf16[2,128,768]{2,1,0:T(8,128)(2,1)S(1)} %collective-permute-done.11.refs_2_, ...), custom_call_target="tpu_custom_call", output_to_operand_aliasing={{}: (8, {})} | custom-call | flops 294912 | bytes 294912 | tf_op jit(solution)/shard_map/pallas_call | solution.py:274
  22.7 0.7 %collective-permute-done.10.refs_2_ = bf16[128,768]{1,0:T(8,128)(2,1)S(1)} collective-permute-done((bf16[128,768]{1,0:T(8,128)(2,1)S(1)}, bf16[128,768]{1,0:T(8,128)(2,1)S(1)}, u32[]{:S(2)}, u32[]{:S(2)}) %collective-permute-start.10) | collective-permute-done | bytes 196640 | tf_op jit(solution)/shard_map/ppermute | solution.py:355
  23.4 1.0 %collective-permute-start.12 = (bf16[128,768]{1,0:T(8,128)(2,1)S(1)}, bf16[128,768]{1,0:T(8,128)(2,1)S(1)}, u32[]{:S(2)}, u32[]{:S(2)}) collective-permute-start(bf16[128,768]{1,0:T(8,128)(2,1)S(1)} %collective-permute-done.10.refs_2_), channel_id=1, source_target_pairs={{0,2},{1,5},{4,0},{5,9},{8,4},{9,13},{12,8},{13,15},{14,12},{15,11... | collective-permute-start | bytes 589832 | tf_op jit(solution)/shard_map/ppermute | solution.py:355
  24.4 0.0 collective-permute-done.3.refs_0_
  24.4 1.5 %collective-permute-start.4 = (bf16[128,768]{1,0:T(8,128)(2,1)S(1)}, bf16[128,768]{1,0:T(8,128)(2,1)S(1)}, u32[]{:S(2)}, u32[]{:S(2)}) collective-permute-start(bf16[128,768]{1,0:T(8,128)(2,1)S(1)} %collective-permute-done.3.refs_0_), channel_id=1, source_target_pairs={{0,4},{1,3},{4,8},{5,1},{8,12},{9,5},{12,14},{13,9},{14,10},{15,13... | collective-permute-start | bytes 589832 | tf_op jit(solution)/shard_map/ppermute | solution.py:355
  25.9 1.7 %collective-permute-done.5.refs_1_ = bf16[128,768]{1,0:T(8,128)(2,1)S(1)} collective-permute-done((bf16[128,768]{1,0:T(8,128)(2,1)S(1)}, bf16[128,768]{1,0:T(8,128)(2,1)S(1)}, u32[]{:S(2)}, u32[]{:S(2)}) %collective-permute-start.5) | collective-permute-done | bytes 196640 | tf_op jit(solution)/shard_map/ppermute | solution.py:355
  27.6 2.5 %collective-permute-start.6 = (bf16[128,768]{1,0:T(8,128)(2,1)S(1)}, bf16[128,768]{1,0:T(8,128)(2,1)S(1)}, u32[]{:S(2)}, u32[]{:S(2)}) collective-permute-start(bf16[128,768]{1,0:T(8,128)(2,1)S(1)} %collective-permute-done.5.refs_1_), channel_id=1, source_target_pairs={{0,4},{1,3},{4,8},{5,1},{8,12},{9,5},{12,14},{13,9},{14,10},{15,13... | collective-permute-start | bytes 589832 | tf_op jit(solution)/shard_map/ppermute | solution.py:355
  30.1 0.1 shard_map.97
  30.2 0.0 collective-permute-done.13.refs_4_
  30.2 0.1 collective-permute-start.16
  30.3 3.1 %shard_map.95.refs_10_ = f32[2,768,128]{2,1,0:T(8,128)S(1)} custom-call(bf16[128,768]{1,0:T(8,128)(2,1)S(1)} %collective-permute-done.3.refs_0_, bf16[128,768]{1,0:T(8,128)(2,1)S(1)} %collective-permute-done.5.refs_1_, bf16[128,768]{1,0:T(8,128)(2,1)S(1)} %collective-permute-done.10.refs_2_, ...), custom_call_target="tpu_custom_call", output_to_operand_aliasing={{}: (10, {})} | custom-call | flops 393216 | bytes 393216 | tf_op jit(solution)/shard_map/pallas_call | solution.py:274
  33.4 0.0 collective-permute-done.12.refs_2_
  33.4 0.0 collective-permute-done.4.refs_0_
  33.4 0.0 collective-permute-done.6.refs_1_
  33.4 0.0 collective-permute-done.14.refs_3_
  33.4 0.1 shard_map.96
  33.5 0.7 %collective-permute-start.15 = (bf16[2,128,768]{2,1,0:T(8,128)(2,1)S(1)}, bf16[2,128,768]{2,1,0:T(8,128)(2,1)S(1)}, u32[]{:S(2)}, u32[]{:S(2)}) collective-permute-start(bf16[2,128,768]{2,1,0:T(8,128)(2,1)S(1)} %shard_map.96), channel_id=1, source_target_pairs={{0,1},{1,0},{2,3},{3,2},{4,5},{5,4},{6,7},{7,6},{8,9},{9,8},{10,11... | collective-permute-start | bytes 1179656 | tf_op jit(solution)/shard_map/ppermute | solution.py:355
  34.2 0.1 shard_map.93
  34.3 2.3 %collective-permute-start.8 = (bf16[128,768]{1,0:T(8,128)(2,1)S(1)}, bf16[128,768]{1,0:T(8,128)(2,1)S(1)}, u32[]{:S(2)}, u32[]{:S(2)}) collective-permute-start(bf16[128,768]{1,0:T(8,128)(2,1)S(1)} %get-tuple-element.33), channel_id=1, source_target_pairs={{0,4},{1,3},{4,8},{5,1},{8,12},{9,5},{12,14},{13,9},{14,10},{15,13... | collective-permute-start | bytes 589832 | tf_op jit(solution)/shard_map/ppermute | solution.py:355
  36.6 0.0 collective-permute-start.9
  36.6 0.0 collective-permute-done.16.refs_4_
  36.6 3.1 %shard_map.98.refs_6_ = f32[2,768,128]{2,1,0:T(8,128)S(1)} custom-call(bf16[128,768]{1,0:T(8,128)(2,1)S(1)} %collective-permute-done.4.refs_0_, bf16[128,768]{1,0:T(8,128)(2,1)S(1)} %collective-permute-done.6.refs_1_, bf16[128,768]{1,0:T(8,128)(2,1)S(1)} %collective-permute-done.12.refs_2_, ...), custom_call_target="tpu_custom_call", output_to_operand_aliasing={{}: (10, {})} | custom-call | flops 393216 | bytes 393216 | tf_op jit(solution)/shard_map/pallas_call | solution.py:274
  39.7 0.0 copy-start
  39.7 0.0 collective-permute-done.15.refs_0_
  39.7 1.8 %shard_map.99.refs_7_ = f32[2,768,128]{2,1,0:T(8,128)S(1)} custom-call(bf16[2,128,768]{2,1,0:T(8,128)(2,1)S(1)} %collective-permute-done.15.refs_0_, bf16[2,768,256]{2,1,0:T(8,128)(2,1)S(1)} %get-tuple-element.35.refs_3_.refs_5_.refs_1_.refs_2_, ...), custom_call_target="tpu_custom_call", output_to_operand_aliasing={{}: (6, {})} | custom-call | flops 196608 | bytes 196608 | tf_op jit(solution)/shard_map/pallas_call | solution.py:274
  41.5 0.0 collective-permute-done.8.refs_0_
  41.5 0.4 collective-permute-done.9.refs_1_
  41.9 0.0 copy-done
  41.9 3.1 %shard_map.100 = (f32[2,768,128]{2,1,0:T(8,128)S(1)}, bf16[2,128,768]{2,1,0:T(8,128)(2,1)}) custom-call(bf16[128,768]{1,0:T(8,128)(2,1)S(1)} %collective-permute-done.8.refs_0_, bf16[128,768]{1,0:T(8,128)(2,1)S(1)} %collective-permute-done.9.refs_1_, ...), custom_call_target="tpu_custom_call", output_to_operand_aliasing={{0}: (7, {})} | custom-call | flops 196608 | bytes 196608 | tf_op jit(solution)/shard_map/pallas_call | solution.py:274
Async XLA Ops:
  0.0 12.6 %collective-permute-start.1 = (bf16[2,128,768]{2,1,0:T(8,128)(2,1)}, bf16[2,128,768]{2,1,0:T(8,128)(2,1)S(1)}, u32[]{:S(2)}, u32[]{:S(2)}) collective-permute-start(bf16[2,128,768]{2,1,0:T(8,128)(2,1)} %refs_0_.1), channel_id=1, source_target_pairs={{0,2},{1,5},{4,0},{5,9},{8,4},{9,13},{12,8},{13,15},{14,12},{15,11... | collective-permute-start | bytes 1179656 | tf_op jit(solution)/shard_map/ppermute | solution.py:355
  3.0 9.7 %collective-permute-start = (bf16[2,128,768]{2,1,0:T(8,128)(2,1)}, bf16[2,128,768]{2,1,0:T(8,128)(2,1)S(1)}, u32[]{:S(2)}, u32[]{:S(2)}) collective-permute-start(bf16[2,128,768]{2,1,0:T(8,128)(2,1)} %refs_0_.1), channel_id=1, source_target_pairs={{0,4},{1,3},{4,8},{5,1},{8,12},{9,5},{12,14},{13,9},{14,10},{15,13... | collective-permute-start | bytes 1179656 | tf_op jit(solution)/shard_map/ppermute | solution.py:355
  3.0 15.0 %collective-permute-start.11 = (bf16[2,128,768]{2,1,0:T(8,128)(2,1)}, bf16[2,128,768]{2,1,0:T(8,128)(2,1)S(1)}, u32[]{:S(2)}, u32[]{:S(2)}) collective-permute-start(bf16[2,128,768]{2,1,0:T(8,128)(2,1)} %refs_0_.1), channel_id=1, source_target_pairs={{0,1},{1,0},{2,3},{3,2},{4,5},{5,4},{6,7},{7,6},{8,9},{9,8},{10,11... | collective-permute-start | bytes 1179656 | tf_op jit(solution)/shard_map/ppermute | solution.py:355
  7.6 5.1 %collective-permute-start.2 = (f32[16,128]{1,0:T(8,128)S(1)}, f32[16,128]{1,0:T(8,128)S(1)}, u32[]{:S(2)}, u32[]{:S(2)}) collective-permute-start(f32[16,128]{1,0:T(8,128)S(1)} %get-tuple-element.29.refs_3_.refs_6_.refs_8_.refs_4_.refs_5_), channel_id=1, source_target_pairs={{0,1},{1,0},{2,3},{3,2},{4,5},{5,4},{6,7},{7,6},{8,9},{9,8},{10,11... | collective-permute-start | bytes 24584 | tf_op jit(solution)/shard_map/ppermute | solution.py:355
  12.8 6.4 %collective-permute-start.7 = (bf16[144,768]{1,0:T(8,128)(2,1)S(1)}, bf16[144,768]{1,0:T(8,128)(2,1)S(1)}, u32[]{:S(2)}, u32[]{:S(2)}) collective-permute-start(bf16[144,768]{1,0:T(8,128)(2,1)S(1)} %get-tuple-element.32), channel_id=1, source_target_pairs={{0,2},{1,5},{4,0},{5,9},{8,4},{9,13},{12,8},{13,15},{14,12},{15,11... | collective-permute-start | bytes 663560 | tf_op jit(solution)/shard_map/ppermute | solution.py:355
  14.3 9.1 %collective-permute-start.10 = (bf16[128,768]{1,0:T(8,128)(2,1)S(1)}, bf16[128,768]{1,0:T(8,128)(2,1)S(1)}, u32[]{:S(2)}, u32[]{:S(2)}) collective-permute-start(bf16[128,768]{1,0:T(8,128)(2,1)S(1)} %get-tuple-element.39), channel_id=1, source_target_pairs={{0,2},{1,5},{4,0},{5,9},{8,4},{9,13},{12,8},{13,15},{14,12},{15,11... | collective-permute-start | bytes 589832 | tf_op jit(solution)/shard_map/ppermute | solution.py:355
  16.0 14.2 %collective-permute-start.13 = (bf16[2,128,768]{2,1,0:T(8,128)(2,1)S(1)}, bf16[2,128,768]{2,1,0:T(8,128)(2,1)S(1)}, u32[]{:S(2)}, u32[]{:S(2)}) collective-permute-start(bf16[2,128,768]{2,1,0:T(8,128)(2,1)S(1)} %get-tuple-element.42), channel_id=1, source_target_pairs={{0,1},{1,0},{2,3},{3,2},{4,5},{5,4},{6,7},{7,6},{8,9},{9,8},{10,11... | collective-permute-start | bytes 1179656 | tf_op jit(solution)/shard_map/ppermute | solution.py:355
  16.4 8.1 %collective-permute-start.3 = (bf16[128,768]{1,0:T(8,128)(2,1)S(1)}, bf16[128,768]{1,0:T(8,128)(2,1)S(1)}, u32[]{:S(2)}, u32[]{:S(2)}) collective-permute-start(bf16[128,768]{1,0:T(8,128)(2,1)S(1)} %get-tuple-element.30), channel_id=1, source_target_pairs={{0,4},{1,3},{4,8},{5,1},{8,12},{9,5},{12,14},{13,9},{14,10},{15,13... | collective-permute-start | bytes 589832 | tf_op jit(solution)/shard_map/ppermute | solution.py:355
  18.0 9.6 %collective-permute-start.5 = (bf16[128,768]{1,0:T(8,128)(2,1)S(1)}, bf16[128,768]{1,0:T(8,128)(2,1)S(1)}, u32[]{:S(2)}, u32[]{:S(2)}) collective-permute-start(bf16[128,768]{1,0:T(8,128)(2,1)S(1)} %get-tuple-element.31), channel_id=1, source_target_pairs={{0,4},{1,3},{4,8},{5,1},{8,12},{9,5},{12,14},{13,9},{14,10},{15,13... | collective-permute-start | bytes 589832 | tf_op jit(solution)/shard_map/ppermute | solution.py:355
  19.2 14.2 %collective-permute-start.14 = (bf16[144,768]{1,0:T(8,128)(2,1)S(1)}, bf16[144,768]{1,0:T(8,128)(2,1)S(1)}, u32[]{:S(2)}, u32[]{:S(2)}) collective-permute-start(bf16[144,768]{1,0:T(8,128)(2,1)S(1)} %collective-permute-done.7.refs_2_.refs_3_), channel_id=1, source_target_pairs={{0,2},{1,5},{4,0},{5,9},{8,4},{9,13},{12,8},{13,15},{14,12},{15,11... | collective-permute-start | bytes 663560 | tf_op jit(solution)/shard_map/ppermute | solution.py:355
  23.4 9.9 %collective-permute-start.12 = (bf16[128,768]{1,0:T(8,128)(2,1)S(1)}, bf16[128,768]{1,0:T(8,128)(2,1)S(1)}, u32[]{:S(2)}, u32[]{:S(2)}) collective-permute-start(bf16[128,768]{1,0:T(8,128)(2,1)S(1)} %collective-permute-done.10.refs_2_), channel_id=1, source_target_pairs={{0,2},{1,5},{4,0},{5,9},{8,4},{9,13},{12,8},{13,15},{14,12},{15,11... | collective-permute-start | bytes 589832 | tf_op jit(solution)/shard_map/ppermute | solution.py:355
  24.4 8.9 %collective-permute-start.4 = (bf16[128,768]{1,0:T(8,128)(2,1)S(1)}, bf16[128,768]{1,0:T(8,128)(2,1)S(1)}, u32[]{:S(2)}, u32[]{:S(2)}) collective-permute-start(bf16[128,768]{1,0:T(8,128)(2,1)S(1)} %collective-permute-done.3.refs_0_), channel_id=1, source_target_pairs={{0,4},{1,3},{4,8},{5,1},{8,12},{9,5},{12,14},{13,9},{14,10},{15,13... | collective-permute-start | bytes 589832 | tf_op jit(solution)/shard_map/ppermute | solution.py:355
  27.6 5.8 %collective-permute-start.6 = (bf16[128,768]{1,0:T(8,128)(2,1)S(1)}, bf16[128,768]{1,0:T(8,128)(2,1)S(1)}, u32[]{:S(2)}, u32[]{:S(2)}) collective-permute-start(bf16[128,768]{1,0:T(8,128)(2,1)S(1)} %collective-permute-done.5.refs_1_), channel_id=1, source_target_pairs={{0,4},{1,3},{4,8},{5,1},{8,12},{9,5},{12,14},{13,9},{14,10},{15,13... | collective-permute-start | bytes 589832 | tf_op jit(solution)/shard_map/ppermute | solution.py:355
  30.2 6.4 %collective-permute-start.16 = (bf16[2,128,768]{2,1,0:T(8,128)(2,1)S(1)}, bf16[2,128,768]{2,1,0:T(8,128)(2,1)S(1)}, u32[]{:S(2)}, u32[]{:S(2)}) collective-permute-start(bf16[2,128,768]{2,1,0:T(8,128)(2,1)S(1)} %shard_map.97), channel_id=1, source_target_pairs={{0,1},{1,0},{2,3},{3,2},{4,5},{5,4},{6,7},{7,6},{8,9},{9,8},{10,11... | collective-permute-start | bytes 1179656 | tf_op jit(solution)/shard_map/ppermute | solution.py:355
  33.5 6.1 %collective-permute-start.15 = (bf16[2,128,768]{2,1,0:T(8,128)(2,1)S(1)}, bf16[2,128,768]{2,1,0:T(8,128)(2,1)S(1)}, u32[]{:S(2)}, u32[]{:S(2)}) collective-permute-start(bf16[2,128,768]{2,1,0:T(8,128)(2,1)S(1)} %shard_map.96), channel_id=1, source_target_pairs={{0,1},{1,0},{2,3},{3,2},{4,5},{5,4},{6,7},{7,6},{8,9},{9,8},{10,11... | collective-permute-start | bytes 1179656 | tf_op jit(solution)/shard_map/ppermute | solution.py:355
  34.3 7.2 %collective-permute-start.8 = (bf16[128,768]{1,0:T(8,128)(2,1)S(1)}, bf16[128,768]{1,0:T(8,128)(2,1)S(1)}, u32[]{:S(2)}, u32[]{:S(2)}) collective-permute-start(bf16[128,768]{1,0:T(8,128)(2,1)S(1)} %get-tuple-element.33), channel_id=1, source_target_pairs={{0,4},{1,3},{4,8},{5,1},{8,12},{9,5},{12,14},{13,9},{14,10},{15,13... | collective-permute-start | bytes 589832 | tf_op jit(solution)/shard_map/ppermute | solution.py:355
  36.6 5.3 %collective-permute-start.9 = (bf16[128,768]{1,0:T(8,128)(2,1)S(1)}, bf16[128,768]{1,0:T(8,128)(2,1)S(1)}, u32[]{:S(2)}, u32[]{:S(2)}) collective-permute-start(bf16[128,768]{1,0:T(8,128)(2,1)S(1)} %get-tuple-element.34), channel_id=1, source_target_pairs={{0,5},{1,2},{4,9},{5,0},{8,13},{9,4},{12,15},{13,8},{14,11},{15,12... | collective-permute-start | bytes 589832 | tf_op jit(solution)/shard_map/ppermute | solution.py:355
  39.7 2.2 %copy-start = (s32[2]{0:T(128)S(1)}, s32[2]{0:T(128)}, u32[]{:S(2)}) copy-start(s32[2]{0:T(128)} %refs_10_.1) | copy-start | bytes 28

commit v7 on v6

--- a/solution.py
+++ b/solution.py
@@ -171,7 +171,7 @@
     take = lambda n: [refs.pop(0) for _ in range(n)]
     sources = [take(n) for _, _, n in slots]
     (arrived,) = take(1) if any(n == 0 for _, _, n in slots) else (None,)
-    spread_q, w_kv, gain, picks, table, _ = take(6)
+    spread_q, w_kv, gain, picks, table, total_in = take(6)
     if last:
         w_out, tokens, counts, total, mixed, mixed_here, counts_here, table_here, sems = refs
     else:
@@ -181,6 +181,7 @@
         copies.append(pltpu.make_async_copy(counts, counts_here, sems.at[1]))
     for copy in copies:
         copy.start()
+    total[...] = total_in[...]
     me = lax.axis_index("img")
     owners = [ring.owner(me, shift, flip) for shift, flip, _ in slots]
     chosen = []
@@ -367,7 +368,7 @@
     state = (spread_q, w_kv, gain_here, picks, table)
     arrived, behind = None, [((0, True, 1), [theirs])]
     for step in range(1, far):
-        down[0], total = lax.optimization_barrier((down[0], total))
+        up[0], down[0], total = lax.optimization_barrier((up[0], down[0], total))
         work = [((step, False, len(up)), up), ((-step, False, len(down)), down)] + behind
         passing = [(step, up), (-step, down)]
         if step == 1:

time: 45.3 us -> 44.9 us (level)
  starting transfers between devices: 18.2 us -> 16.1 us
  waiting for transfers between devices: 8.11 us -> 9.5 us
    ppermute x17, starting transfers between devices: 18.2 us -> 16.1 us  [shards(): send = lambda array, to: lax.ppermute(array, 'img', to)]
    ppermute x17, waiting for transfers between devices: 8.11 us -> 9.5 us  [shards(): send = lambda array, to: lax.ppermute(array, 'img', to)]
  transfers between devices with their start and end apart: 17 -> 17, of which waited for: 5 -> 5; matrix products, arithmetic and copies ran while one was open for 0% -> 0% of each run, Pallas kernels for 34% -> 35%
where the time goes in v7:
time: 44.9 us; the launch traced here: 44.7 us
  Pallas kernels  18.9 us (42%)
  starting transfers between devices  16.1 us (36%)
  waiting for transfers between devices  9.5 us (21%)
    ppermute x17, starting transfers between devices, shards(): send = lambda array, to: lax.ppermute(array, 'img', to)  16.1 us
    pallas_call x5, Pallas kernels, later_stage(): pl.pallas_call(functools.partial(later_kernel, ring, slots, last, own, to...  13.8 us
    ppermute x17, waiting for transfers between devices, shards(): send = lambda array, to: lax.ppermute(array, 'img', to)  9.5 us
    pallas_call x1, Pallas kernels, first_stage(): pl.pallas_call(functools.partial(first_kernel, ring, slots, own, listed,...  4.52 us
  transfers between devices with their start and end apart: 17, of which 5 were waited for; matrix products, arithmetic and copies ran while one was open for 0% of the time, Pallas kernels for 35%

profile of v7, /device:TPU:0, one launch (start us, length us, event | category | flops | bytes accessed | tf_op | source)
XLA Modules:
  0.0 44.7 jit_solution(12544500251631684701)
XLA Ops:
  0.0 3.0 %collective-permute-start = (bf16[2,128,768]{2,1,0:T(8,128)(2,1)}, bf16[2,128,768]{2,1,0:T(8,128)(2,1)S(1)}, u32[]{:S(2)}, u32[]{:S(2)}) collective-permute-start(bf16[2,128,768]{2,1,0:T(8,128)(2,1)} %refs_0_.1), channel_id=1, source_target_pairs={{0,4},{1,3},{4,8},{5,1},{8,12},{9,5},{12,14},{13,9},{14,10},{15,13... | collective-permute-start | bytes 1179656 | tf_op jit(solution)/shard_map/ppermute | solution.py:356
  3.0 0.0 collective-permute-start.1
  3.0 0.0 collective-permute-start.5
  3.0 4.5 %shard_map.91 = (f32[2,768,128]{2,1,0:T(8,128)S(1)}, bf16[2,768,256]{2,1,0:T(8,128)(2,1)S(1)}, bf16[768,1536]{1,0:T(8,128)(2,1)S(1)}, bf16[768,768]{1,0:T(8,128)...) custom-call(bf16[2,128,768]{2,1,0:T(8,128)(2,1)} %refs_0_.1, ...), custom_call_target="tpu_custom_call" | custom-call | flops 196608 | bytes 196608 | tf_op jit(solution)/shard_map/pallas_call | solution.py:248
  7.6 0.6 %collective-permute-start.2 = (f32[16,128]{1,0:T(8,128)S(1)}, f32[16,128]{1,0:T(8,128)S(1)}, u32[]{:S(2)}, u32[]{:S(2)}) collective-permute-start(f32[16,128]{1,0:T(8,128)S(1)} %get-tuple-element.33.refs_3_.refs_6_.refs_8_.refs_4_.refs_5_), channel_id=1, source_target_pairs={{0,1},{1,0},{2,3},{3,2},{4,5},{5,4},{6,7},{7,6},{8,9},{9,8},{10,11... | collective-permute-start | bytes 24584 | tf_op jit(solution)/shard_map/ppermute | solution.py:356
  8.1 4.5 %collective-permute-done.refs_0_ = bf16[2,128,768]{2,1,0:T(8,128)(2,1)S(1)} collective-permute-done((bf16[2,128,768]{2,1,0:T(8,128)(2,1)}, bf16[2,128,768]{2,1,0:T(8,128)(2,1)S(1)}, u32[]{:S(2)}, u32[]{:S(2)}) %collective-permute-start) | collective-permute-done | bytes 393248 | tf_op jit(solution)/shard_map/ppermute | solution.py:356
  12.6 0.0 collective-permute-done.1.refs_1_
  12.6 0.0 collective-permute-done.2.refs_2_.refs_4_
  12.6 0.1 shard_map.92
  12.7 2.5 %collective-permute-start.9 = (bf16[144,768]{1,0:T(8,128)(2,1)S(1)}, bf16[144,768]{1,0:T(8,128)(2,1)S(1)}, u32[]{:S(2)}, u32[]{:S(2)}) collective-permute-start(bf16[144,768]{1,0:T(8,128)(2,1)S(1)} %get-tuple-element.44), channel_id=1, source_target_pairs={{0,2},{1,5},{4,0},{5,9},{8,4},{9,13},{12,8},{13,15},{14,12},{15,11... | collective-permute-start | bytes 663560 | tf_op jit(solution)/shard_map/ppermute | solution.py:356
  15.2 0.0 collective-permute-start.3
  15.2 2.0 %collective-permute-start.4 = (bf16[128,768]{1,0:T(8,128)(2,1)S(1)}, bf16[128,768]{1,0:T(8,128)(2,1)S(1)}, u32[]{:S(2)}, u32[]{:S(2)}) collective-permute-start(bf16[128,768]{1,0:T(8,128)(2,1)S(1)} %get-tuple-element.35), channel_id=1, source_target_pairs={{0,2},{1,5},{4,0},{5,9},{8,4},{9,13},{12,8},{13,15},{14,12},{15,11... | collective-permute-start | bytes 589832 | tf_op jit(solution)/shard_map/ppermute | solution.py:356
  17.2 0.0 collective-permute-start.10
  17.2 0.0 collective-permute-done.5.refs_2_
  17.2 0.0 collective-permute-start.8
  17.3 3.2 %collective-permute-done.9.refs_3_.refs_2_ = bf16[144,768]{1,0:T(8,128)(2,1)S(1)} collective-permute-done((bf16[144,768]{1,0:T(8,128)(2,1)S(1)}, bf16[144,768]{1,0:T(8,128)(2,1)S(1)}, u32[]{:S(2)}, u32[]{:S(2)}) %collective-permute-start.9) | collective-permute-done | bytes 221216 | tf_op jit(solution)/shard_map/ppermute | solution.py:356
  20.4 2.5 %collective-permute-start.14 = (bf16[144,768]{1,0:T(8,128)(2,1)S(1)}, bf16[144,768]{1,0:T(8,128)(2,1)S(1)}, u32[]{:S(2)}, u32[]{:S(2)}) collective-permute-start(bf16[144,768]{1,0:T(8,128)(2,1)S(1)} %collective-permute-done.9.refs_3_.refs_2_), channel_id=1, source_target_pairs={{0,2},{1,5},{4,0},{5,9},{8,4},{9,13},{12,8},{13,15},{14,12},{15,11... | collective-permute-start | bytes 663560 | tf_op jit(solution)/shard_map/ppermute | solution.py:356
  22.9 2.5 %shard_map.93.refs_10_ = f32[2,768,128]{2,1,0:T(8,128)S(1)} custom-call(bf16[2,128,768]{2,1,0:T(8,128)(2,1)S(1)} %collective-permute-done.refs_0_, bf16[2,128,768]{2,1,0:T(8,128)(2,1)S(1)} %collective-permute-done.1.refs_1_, bf16[2,128,768]{2,1,0:T(8,128)(2,1)S(1)} %collective-permute-done.5.refs_2_, ...), custom_call_target="tpu_custom_call", output_to_operand_aliasing={{}: (8, {})} | custom-call | flops 294912 | bytes 294912 | tf_op jit(solution)/shard_map/pallas_call | solution.py:275
  25.5 0.0 collective-permute-done.3.refs_0_
  25.5 0.0 collective-permute-done.4.refs_2_
  25.5 1.2 %collective-permute-start.6 = (bf16[128,768]{1,0:T(8,128)(2,1)S(1)}, bf16[128,768]{1,0:T(8,128)(2,1)S(1)}, u32[]{:S(2)}, u32[]{:S(2)}) collective-permute-start(bf16[128,768]{1,0:T(8,128)(2,1)S(1)} %collective-permute-done.3.refs_0_), channel_id=1, source_target_pairs={{0,4},{1,3},{4,8},{5,1},{8,12},{9,5},{12,14},{13,9},{14,10},{15,13... | collective-permute-start | bytes 589832 | tf_op jit(solution)/shard_map/ppermute | solution.py:356
  26.7 0.8 %collective-permute-start.7 = (bf16[128,768]{1,0:T(8,128)(2,1)S(1)}, bf16[128,768]{1,0:T(8,128)(2,1)S(1)}, u32[]{:S(2)}, u32[]{:S(2)}) collective-permute-start(bf16[128,768]{1,0:T(8,128)(2,1)S(1)} %collective-permute-done.4.refs_2_), channel_id=1, source_target_pairs={{0,2},{1,5},{4,0},{5,9},{8,4},{9,13},{12,8},{13,15},{14,12},{15,11... | collective-permute-start | bytes 589832 | tf_op jit(solution)/shard_map/ppermute | solution.py:356
  27.6 0.0 collective-permute-done.8.refs_1_
  27.6 1.2 %collective-permute-start.11 = (bf16[128,768]{1,0:T(8,128)(2,1)S(1)}, bf16[128,768]{1,0:T(8,128)(2,1)S(1)}, u32[]{:S(2)}, u32[]{:S(2)}) collective-permute-start(bf16[128,768]{1,0:T(8,128)(2,1)S(1)} %collective-permute-done.8.refs_1_), channel_id=1, source_target_pairs={{0,4},{1,3},{4,8},{5,1},{8,12},{9,5},{12,14},{13,9},{14,10},{15,13... | collective-permute-start | bytes 589832 | tf_op jit(solution)/shard_map/ppermute | solution.py:356
  28.8 0.1 shard_map.97
  28.9 0.0 collective-permute-done.10.refs_4_
  28.9 0.1 collective-permute-start.16
  29.0 3.1 %shard_map.94.refs_10_ = f32[2,768,128]{2,1,0:T(8,128)S(1)} custom-call(bf16[128,768]{1,0:T(8,128)(2,1)S(1)} %collective-permute-done.3.refs_0_, bf16[128,768]{1,0:T(8,128)(2,1)S(1)} %collective-permute-done.8.refs_1_, bf16[128,768]{1,0:T(8,128)(2,1)S(1)} %collective-permute-done.4.refs_2_, ...), custom_call_target="tpu_custom_call", output_to_operand_aliasing={{}: (10, {})} | custom-call | flops 393216 | bytes 393216 | tf_op jit(solution)/shard_map/pallas_call | solution.py:275
  32.1 0.0 collective-permute-done.6.refs_0_
  32.1 1.1 %collective-permute-done.7.refs_2_ = bf16[128,768]{1,0:T(8,128)(2,1)S(1)} collective-permute-done((bf16[128,768]{1,0:T(8,128)(2,1)S(1)}, bf16[128,768]{1,0:T(8,128)(2,1)S(1)}, u32[]{:S(2)}, u32[]{:S(2)}) %collective-permute-start.7) | collective-permute-done | bytes 196640 | tf_op jit(solution)/shard_map/ppermute | solution.py:356
  33.2 0.3 collective-permute-done.11.refs_1_
  33.6 0.0 collective-permute-done.14.refs_3_
  33.6 0.1 shard_map.96
  33.7 0.1 collective-permute-start.15
  33.8 0.1 shard_map.95
  33.9 1.6 %collective-permute-start.12 = (bf16[128,768]{1,0:T(8,128)(2,1)S(1)}, bf16[128,768]{1,0:T(8,128)(2,1)S(1)}, u32[]{:S(2)}, u32[]{:S(2)}) collective-permute-start(bf16[128,768]{1,0:T(8,128)(2,1)S(1)} %get-tuple-element.48), channel_id=1, source_target_pairs={{0,4},{1,3},{4,8},{5,1},{8,12},{9,5},{12,14},{13,9},{14,10},{15,13... | collective-permute-start | bytes 589832 | tf_op jit(solution)/shard_map/ppermute | solution.py:356
  35.5 0.5 %collective-permute-start.13 = (bf16[128,768]{1,0:T(8,128)(2,1)S(1)}, bf16[128,768]{1,0:T(8,128)(2,1)S(1)}, u32[]{:S(2)}, u32[]{:S(2)}) collective-permute-start(bf16[128,768]{1,0:T(8,128)(2,1)S(1)} %get-tuple-element.49), channel_id=1, source_target_pairs={{0,5},{1,2},{4,9},{5,0},{8,13},{9,4},{12,15},{13,8},{14,11},{15,12... | collective-permute-start | bytes 589832 | tf_op jit(solution)/shard_map/ppermute | solution.py:356
  36.0 0.0 collective-permute-done.16.refs_4_
  36.0 3.1 %shard_map.98.refs_6_ = f32[2,768,128]{2,1,0:T(8,128)S(1)} custom-call(bf16[128,768]{1,0:T(8,128)(2,1)S(1)} %collective-permute-done.6.refs_0_, bf16[128,768]{1,0:T(8,128)(2,1)S(1)} %collective-permute-done.11.refs_1_, bf16[128,768]{1,0:T(8,128)(2,1)S(1)} %collective-permute-done.7.refs_2_, ...), custom_call_target="tpu_custom_call", output_to_operand_aliasing={{}: (10, {})} | custom-call | flops 393216 | bytes 393216 | tf_op jit(solution)/shard_map/pallas_call | solution.py:275
  39.1 0.0 copy-start
  39.1 0.0 collective-permute-done.15.refs_0_
  39.2 1.9 %shard_map.99.refs_7_ = f32[2,768,128]{2,1,0:T(8,128)S(1)} custom-call(bf16[2,128,768]{2,1,0:T(8,128)(2,1)S(1)} %collective-permute-done.15.refs_0_, bf16[2,768,256]{2,1,0:T(8,128)(2,1)S(1)} %get-tuple-element.36.refs_3_.refs_5_.refs_1_.refs_2_, ...), custom_call_target="tpu_custom_call", output_to_operand_aliasing={{}: (6, {})} | custom-call | flops 196608 | bytes 196608 | tf_op jit(solution)/shard_map/pallas_call | solution.py:275
  41.0 0.0 collective-permute-done.12.refs_0_
  41.0 0.4 collective-permute-done.13.refs_1_
  41.4 0.0 copy-done
  41.4 3.1 %shard_map.100 = (f32[2,768,128]{2,1,0:T(8,128)S(1)}, bf16[2,128,768]{2,1,0:T(8,128)(2,1)}) custom-call(bf16[128,768]{1,0:T(8,128)(2,1)S(1)} %collective-permute-done.12.refs_0_, bf16[128,768]{1,0:T(8,128)(2,1)S(1)} %collective-permute-done.13.refs_1_, ...), custom_call_target="tpu_custom_call", output_to_operand_aliasing={{0}: (7, {})} | custom-call | flops 196608 | bytes 196608 | tf_op jit(solution)/shard_map/pallas_call | solution.py:275
Async XLA Ops:
  0.0 12.6 %collective-permute-start = (bf16[2,128,768]{2,1,0:T(8,128)(2,1)}, bf16[2,128,768]{2,1,0:T(8,128)(2,1)S(1)}, u32[]{:S(2)}, u32[]{:S(2)}) collective-permute-start(bf16[2,128,768]{2,1,0:T(8,128)(2,1)} %refs_0_.1), channel_id=1, source_target_pairs={{0,4},{1,3},{4,8},{5,1},{8,12},{9,5},{12,14},{13,9},{14,10},{15,13... | collective-permute-start | bytes 1179656 | tf_op jit(solution)/shard_map/ppermute | solution.py:356
  3.0 9.6 %collective-permute-start.1 = (bf16[2,128,768]{2,1,0:T(8,128)(2,1)}, bf16[2,128,768]{2,1,0:T(8,128)(2,1)S(1)}, u32[]{:S(2)}, u32[]{:S(2)}) collective-permute-start(bf16[2,128,768]{2,1,0:T(8,128)(2,1)} %refs_0_.1), channel_id=1, source_target_pairs={{0,2},{1,5},{4,0},{5,9},{8,4},{9,13},{12,8},{13,15},{14,12},{15,11... | collective-permute-start | bytes 1179656 | tf_op jit(solution)/shard_map/ppermute | solution.py:356
  3.0 14.2 %collective-permute-start.5 = (bf16[2,128,768]{2,1,0:T(8,128)(2,1)}, bf16[2,128,768]{2,1,0:T(8,128)(2,1)S(1)}, u32[]{:S(2)}, u32[]{:S(2)}) collective-permute-start(bf16[2,128,768]{2,1,0:T(8,128)(2,1)} %refs_0_.1), channel_id=1, source_target_pairs={{0,1},{1,0},{2,3},{3,2},{4,5},{5,4},{6,7},{7,6},{8,9},{9,8},{10,11... | collective-permute-start | bytes 1179656 | tf_op jit(solution)/shard_map/ppermute | solution.py:356
  7.6 5.0 %collective-permute-start.2 = (f32[16,128]{1,0:T(8,128)S(1)}, f32[16,128]{1,0:T(8,128)S(1)}, u32[]{:S(2)}, u32[]{:S(2)}) collective-permute-start(f32[16,128]{1,0:T(8,128)S(1)} %get-tuple-element.33.refs_3_.refs_6_.refs_8_.refs_4_.refs_5_), channel_id=1, source_target_pairs={{0,1},{1,0},{2,3},{3,2},{4,5},{5,4},{6,7},{7,6},{8,9},{9,8},{10,11... | collective-permute-start | bytes 24584 | tf_op jit(solution)/shard_map/ppermute | solution.py:356
  12.7 7.7 %collective-permute-start.9 = (bf16[144,768]{1,0:T(8,128)(2,1)S(1)}, bf16[144,768]{1,0:T(8,128)(2,1)S(1)}, u32[]{:S(2)}, u32[]{:S(2)}) collective-permute-start(bf16[144,768]{1,0:T(8,128)(2,1)S(1)} %get-tuple-element.44), channel_id=1, source_target_pairs={{0,2},{1,5},{4,0},{5,9},{8,4},{9,13},{12,8},{13,15},{14,12},{15,11... | collective-permute-start | bytes 663560 | tf_op jit(solution)/shard_map/ppermute | solution.py:356
  15.2 10.3 %collective-permute-start.3 = (bf16[128,768]{1,0:T(8,128)(2,1)S(1)}, bf16[128,768]{1,0:T(8,128)(2,1)S(1)}, u32[]{:S(2)}, u32[]{:S(2)}) collective-permute-start(bf16[128,768]{1,0:T(8,128)(2,1)S(1)} %get-tuple-element.34), channel_id=1, source_target_pairs={{0,4},{1,3},{4,8},{5,1},{8,12},{9,5},{12,14},{13,9},{14,10},{15,13... | collective-permute-start | bytes 589832 | tf_op jit(solution)/shard_map/ppermute | solution.py:356
  15.2 10.3 %collective-permute-start.4 = (bf16[128,768]{1,0:T(8,128)(2,1)S(1)}, bf16[128,768]{1,0:T(8,128)(2,1)S(1)}, u32[]{:S(2)}, u32[]{:S(2)}) collective-permute-start(bf16[128,768]{1,0:T(8,128)(2,1)S(1)} %get-tuple-element.35), channel_id=1, source_target_pairs={{0,2},{1,5},{4,0},{5,9},{8,4},{9,13},{12,8},{13,15},{14,12},{15,11... | collective-permute-start | bytes 589832 | tf_op jit(solution)/shard_map/ppermute | solution.py:356
  17.2 11.7 %collective-permute-start.10 = (bf16[2,128,768]{2,1,0:T(8,128)(2,1)S(1)}, bf16[2,128,768]{2,1,0:T(8,128)(2,1)S(1)}, u32[]{:S(2)}, u32[]{:S(2)}) collective-permute-start(bf16[2,128,768]{2,1,0:T(8,128)(2,1)S(1)} %get-tuple-element.45), channel_id=1, source_target_pairs={{0,1},{1,0},{2,3},{3,2},{4,5},{5,4},{6,7},{7,6},{8,9},{9,8},{10,11... | collective-permute-start | bytes 1179656 | tf_op jit(solution)/shard_map/ppermute | solution.py:356
  17.2 10.3 %collective-permute-start.8 = (bf16[128,768]{1,0:T(8,128)(2,1)S(1)}, bf16[128,768]{1,0:T(8,128)(2,1)S(1)}, u32[]{:S(2)}, u32[]{:S(2)}) collective-permute-start(bf16[128,768]{1,0:T(8,128)(2,1)S(1)} %get-tuple-element.43), channel_id=1, source_target_pairs={{0,4},{1,3},{4,8},{5,1},{8,12},{9,5},{12,14},{13,9},{14,10},{15,13... | collective-permute-start | bytes 589832 | tf_op jit(solution)/shard_map/ppermute | solution.py:356
  20.4 13.1 %collective-permute-start.14 = (bf16[144,768]{1,0:T(8,128)(2,1)S(1)}, bf16[144,768]{1,0:T(8,128)(2,1)S(1)}, u32[]{:S(2)}, u32[]{:S(2)}) collective-permute-start(bf16[144,768]{1,0:T(8,128)(2,1)S(1)} %collective-permute-done.9.refs_3_.refs_2_), channel_id=1, source_target_pairs={{0,2},{1,5},{4,0},{5,9},{8,4},{9,13},{12,8},{13,15},{14,12},{15,11... | collective-permute-start | bytes 663560 | tf_op jit(solution)/shard_map/ppermute | solution.py:356
  25.5 6.6 %collective-permute-start.6 = (bf16[128,768]{1,0:T(8,128)(2,1)S(1)}, bf16[128,768]{1,0:T(8,128)(2,1)S(1)}, u32[]{:S(2)}, u32[]{:S(2)}) collective-permute-start(bf16[128,768]{1,0:T(8,128)(2,1)S(1)} %collective-permute-done.3.refs_0_), channel_id=1, source_target_pairs={{0,4},{1,3},{4,8},{5,1},{8,12},{9,5},{12,14},{13,9},{14,10},{15,13... | collective-permute-start | bytes 589832 | tf_op jit(solution)/shard_map/ppermute | solution.py:356
  26.7 6.5 %collective-permute-start.7 = (bf16[128,768]{1,0:T(8,128)(2,1)S(1)}, bf16[128,768]{1,0:T(8,128)(2,1)S(1)}, u32[]{:S(2)}, u32[]{:S(2)}) collective-permute-start(bf16[128,768]{1,0:T(8,128)(2,1)S(1)} %collective-permute-done.4.refs_2_), channel_id=1, source_target_pairs={{0,2},{1,5},{4,0},{5,9},{8,4},{9,13},{12,8},{13,15},{14,12},{15,11... | collective-permute-start | bytes 589832 | tf_op jit(solution)/shard_map/ppermute | solution.py:356
  27.6 6.0 %collective-permute-start.11 = (bf16[128,768]{1,0:T(8,128)(2,1)S(1)}, bf16[128,768]{1,0:T(8,128)(2,1)S(1)}, u32[]{:S(2)}, u32[]{:S(2)}) collective-permute-start(bf16[128,768]{1,0:T(8,128)(2,1)S(1)} %collective-permute-done.8.refs_1_), channel_id=1, source_target_pairs={{0,4},{1,3},{4,8},{5,1},{8,12},{9,5},{12,14},{13,9},{14,10},{15,13... | collective-permute-start | bytes 589832 | tf_op jit(solution)/shard_map/ppermute | solution.py:356
  28.9 7.1 %collective-permute-start.16 = (bf16[2,128,768]{2,1,0:T(8,128)(2,1)S(1)}, bf16[2,128,768]{2,1,0:T(8,128)(2,1)S(1)}, u32[]{:S(2)}, u32[]{:S(2)}) collective-permute-start(bf16[2,128,768]{2,1,0:T(8,128)(2,1)S(1)} %shard_map.97), channel_id=1, source_target_pairs={{0,1},{1,0},{2,3},{3,2},{4,5},{5,4},{6,7},{7,6},{8,9},{9,8},{10,11... | collective-permute-start | bytes 1179656 | tf_op jit(solution)/shard_map/ppermute | solution.py:356
  33.7 5.5 %collective-permute-start.15 = (bf16[2,128,768]{2,1,0:T(8,128)(2,1)S(1)}, bf16[2,128,768]{2,1,0:T(8,128)(2,1)S(1)}, u32[]{:S(2)}, u32[]{:S(2)}) collective-permute-start(bf16[2,128,768]{2,1,0:T(8,128)(2,1)S(1)} %shard_map.96), channel_id=1, source_target_pairs={{0,1},{1,0},{2,3},{3,2},{4,5},{5,4},{6,7},{7,6},{8,9},{9,8},{10,11... | collective-permute-start | bytes 1179656 | tf_op jit(solution)/shard_map/ppermute | solution.py:356
  33.9 7.1 %collective-permute-start.12 = (bf16[128,768]{1,0:T(8,128)(2,1)S(1)}, bf16[128,768]{1,0:T(8,128)(2,1)S(1)}, u32[]{:S(2)}, u32[]{:S(2)}) collective-permute-start(bf16[128,768]{1,0:T(8,128)(2,1)S(1)} %get-tuple-element.48), channel_id=1, source_target_pairs={{0,4},{1,3},{4,8},{5,1},{8,12},{9,5},{12,14},{13,9},{14,10},{15,13... | collective-permute-start | bytes 589832 | tf_op jit(solution)/shard_map/ppermute | solution.py:356
  35.5 6.0 %collective-permute-start.13 = (bf16[128,768]{1,0:T(8,128)(2,1)S(1)}, bf16[128,768]{1,0:T(8,128)(2,1)S(1)}, u32[]{:S(2)}, u32[]{:S(2)}) collective-permute-start(bf16[128,768]{1,0:T(8,128)(2,1)S(1)} %get-tuple-element.49), channel_id=1, source_target_pairs={{0,5},{1,2},{4,9},{5,0},{8,13},{9,4},{12,15},{13,8},{14,11},{15,12... | collective-permute-start | bytes 589832 | tf_op jit(solution)/shard_map/ppermute | solution.py:356
  39.1 2.3 %copy-start = (s32[2]{0:T(128)S(1)}, s32[2]{0:T(128)}, u32[]{:S(2)}) copy-start(s32[2]{0:T(128)} %refs_10_.1) | copy-start | bytes 28

commit v8 on v7

--- a/solution.py
+++ b/solution.py
@@ -370,6 +370,10 @@
     for step in range(1, far):
         up[0], down[0], total = lax.optimization_barrier((up[0], down[0], total))
         work = [((step, False, len(up)), up), ((-step, False, len(down)), down)] + behind
+        if step + 1 == far:
+            same, other = far_stage(ring, step, up, carried, **sizes)
+            same, other, up, down = lax.optimization_barrier((same, other, up, down))
+            same, other = send(same, ahead), send(other, cross)
         passing = [(step, up), (-step, down)]
         if step == 1:
             passed, *singles = pass_stage(ring, passing, sibling_picks, [picks], **sizes)
@@ -381,9 +385,6 @@
         came = send(passed, sibling)
         if step + 1 < far:
             up, down = [send(image, ahead) for image in up], [send(image, back) for image in down]
-        else:
-            same, other = far_stage(ring, step, up, carried, **sizes)
-            same, other = send(same, ahead), send(other, cross)
         (total,) = later_stage(ring, work, arrived, state, (), total, **sizes)
         arrived = came
         behind = [((step, True, 0), []), ((-step, True, 0), [])]

time: 44.9 us -> 44.7 us (level)
  no operation moved by 1% of the time
where the time goes in v8:
time: 44.7 us; the launch traced here: 44.5 us
  Pallas kernels  18.8 us (42%)
  starting transfers between devices  15.8 us (35%)
  waiting for transfers between devices  9.52 us (21%)
    ppermute x17, starting transfers between devices, shards(): send = lambda array, to: lax.ppermute(array, 'img', to)  15.8 us
    pallas_call x5, Pallas kernels, later_stage(): pl.pallas_call(functools.partial(later_kernel, ring, slots, last, own, to...  13.8 us
    ppermute x17, waiting for transfers between devices, shards(): send = lambda array, to: lax.ppermute(array, 'img', to)  9.52 us
    pallas_call x1, Pallas kernels, first_stage(): pl.pallas_call(functools.partial(first_kernel, ring, slots, own, listed,...  4.52 us
  transfers between devices with their start and end apart: 17, of which 5 were waited for; matrix products, arithmetic and copies ran while one was open for 0% of the time, Pallas kernels for 35%

profile of v8, /device:TPU:0, one launch (start us, length us, event | category | flops | bytes accessed | tf_op | source)
XLA Modules:
  0.0 44.5 jit_solution(4809203928349123925)
XLA Ops:
  0.0 3.0 %collective-permute-start = (bf16[2,128,768]{2,1,0:T(8,128)(2,1)}, bf16[2,128,768]{2,1,0:T(8,128)(2,1)S(1)}, u32[]{:S(2)}, u32[]{:S(2)}) collective-permute-start(bf16[2,128,768]{2,1,0:T(8,128)(2,1)} %refs_0_.1), channel_id=1, source_target_pairs={{0,4},{1,3},{4,8},{5,1},{8,12},{9,5},{12,14},{13,9},{14,10},{15,13... | collective-permute-start | bytes 1179656 | tf_op jit(solution)/shard_map/ppermute | solution.py:356
  3.0 0.0 collective-permute-start.1
  3.0 0.0 collective-permute-start.5
  3.0 4.5 %shard_map.91 = (f32[2,768,128]{2,1,0:T(8,128)S(1)}, bf16[2,768,256]{2,1,0:T(8,128)(2,1)S(1)}, bf16[768,1536]{1,0:T(8,128)(2,1)S(1)}, bf16[768,768]{1,0:T(8,128)...) custom-call(bf16[2,128,768]{2,1,0:T(8,128)(2,1)} %refs_0_.1, ...), custom_call_target="tpu_custom_call" | custom-call | flops 196608 | bytes 196608 | tf_op jit(solution)/shard_map/pallas_call | solution.py:248
  7.6 0.6 %collective-permute-start.2 = (f32[16,128]{1,0:T(8,128)S(1)}, f32[16,128]{1,0:T(8,128)S(1)}, u32[]{:S(2)}, u32[]{:S(2)}) collective-permute-start(f32[16,128]{1,0:T(8,128)S(1)} %get-tuple-element.39.refs_3_.refs_6_.refs_8_.refs_4_.refs_5_), channel_id=1, source_target_pairs={{0,1},{1,0},{2,3},{3,2},{4,5},{5,4},{6,7},{7,6},{8,9},{9,8},{10,11... | collective-permute-start | bytes 24584 | tf_op jit(solution)/shard_map/ppermute | solution.py:356
  8.1 4.5 %collective-permute-done.refs_0_ = bf16[2,128,768]{2,1,0:T(8,128)(2,1)S(1)} collective-permute-done((bf16[2,128,768]{2,1,0:T(8,128)(2,1)}, bf16[2,128,768]{2,1,0:T(8,128)(2,1)S(1)}, u32[]{:S(2)}, u32[]{:S(2)}) %collective-permute-start) | collective-permute-done | bytes 393248 | tf_op jit(solution)/shard_map/ppermute | solution.py:356
  12.6 0.0 collective-permute-done.1.refs_1_
  12.6 0.0 collective-permute-done.2.refs_2_.refs_4_
  12.6 0.1 shard_map.92
  12.7 2.5 %collective-permute-start.9 = (bf16[144,768]{1,0:T(8,128)(2,1)S(1)}, bf16[144,768]{1,0:T(8,128)(2,1)S(1)}, u32[]{:S(2)}, u32[]{:S(2)}) collective-permute-start(bf16[144,768]{1,0:T(8,128)(2,1)S(1)} %get-tuple-element.50), channel_id=1, source_target_pairs={{0,2},{1,5},{4,0},{5,9},{8,4},{9,13},{12,8},{13,15},{14,12},{15,11... | collective-permute-start | bytes 663560 | tf_op jit(solution)/shard_map/ppermute | solution.py:356
  15.2 0.0 collective-permute-start.3
  15.2 2.0 %collective-permute-start.4 = (bf16[128,768]{1,0:T(8,128)(2,1)S(1)}, bf16[128,768]{1,0:T(8,128)(2,1)S(1)}, u32[]{:S(2)}, u32[]{:S(2)}) collective-permute-start(bf16[128,768]{1,0:T(8,128)(2,1)S(1)} %get-tuple-element.41), channel_id=1, source_target_pairs={{0,2},{1,5},{4,0},{5,9},{8,4},{9,13},{12,8},{13,15},{14,12},{15,11... | collective-permute-start | bytes 589832 | tf_op jit(solution)/shard_map/ppermute | solution.py:356
  17.2 0.0 collective-permute-start.10
  17.2 0.0 collective-permute-done.5.refs_2_
  17.2 0.0 collective-permute-start.8
  17.3 3.2 %collective-permute-done.9.refs_3_.refs_2_ = bf16[144,768]{1,0:T(8,128)(2,1)S(1)} collective-permute-done((bf16[144,768]{1,0:T(8,128)(2,1)S(1)}, bf16[144,768]{1,0:T(8,128)(2,1)S(1)}, u32[]{:S(2)}, u32[]{:S(2)}) %collective-permute-start.9) | collective-permute-done | bytes 221216 | tf_op jit(solution)/shard_map/ppermute | solution.py:356
  20.4 2.5 %collective-permute-start.12 = (bf16[144,768]{1,0:T(8,128)(2,1)S(1)}, bf16[144,768]{1,0:T(8,128)(2,1)S(1)}, u32[]{:S(2)}, u32[]{:S(2)}) collective-permute-start(bf16[144,768]{1,0:T(8,128)(2,1)S(1)} %collective-permute-done.9.refs_3_.refs_2_), channel_id=1, source_target_pairs={{0,2},{1,5},{4,0},{5,9},{8,4},{9,13},{12,8},{13,15},{14,12},{15,11... | collective-permute-start | bytes 663560 | tf_op jit(solution)/shard_map/ppermute | solution.py:356
  22.9 2.5 %shard_map.93.refs_10_ = f32[2,768,128]{2,1,0:T(8,128)S(1)} custom-call(bf16[2,128,768]{2,1,0:T(8,128)(2,1)S(1)} %collective-permute-done.refs_0_, bf16[2,128,768]{2,1,0:T(8,128)(2,1)S(1)} %collective-permute-done.1.refs_1_, bf16[2,128,768]{2,1,0:T(8,128)(2,1)S(1)} %collective-permute-done.5.refs_2_, ...), custom_call_target="tpu_custom_call", output_to_operand_aliasing={{}: (8, {})} | custom-call | flops 294912 | bytes 294912 | tf_op jit(solution)/shard_map/pallas_call | solution.py:275
  25.5 0.0 collective-permute-done.3.refs_0_
  25.5 0.0 collective-permute-done.4.refs_2_
  25.5 1.2 %collective-permute-start.6 = (bf16[128,768]{1,0:T(8,128)(2,1)S(1)}, bf16[128,768]{1,0:T(8,128)(2,1)S(1)}, u32[]{:S(2)}, u32[]{:S(2)}) collective-permute-start(bf16[128,768]{1,0:T(8,128)(2,1)S(1)} %collective-permute-done.3.refs_0_), channel_id=1, source_target_pairs={{0,4},{1,3},{4,8},{5,1},{8,12},{9,5},{12,14},{13,9},{14,10},{15,13... | collective-permute-start | bytes 589832 | tf_op jit(solution)/shard_map/ppermute | solution.py:356
  26.7 0.8 %collective-permute-start.7 = (bf16[128,768]{1,0:T(8,128)(2,1)S(1)}, bf16[128,768]{1,0:T(8,128)(2,1)S(1)}, u32[]{:S(2)}, u32[]{:S(2)}) collective-permute-start(bf16[128,768]{1,0:T(8,128)(2,1)S(1)} %collective-permute-done.4.refs_2_), channel_id=1, source_target_pairs={{0,2},{1,5},{4,0},{5,9},{8,4},{9,13},{12,8},{13,15},{14,12},{15,11... | collective-permute-start | bytes 589832 | tf_op jit(solution)/shard_map/ppermute | solution.py:356
  27.6 0.0 collective-permute-done.8.refs_1_
  27.6 1.2 %collective-permute-start.11 = (bf16[128,768]{1,0:T(8,128)(2,1)S(1)}, bf16[128,768]{1,0:T(8,128)(2,1)S(1)}, u32[]{:S(2)}, u32[]{:S(2)}) collective-permute-start(bf16[128,768]{1,0:T(8,128)(2,1)S(1)} %collective-permute-done.8.refs_1_), channel_id=1, source_target_pairs={{0,4},{1,3},{4,8},{5,1},{8,12},{9,5},{12,14},{13,9},{14,10},{15,13... | collective-permute-start | bytes 589832 | tf_op jit(solution)/shard_map/ppermute | solution.py:356
  28.8 0.1 shard_map.97
  28.9 0.0 collective-permute-done.10.refs_4_
  28.9 0.1 collective-permute-start.16
  29.0 3.1 %shard_map.94.refs_10_ = f32[2,768,128]{2,1,0:T(8,128)S(1)} custom-call(bf16[128,768]{1,0:T(8,128)(2,1)S(1)} %collective-permute-done.3.refs_0_, bf16[128,768]{1,0:T(8,128)(2,1)S(1)} %collective-permute-done.8.refs_1_, bf16[128,768]{1,0:T(8,128)(2,1)S(1)} %collective-permute-done.4.refs_2_, ...), custom_call_target="tpu_custom_call", output_to_operand_aliasing={{}: (10, {})} | custom-call | flops 393216 | bytes 393216 | tf_op jit(solution)/shard_map/pallas_call | solution.py:275
  32.1 0.0 collective-permute-done.6.refs_0_
  32.1 1.1 %collective-permute-done.7.refs_2_ = bf16[128,768]{1,0:T(8,128)(2,1)S(1)} collective-permute-done((bf16[128,768]{1,0:T(8,128)(2,1)S(1)}, bf16[128,768]{1,0:T(8,128)(2,1)S(1)}, u32[]{:S(2)}, u32[]{:S(2)}) %collective-permute-start.7) | collective-permute-done | bytes 196640 | tf_op jit(solution)/shard_map/ppermute | solution.py:356
  33.2 0.3 collective-permute-done.11.refs_1_
  33.6 0.1 shard_map.95
  33.7 0.0 collective-permute-done.12.refs_3_
  33.7 0.1 shard_map.96
  33.8 0.1 collective-permute-start.15
  33.9 1.6 %collective-permute-start.13 = (bf16[128,768]{1,0:T(8,128)(2,1)S(1)}, bf16[128,768]{1,0:T(8,128)(2,1)S(1)}, u32[]{:S(2)}, u32[]{:S(2)}) collective-permute-start(bf16[128,768]{1,0:T(8,128)(2,1)S(1)} %get-tuple-element.57), channel_id=1, source_target_pairs={{0,4},{1,3},{4,8},{5,1},{8,12},{9,5},{12,14},{13,9},{14,10},{15,13... | collective-permute-start | bytes 589832 | tf_op jit(solution)/shard_map/ppermute | solution.py:356
  35.5 0.3 collective-permute-start.14
  35.8 0.0 collective-permute-done.16.refs_4_
  35.8 3.1 %shard_map.98.refs_6_ = f32[2,768,128]{2,1,0:T(8,128)S(1)} custom-call(bf16[128,768]{1,0:T(8,128)(2,1)S(1)} %collective-permute-done.6.refs_0_, bf16[128,768]{1,0:T(8,128)(2,1)S(1)} %collective-permute-done.11.refs_1_, bf16[128,768]{1,0:T(8,128)(2,1)S(1)} %collective-permute-done.7.refs_2_, ...), custom_call_target="tpu_custom_call", output_to_operand_aliasing={{}: (10, {})} | custom-call | flops 393216 | bytes 393216 | tf_op jit(solution)/shard_map/pallas_call | solution.py:275
  38.9 0.0 copy-start
  38.9 0.0 collective-permute-done.15.refs_0_
  38.9 1.8 %shard_map.99.refs_7_ = f32[2,768,128]{2,1,0:T(8,128)S(1)} custom-call(bf16[2,128,768]{2,1,0:T(8,128)(2,1)S(1)} %collective-permute-done.15.refs_0_, bf16[2,768,256]{2,1,0:T(8,128)(2,1)S(1)} %get-tuple-element.42.refs_3_.refs_5_.refs_1_.refs_2_, ...), custom_call_target="tpu_custom_call", output_to_operand_aliasing={{}: (6, {})} | custom-call | flops 196608 | bytes 196608 | tf_op jit(solution)/shard_map/pallas_call | solution.py:275
  40.8 0.0 collective-permute-done.13.refs_0_
  40.8 0.4 collective-permute-done.14.refs_1_
  41.2 0.0 copy-done
  41.2 3.1 %shard_map.100 = (f32[2,768,128]{2,1,0:T(8,128)S(1)}, bf16[2,128,768]{2,1,0:T(8,128)(2,1)}) custom-call(bf16[128,768]{1,0:T(8,128)(2,1)S(1)} %collective-permute-done.13.refs_0_, bf16[128,768]{1,0:T(8,128)(2,1)S(1)} %collective-permute-done.14.refs_1_, ...), custom_call_target="tpu_custom_call", output_to_operand_aliasing={{0}: (7, {})} | custom-call | flops 196608 | bytes 196608 | tf_op jit(solution)/shard_map/pallas_call | solution.py:275
Async XLA Ops:
  0.0 12.6 %collective-permute-start = (bf16[2,128,768]{2,1,0:T(8,128)(2,1)}, bf16[2,128,768]{2,1,0:T(8,128)(2,1)S(1)}, u32[]{:S(2)}, u32[]{:S(2)}) collective-permute-start(bf16[2,128,768]{2,1,0:T(8,128)(2,1)} %refs_0_.1), channel_id=1, source_target_pairs={{0,4},{1,3},{4,8},{5,1},{8,12},{9,5},{12,14},{13,9},{14,10},{15,13... | collective-permute-start | bytes 1179656 | tf_op jit(solution)/shard_map/ppermute | solution.py:356
  3.0 9.6 %collective-permute-start.1 = (bf16[2,128,768]{2,1,0:T(8,128)(2,1)}, bf16[2,128,768]{2,1,0:T(8,128)(2,1)S(1)}, u32[]{:S(2)}, u32[]{:S(2)}) collective-permute-start(bf16[2,128,768]{2,1,0:T(8,128)(2,1)} %refs_0_.1), channel_id=1, source_target_pairs={{0,2},{1,5},{4,0},{5,9},{8,4},{9,13},{12,8},{13,15},{14,12},{15,11... | collective-permute-start | bytes 1179656 | tf_op jit(solution)/shard_map/ppermute | solution.py:356
  3.0 14.2 %collective-permute-start.5 = (bf16[2,128,768]{2,1,0:T(8,128)(2,1)}, bf16[2,128,768]{2,1,0:T(8,128)(2,1)S(1)}, u32[]{:S(2)}, u32[]{:S(2)}) collective-permute-start(bf16[2,128,768]{2,1,0:T(8,128)(2,1)} %refs_0_.1), channel_id=1, source_target_pairs={{0,1},{1,0},{2,3},{3,2},{4,5},{5,4},{6,7},{7,6},{8,9},{9,8},{10,11... | collective-permute-start | bytes 1179656 | tf_op jit(solution)/shard_map/ppermute | solution.py:356
  7.6 5.0 %collective-permute-start.2 = (f32[16,128]{1,0:T(8,128)S(1)}, f32[16,128]{1,0:T(8,128)S(1)}, u32[]{:S(2)}, u32[]{:S(2)}) collective-permute-start(f32[16,128]{1,0:T(8,128)S(1)} %get-tuple-element.39.refs_3_.refs_6_.refs_8_.refs_4_.refs_5_), channel_id=1, source_target_pairs={{0,1},{1,0},{2,3},{3,2},{4,5},{5,4},{6,7},{7,6},{8,9},{9,8},{10,11... | collective-permute-start | bytes 24584 | tf_op jit(solution)/shard_map/ppermute | solution.py:356
  12.7 7.7 %collective-permute-start.9 = (bf16[144,768]{1,0:T(8,128)(2,1)S(1)}, bf16[144,768]{1,0:T(8,128)(2,1)S(1)}, u32[]{:S(2)}, u32[]{:S(2)}) collective-permute-start(bf16[144,768]{1,0:T(8,128)(2,1)S(1)} %get-tuple-element.50), channel_id=1, source_target_pairs={{0,2},{1,5},{4,0},{5,9},{8,4},{9,13},{12,8},{13,15},{14,12},{15,11... | collective-permute-start | bytes 663560 | tf_op jit(solution)/shard_map/ppermute | solution.py:356
  15.2 10.3 %collective-permute-start.3 = (bf16[128,768]{1,0:T(8,128)(2,1)S(1)}, bf16[128,768]{1,0:T(8,128)(2,1)S(1)}, u32[]{:S(2)}, u32[]{:S(2)}) collective-permute-start(bf16[128,768]{1,0:T(8,128)(2,1)S(1)} %get-tuple-element.40), channel_id=1, source_target_pairs={{0,4},{1,3},{4,8},{5,1},{8,12},{9,5},{12,14},{13,9},{14,10},{15,13... | collective-permute-start | bytes 589832 | tf_op jit(solution)/shard_map/ppermute | solution.py:356
  15.2 10.3 %collective-permute-start.4 = (bf16[128,768]{1,0:T(8,128)(2,1)S(1)}, bf16[128,768]{1,0:T(8,128)(2,1)S(1)}, u32[]{:S(2)}, u32[]{:S(2)}) collective-permute-start(bf16[128,768]{1,0:T(8,128)(2,1)S(1)} %get-tuple-element.41), channel_id=1, source_target_pairs={{0,2},{1,5},{4,0},{5,9},{8,4},{9,13},{12,8},{13,15},{14,12},{15,11... | collective-permute-start | bytes 589832 | tf_op jit(solution)/shard_map/ppermute | solution.py:356
  17.2 11.7 %collective-permute-start.10 = (bf16[2,128,768]{2,1,0:T(8,128)(2,1)S(1)}, bf16[2,128,768]{2,1,0:T(8,128)(2,1)S(1)}, u32[]{:S(2)}, u32[]{:S(2)}) collective-permute-start(bf16[2,128,768]{2,1,0:T(8,128)(2,1)S(1)} %get-tuple-element.51), channel_id=1, source_target_pairs={{0,1},{1,0},{2,3},{3,2},{4,5},{5,4},{6,7},{7,6},{8,9},{9,8},{10,11... | collective-permute-start | bytes 1179656 | tf_op jit(solution)/shard_map/ppermute | solution.py:356
  17.2 10.3 %collective-permute-start.8 = (bf16[128,768]{1,0:T(8,128)(2,1)S(1)}, bf16[128,768]{1,0:T(8,128)(2,1)S(1)}, u32[]{:S(2)}, u32[]{:S(2)}) collective-permute-start(bf16[128,768]{1,0:T(8,128)(2,1)S(1)} %get-tuple-element.49), channel_id=1, source_target_pairs={{0,4},{1,3},{4,8},{5,1},{8,12},{9,5},{12,14},{13,9},{14,10},{15,13... | collective-permute-start | bytes 589832 | tf_op jit(solution)/shard_map/ppermute | solution.py:356
  20.4 13.2 %collective-permute-start.12 = (bf16[144,768]{1,0:T(8,128)(2,1)S(1)}, bf16[144,768]{1,0:T(8,128)(2,1)S(1)}, u32[]{:S(2)}, u32[]{:S(2)}) collective-permute-start(bf16[144,768]{1,0:T(8,128)(2,1)S(1)} %collective-permute-done.9.refs_3_.refs_2_), channel_id=1, source_target_pairs={{0,2},{1,5},{4,0},{5,9},{8,4},{9,13},{12,8},{13,15},{14,12},{15,11... | collective-permute-start | bytes 663560 | tf_op jit(solution)/shard_map/ppermute | solution.py:356
  25.5 6.6 %collective-permute-start.6 = (bf16[128,768]{1,0:T(8,128)(2,1)S(1)}, bf16[128,768]{1,0:T(8,128)(2,1)S(1)}, u32[]{:S(2)}, u32[]{:S(2)}) collective-permute-start(bf16[128,768]{1,0:T(8,128)(2,1)S(1)} %collective-permute-done.3.refs_0_), channel_id=1, source_target_pairs={{0,4},{1,3},{4,8},{5,1},{8,12},{9,5},{12,14},{13,9},{14,10},{15,13... | collective-permute-start | bytes 589832 | tf_op jit(solution)/shard_map/ppermute | solution.py:356
  26.7 6.5 %collective-permute-start.7 = (bf16[128,768]{1,0:T(8,128)(2,1)S(1)}, bf16[128,768]{1,0:T(8,128)(2,1)S(1)}, u32[]{:S(2)}, u32[]{:S(2)}) collective-permute-start(bf16[128,768]{1,0:T(8,128)(2,1)S(1)} %collective-permute-done.4.refs_2_), channel_id=1, source_target_pairs={{0,2},{1,5},{4,0},{5,9},{8,4},{9,13},{12,8},{13,15},{14,12},{15,11... | collective-permute-start | bytes 589832 | tf_op jit(solution)/shard_map/ppermute | solution.py:356
  27.6 6.0 %collective-permute-start.11 = (bf16[128,768]{1,0:T(8,128)(2,1)S(1)}, bf16[128,768]{1,0:T(8,128)(2,1)S(1)}, u32[]{:S(2)}, u32[]{:S(2)}) collective-permute-start(bf16[128,768]{1,0:T(8,128)(2,1)S(1)} %collective-permute-done.8.refs_1_), channel_id=1, source_target_pairs={{0,4},{1,3},{4,8},{5,1},{8,12},{9,5},{12,14},{13,9},{14,10},{15,13... | collective-permute-start | bytes 589832 | tf_op jit(solution)/shard_map/ppermute | solution.py:356
  28.9 6.9 %collective-permute-start.16 = (bf16[2,128,768]{2,1,0:T(8,128)(2,1)S(1)}, bf16[2,128,768]{2,1,0:T(8,128)(2,1)S(1)}, u32[]{:S(2)}, u32[]{:S(2)}) collective-permute-start(bf16[2,128,768]{2,1,0:T(8,128)(2,1)S(1)} %shard_map.97), channel_id=1, source_target_pairs={{0,1},{1,0},{2,3},{3,2},{4,5},{5,4},{6,7},{7,6},{8,9},{9,8},{10,11... | collective-permute-start | bytes 1179656 | tf_op jit(solution)/shard_map/ppermute | solution.py:356
  33.8 5.1 %collective-permute-start.15 = (bf16[2,128,768]{2,1,0:T(8,128)(2,1)S(1)}, bf16[2,128,768]{2,1,0:T(8,128)(2,1)S(1)}, u32[]{:S(2)}, u32[]{:S(2)}) collective-permute-start(bf16[2,128,768]{2,1,0:T(8,128)(2,1)S(1)} %shard_map.96), channel_id=1, source_target_pairs={{0,1},{1,0},{2,3},{3,2},{4,5},{5,4},{6,7},{7,6},{8,9},{9,8},{10,11... | collective-permute-start | bytes 1179656 | tf_op jit(solution)/shard_map/ppermute | solution.py:356
  33.9 6.9 %collective-permute-start.13 = (bf16[128,768]{1,0:T(8,128)(2,1)S(1)}, bf16[128,768]{1,0:T(8,128)(2,1)S(1)}, u32[]{:S(2)}, u32[]{:S(2)}) collective-permute-start(bf16[128,768]{1,0:T(8,128)(2,1)S(1)} %get-tuple-element.57), channel_id=1, source_target_pairs={{0,4},{1,3},{4,8},{5,1},{8,12},{9,5},{12,14},{13,9},{14,10},{15,13... | collective-permute-start | bytes 589832 | tf_op jit(solution)/shard_map/ppermute | solution.py:356
  35.5 5.7 %collective-permute-start.14 = (bf16[128,768]{1,0:T(8,128)(2,1)S(1)}, bf16[128,768]{1,0:T(8,128)(2,1)S(1)}, u32[]{:S(2)}, u32[]{:S(2)}) collective-permute-start(bf16[128,768]{1,0:T(8,128)(2,1)S(1)} %get-tuple-element.58), channel_id=1, source_target_pairs={{0,5},{1,2},{4,9},{5,0},{8,13},{9,4},{12,15},{13,8},{14,11},{15,12... | collective-permute-start | bytes 589832 | tf_op jit(solution)/shard_map/ppermute | solution.py:356
  38.9 2.3 %copy-start = (s32[2]{0:T(128)S(1)}, s32[2]{0:T(128)}, u32[]{:S(2)}) copy-start(s32[2]{0:T(128)} %refs_10_.1) | copy-start | bytes 28
